TPU v7x, 32 devices: a whole 2x2x4 slice. The times are simulated.
32 devices in a mesh: fsdp: 2 (over y), ctx: 16 (over z, x, core).
Axes of the slice: x: 2, y: 2, z: 4, core: 2. Of those that a mesh axis runs over, the one named last changes fastest.
Arguments:
- tokens: bfloat16 [16, 2048, 576], P('fsdp', 'ctx'), may hold values from -6 to 6
- gain_attn: bfloat16 [576], P('fsdp'), may hold values from 0.5 to 1.5
- w_query: bfloat16 [576, 576], P('fsdp'), may hold values from -0.25 to 0.25
- w_key: bfloat16 [576, 192], P('fsdp'), may hold values from -0.25 to 0.25
- w_value: bfloat16 [576, 192], P('fsdp'), may hold values from -0.25 to 0.25
- w_out: bfloat16 [576, 576], P('fsdp'), may hold values from -2 to 2
- gain_ffn: bfloat16 [576], P('fsdp'), may hold values from 0.5 to 1.5
- w_gate: bfloat16 [576, 1536], P('fsdp'), may hold values from -0.25 to 0.25
- w_up: bfloat16 [576, 1536], P('fsdp'), may hold values from -0.25 to 0.25
- w_down: bfloat16 [1536, 576], P('fsdp'), may hold values from -0.15625 to 0.15625
- cotangent: bfloat16 [16, 2048, 576], P('fsdp', 'ctx'), may hold values from -6 to 6
Outputs:
- mixed_out: bfloat16 [16, 2048, 576], P('fsdp', 'ctx')
- grad_tokens: bfloat16 [16, 2048, 576], P('fsdp', 'ctx')
- grad_gain_attn: float32 [576], P('fsdp')
- grad_query: float32 [576, 576], P('fsdp')
- grad_key: float32 [576, 192], P('fsdp')
- grad_value: float32 [576, 192], P('fsdp')
- grad_out: float32 [576, 576], P('fsdp')
- grad_gain_ffn: float32 [576], P('fsdp')
- grad_gate: float32 [576, 1536], P('fsdp')
- grad_up: float32 [576, 1536], P('fsdp')
- grad_down: float32 [1536, 576], P('fsdp')
All inputs are finite; a program needn't handle non-finite values.
Results may differ from a plain program's by a relative error of at most 0.03.
Values may be sent and summed in bfloat16 or wider, within the bound.
No kernel may reach another device: no remote copies, remote signals or barrier semaphores. Data moves between devices by JAX's collectives and lax.ppermute only.
A program may use at most 256 MiB of HBM per device.

v0:
```python
import jax
import jax.numpy as jnp
from jax import lax
from jax.sharding import PartitionSpec as P

HEADS = 9
KV_HEADS = 3
HEAD_DIM = 64


EPSILON = 1e-05
THETA = 100000.0
NEGATIVE = -1e30


def rope_tables(positions, head_size):
    halves = head_size // 2
    frequency = THETA ** (-jnp.arange(halves, dtype=jnp.float32) * 2.0 / head_size)
    angles = positions.astype(jnp.float32)[:, None] * frequency[None, :]
    return (jnp.cos(angles), jnp.sin(angles))


def rotate(values, cosine, sine):
    halves = values.shape[-1] // 2
    leading = values[..., :halves]
    trailing = values[..., halves:]
    cos_rows = cosine[:, None, :]
    sin_rows = sine[:, None, :]
    return jnp.concatenate(
        [leading * cos_rows - trailing * sin_rows, trailing * cos_rows + leading * sin_rows],
        axis=-1,
    )


def rms_scale(values):
    return lax.rsqrt(jnp.mean(values * values, axis=-1, keepdims=True) + EPSILON)


def block_length(local_len, ctx_count):
    per_block = max(1, min(ctx_count, 512 // local_len))
    while ctx_count % per_block:
        per_block -= 1
    return local_len * per_block


def key_scores(queries, key_block, query_pos, key_start, factor):
    key_count = key_block.shape[1]
    key_four = key_block.reshape(key_block.shape[0], key_count, queries.shape[2], queries.shape[4])
    scores = (
        jnp.einsum("sqkgd,snkd->skgqn", queries, key_four, preferred_element_type=jnp.float32)
        * factor
    )
    key_pos = key_start + jnp.arange(key_count, dtype=jnp.int32)
    causal = query_pos[:, None] >= key_pos[None, :]
    return (scores, causal, key_four)


def fold_block(running, key_block, value_block, key_start, queries, query_pos, factor):
    top_now, summed, accumulated = running
    scores, causal, key_four = key_scores(queries, key_block, query_pos, key_start, factor)
    scores = jnp.where(causal, scores, NEGATIVE)
    top_new = jnp.maximum(top_now, jnp.max(scores, axis=-1))
    rescale = jnp.exp(top_now - top_new)
    weights = jnp.where(causal, jnp.exp(scores - top_new[..., None]), 0.0)
    summed = summed * rescale + jnp.sum(weights, axis=-1)
    value_four = value_block.reshape(key_four.shape)
    update = jnp.einsum(
        "skgqn,snkd->skgqd",
        weights.astype(jnp.bfloat16),
        value_four,
        preferred_element_type=jnp.float32,
    )
    return (top_new, summed, accumulated * rescale[..., None] + update)


def fold_piece(running, pieces, queries, query_pos, factor, key_span, last_query):
    key_piece, value_piece = pieces
    key_count = key_piece.shape[1]
    needed = jnp.clip(last_query // key_span + 1, 0, key_count // key_span)

    def fold_step(block_index, carried):
        offset = block_index * key_span
        key_block = lax.dynamic_slice_in_dim(key_piece, offset, key_span, 1)
        value_block = lax.dynamic_slice_in_dim(value_piece, offset, key_span, 1)
        return fold_block(carried, key_block, value_block, offset, queries, query_pos, factor)

    return lax.fori_loop(jnp.int32(0), needed, fold_step, running)


def score_grads(
    key_block, value_block, key_start, queries, grad_attn, log_total, row_dot, query_pos, factor
):
    scores, causal, key_four = key_scores(queries, key_block, query_pos, key_start, factor)
    probability = jnp.where(causal, jnp.exp(scores - log_total[..., None]), 0.0)
    value_four = value_block.reshape(key_four.shape)
    grad_prob = jnp.einsum(
        "sqkgd,snkd->skgqn", grad_attn, value_four, preferred_element_type=jnp.float32
    )
    grad_score = (probability * (grad_prob - row_dot[..., None])).astype(jnp.bfloat16)
    return (grad_score, probability.astype(jnp.bfloat16), key_four)


def key_value_terms(grad_score, prob_low, queries, grad_attn, factor, flat_shape):
    part_key = (
        jnp.einsum("skgqn,sqkgd->snkd", grad_score, queries, preferred_element_type=jnp.float32)
        * factor
    )
    part_value = jnp.einsum(
        "skgqn,sqkgd->snkd", prob_low, grad_attn, preferred_element_type=jnp.float32
    )
    return (part_key.reshape(flat_shape), part_value.reshape(flat_shape))


def norm_backward(grad_hidden, normed, scale_rows, gain_rows):
    grad_gain = jnp.sum(grad_hidden * normed, axis=0)
    grad_normed = grad_hidden * gain_rows
    inner_mean = jnp.mean(grad_normed * normed, axis=-1, keepdims=True)
    return (grad_gain, scale_rows * (grad_normed - normed * inner_mean))


def local(
    tokens, gain_attn, w_query, w_key, w_value, w_out, gain_ffn, w_gate, w_up, w_down, cotangent
):
    seq_count, local_len, model_width = tokens.shape
    row_count = seq_count * local_len
    group_size = HEADS // KV_HEADS
    kv_width = KV_HEADS * HEAD_DIM
    key_span = block_length(local_len, lax.axis_size("ctx"))
    factor = HEAD_DIM ** (-0.5)
    first_query = lax.axis_index("ctx") * local_len
    last_query = first_query + local_len - 1
    query_pos = first_query + jnp.arange(local_len, dtype=jnp.int32)
    cosine, sine = rope_tables(query_pos, HEAD_DIM)
    gain_one, query_w, key_w, value_w, out_w = (
        lax.all_gather(gain_attn, "fsdp", axis=0, tiled=True),
        lax.all_gather(w_query, "fsdp", axis=0, tiled=True),
        lax.all_gather(w_key, "fsdp", axis=0, tiled=True),
        lax.all_gather(w_value, "fsdp", axis=0, tiled=True),
        lax.all_gather(w_out, "fsdp", axis=0, tiled=True),
    )
    source = tokens.reshape(row_count, model_width).astype(jnp.float32)
    scale_one = rms_scale(source)
    normed_one = source * scale_one
    gain_first = gain_one.astype(jnp.float32)
    hidden_one = (normed_one * gain_first).astype(jnp.bfloat16)
    query_lin = jnp.dot(hidden_one, query_w, preferred_element_type=jnp.float32)
    key_lin = jnp.dot(hidden_one, key_w, preferred_element_type=jnp.float32)
    value_loc = jnp.dot(hidden_one, value_w, preferred_element_type=jnp.float32).astype(
        jnp.bfloat16
    )
    value_loc = value_loc.reshape(seq_count, local_len, kv_width)
    query_rot = rotate(
        query_lin.reshape(seq_count, local_len, HEADS, HEAD_DIM), cosine, sine
    ).astype(jnp.bfloat16)
    query_rot = query_rot.reshape(seq_count, local_len, KV_HEADS, group_size, HEAD_DIM)
    key_rot = rotate(
        key_lin.reshape(seq_count, local_len, KV_HEADS, HEAD_DIM), cosine, sine
    ).astype(jnp.bfloat16)
    key_rot = key_rot.reshape(seq_count, local_len, kv_width)
    stat_shape = (seq_count, KV_HEADS, group_size, local_len)
    start_state = (
        jnp.full(stat_shape, NEGATIVE, jnp.float32),
        jnp.zeros(stat_shape, jnp.float32),
        jnp.zeros(stat_shape + (HEAD_DIM,), jnp.float32),
    )
    top_final, summed, accumulated = fold_piece(
        start_state,
        (
            lax.all_gather(key_rot, "ctx", axis=1, tiled=True),
            lax.all_gather(value_loc, "ctx", axis=1, tiled=True),
        ),
        query_rot,
        query_pos,
        factor,
        key_span,
        last_query,
    )
    attended = jnp.transpose(accumulated / summed[..., None], (0, 3, 1, 2, 4))
    log_total = top_final + jnp.log(summed)
    attn_mixed = attended.reshape(row_count, model_width).astype(jnp.bfloat16)
    residual = source + jnp.dot(attn_mixed, out_w, preferred_element_type=jnp.float32)
    gain_two, gate_w, up_w, down_w = (
        lax.all_gather(gain_ffn, "fsdp", axis=0, tiled=True),
        lax.all_gather(w_gate, "fsdp", axis=0, tiled=True),
        lax.all_gather(w_up, "fsdp", axis=0, tiled=True),
        lax.all_gather(w_down, "fsdp", axis=0, tiled=True),
    )
    scale_two = rms_scale(residual)
    normed_two = residual * scale_two
    gain_second = gain_two.astype(jnp.float32)
    hidden_two = (normed_two * gain_second).astype(jnp.bfloat16)
    gate_lin = jnp.dot(hidden_two, gate_w, preferred_element_type=jnp.float32)
    up_lin = jnp.dot(hidden_two, up_w, preferred_element_type=jnp.float32)
    sigmoid_gate = jax.nn.sigmoid(gate_lin)
    silu_gate = gate_lin * sigmoid_gate
    activated = (silu_gate * up_lin).astype(jnp.bfloat16)
    mixed_out = residual + jnp.dot(activated, down_w, preferred_element_type=jnp.float32)
    cot_rows = cotangent.reshape(row_count, model_width)
    grad_act = jnp.dot(cot_rows, down_w.T, preferred_element_type=jnp.float32)
    grad_down = jnp.dot(activated.T, cot_rows, preferred_element_type=jnp.float32)
    grad_gate_lin = (
        grad_act * up_lin * sigmoid_gate * (1.0 + gate_lin * (1.0 - sigmoid_gate))
    ).astype(jnp.bfloat16)
    grad_up_lin = (grad_act * silu_gate).astype(jnp.bfloat16)
    grad_gate = jnp.dot(hidden_two.T, grad_gate_lin, preferred_element_type=jnp.float32)
    grad_up = jnp.dot(hidden_two.T, grad_up_lin, preferred_element_type=jnp.float32)
    grad_hidden_two = jnp.dot(
        grad_gate_lin, gate_w.T, preferred_element_type=jnp.float32
    ) + jnp.dot(grad_up_lin, up_w.T, preferred_element_type=jnp.float32)
    grad_gain_ffn, grad_res_norm = norm_backward(
        grad_hidden_two, normed_two, scale_two, gain_second
    )
    grad_residual = cot_rows.astype(jnp.float32) + grad_res_norm
    grad_res_low = grad_residual.astype(jnp.bfloat16)
    grad_out = jnp.dot(attn_mixed.T, grad_res_low, preferred_element_type=jnp.float32)
    grad_attn = jnp.dot(grad_res_low, out_w.T, preferred_element_type=jnp.float32).astype(
        jnp.bfloat16
    )
    grad_attn = grad_attn.reshape(seq_count, local_len, KV_HEADS, group_size, HEAD_DIM)
    row_dot = jnp.transpose(
        jnp.sum(grad_attn.astype(jnp.float32) * attended, axis=-1), (0, 2, 3, 1)
    )
    key_all, value_all = (
        lax.all_gather(key_rot, "ctx", axis=1, tiled=True),
        lax.all_gather(value_loc, "ctx", axis=1, tiled=True),
    )
    whole_len = key_all.shape[1]
    needed_blocks = last_query // key_span + 1
    query_grad_shape = (seq_count, local_len, KV_HEADS, group_size, HEAD_DIM)

    def grad_step(block_index, carried):
        grad_queries, grad_keys, grad_values = carried
        offset = block_index * key_span
        key_block = lax.dynamic_slice_in_dim(key_all, offset, key_span, 1)
        value_block = lax.dynamic_slice_in_dim(value_all, offset, key_span, 1)
        grad_score, prob_low, key_four = score_grads(
            key_block,
            value_block,
            offset,
            query_rot,
            grad_attn,
            log_total,
            row_dot,
            query_pos,
            factor,
        )
        part_query = (
            jnp.einsum(
                "skgqn,snkd->sqkgd", grad_score, key_four, preferred_element_type=jnp.float32
            )
            * factor
        )
        part_key, part_value = key_value_terms(
            grad_score, prob_low, query_rot, grad_attn, factor, key_block.shape
        )
        grad_keys = lax.dynamic_update_slice_in_dim(grad_keys, part_key, offset, 1)
        grad_values = lax.dynamic_update_slice_in_dim(grad_values, part_value, offset, 1)
        return (grad_queries + part_query, grad_keys, grad_values)

    start_grads = (
        jnp.zeros(query_grad_shape, jnp.float32),
        jnp.zeros((seq_count, whole_len, kv_width), jnp.float32),
        jnp.zeros((seq_count, whole_len, kv_width), jnp.float32),
    )
    grad_queries, grad_keys, grad_values = lax.fori_loop(
        jnp.int32(0), needed_blocks, grad_step, start_grads
    )
    own_key, own_value = (
        lax.psum_scatter(
            grad_keys.astype(jnp.bfloat16), "ctx", scatter_dimension=1, tiled=True
        ).astype(jnp.float32),
        lax.psum_scatter(
            grad_values.astype(jnp.bfloat16), "ctx", scatter_dimension=1, tiled=True
        ).astype(jnp.float32),
    )
    query_back = rotate(
        grad_queries.reshape(seq_count, local_len, HEADS, HEAD_DIM), cosine, -sine
    ).astype(jnp.bfloat16)
    query_back = query_back.reshape(row_count, model_width)
    key_back = rotate(
        own_key.reshape(seq_count, local_len, KV_HEADS, HEAD_DIM), cosine, -sine
    ).astype(jnp.bfloat16)
    key_back = key_back.reshape(row_count, kv_width)
    value_back = own_value.astype(jnp.bfloat16).reshape(row_count, kv_width)
    grad_query = jnp.dot(hidden_one.T, query_back, preferred_element_type=jnp.float32)
    grad_key = jnp.dot(hidden_one.T, key_back, preferred_element_type=jnp.float32)
    grad_value = jnp.dot(hidden_one.T, value_back, preferred_element_type=jnp.float32)
    grad_hidden_one = jnp.dot(query_back, query_w.T, preferred_element_type=jnp.float32)
    grad_hidden_one = grad_hidden_one + jnp.dot(
        key_back, key_w.T, preferred_element_type=jnp.float32
    )
    grad_hidden_one = grad_hidden_one + jnp.dot(
        value_back, value_w.T, preferred_element_type=jnp.float32
    )
    grad_gain_attn, grad_src_norm = norm_backward(
        grad_hidden_one, normed_one, scale_one, gain_first
    )
    grad_source = (grad_residual + grad_src_norm).astype(jnp.bfloat16)
    local_grads = (
        grad_gain_attn,
        grad_query,
        grad_key,
        grad_value,
        grad_out,
        grad_gain_ffn,
        grad_gate,
        grad_up,
        grad_down,
    )
    summed_grads = (
        lax.psum(local_grads[0].astype(jnp.bfloat16), "ctx").astype(jnp.float32),
        lax.psum(local_grads[1].astype(jnp.bfloat16), "ctx").astype(jnp.float32),
        lax.psum(local_grads[2].astype(jnp.bfloat16), "ctx").astype(jnp.float32),
        lax.psum(local_grads[3].astype(jnp.bfloat16), "ctx").astype(jnp.float32),
        lax.psum(local_grads[4].astype(jnp.bfloat16), "ctx").astype(jnp.float32),
        lax.psum(local_grads[5].astype(jnp.bfloat16), "ctx").astype(jnp.float32),
        lax.psum(local_grads[6].astype(jnp.bfloat16), "ctx").astype(jnp.float32),
        lax.psum(local_grads[7].astype(jnp.bfloat16), "ctx").astype(jnp.float32),
        lax.psum(local_grads[8].astype(jnp.bfloat16), "ctx").astype(jnp.float32),
    )
    owned = (
        lax.psum_scatter(
            summed_grads[0].astype(jnp.bfloat16), "fsdp", scatter_dimension=0, tiled=True
        ).astype(jnp.float32),
        lax.psum_scatter(
            summed_grads[1].astype(jnp.bfloat16), "fsdp", scatter_dimension=0, tiled=True
        ).astype(jnp.float32),
        lax.psum_scatter(
            summed_grads[2].astype(jnp.bfloat16), "fsdp", scatter_dimension=0, tiled=True
        ).astype(jnp.float32),
        lax.psum_scatter(
            summed_grads[3].astype(jnp.bfloat16), "fsdp", scatter_dimension=0, tiled=True
        ).astype(jnp.float32),
        lax.psum_scatter(
            summed_grads[4].astype(jnp.bfloat16), "fsdp", scatter_dimension=0, tiled=True
        ).astype(jnp.float32),
        lax.psum_scatter(
            summed_grads[5].astype(jnp.bfloat16), "fsdp", scatter_dimension=0, tiled=True
        ).astype(jnp.float32),
        lax.psum_scatter(
            summed_grads[6].astype(jnp.bfloat16), "fsdp", scatter_dimension=0, tiled=True
        ).astype(jnp.float32),
        lax.psum_scatter(
            summed_grads[7].astype(jnp.bfloat16), "fsdp", scatter_dimension=0, tiled=True
        ).astype(jnp.float32),
        lax.psum_scatter(
            summed_grads[8].astype(jnp.bfloat16), "fsdp", scatter_dimension=0, tiled=True
        ).astype(jnp.float32),
    )
    return (
        mixed_out.astype(jnp.bfloat16).reshape(seq_count, local_len, model_width),
        grad_source.reshape(seq_count, local_len, model_width),
        owned[0],
        owned[1],
        owned[2],
        owned[3],
        owned[4],
        owned[5],
        owned[6],
        owned[7],
        owned[8],
    )


def solution(mesh):
    placed = (
        P("fsdp", "ctx", None),
        P("fsdp"),
        P("fsdp", None),
        P("fsdp", None),
        P("fsdp", None),
        P("fsdp", None),
        P("fsdp"),
        P("fsdp", None),
        P("fsdp", None),
        P("fsdp", None),
        P("fsdp", "ctx", None),
    )
    return jax.shard_map(
        local,
        mesh=mesh,
        in_specs=placed,
        out_specs=(
            P("fsdp", "ctx", None),
            P("fsdp", "ctx", None),
            P("fsdp"),
            P("fsdp", None),
            P("fsdp", None),
            P("fsdp", None),
            P("fsdp", None),
            P("fsdp"),
            P("fsdp", None),
            P("fsdp", None),
            P("fsdp", None),
        ),
        check_vma=False,
    )
```

profile of v0, /device:TPU:1, one launch (start us, length us, event | category | flops | bytes accessed | tf_op | source)
XLA Modules:
  0.0 1051.1 jit_solution(8041149837392644139)
XLA Ops:
  34.6 7.4 all_gather.38
  42.0 9.3 all_gather.41
  57.5 37.9 %all-gather.8.cloned.1.call-done = bf16[8,2048,192]{1,2,0:T(8,128)(2,1)} async-done(((bf16[8,128,192]{1,2,0:T(8,128)(2,1)}), bf16[8,2048,192]{1,2,0:T(8,128)(2,1)}) %all-gather.8.cloned.1.call-update) | async-done | bytes 6291472 | tf_op jit(solution)/shard_map/all_gather | solution.py:170
  95.4 66.6 %all-gather.6.cloned.1.call-done = bf16[8,2048,192]{1,2,0:T(8,128)(2,1)} async-done(((bf16[8,128,192]{1,2,0:T(8,128)(2,1)}), bf16[8,2048,192]{1,2,0:T(8,128)(2,1)}) %all-gather.6.cloned.1.call-update) | async-done | bytes 6291472 | tf_op jit(solution)/shard_map/all_gather | solution.py:169
  163.7 37.7 %while.30 = (s32[]{:T(128)}, f32[8,3,3,128]{3,2,1,0:T(4,128)S(1)}, f32[8,3,3,128]{3,2,1,0:T(4,128)S(1)}, f32[8,3,3,128,64]{3,4,2,1,0:T(8,128)}, s32[]{:T(128)}, ...) while((s32[]{:T(128)}, f32[8,3,3,128]{3,2,1,0:T(4,128)S(1)}, ...), condition=%wide.region_4.5_spmd.clone, body=%wide.region_1.4_spmd.clone.sunk | while | flops 1270565504 | bytes 72815800 | solution.py:87
  167.5 8.1 fusion.147
  175.6 11.6 %fusion.148 = f32[8,3,3,128]{3,2,1,0:T(4,128)S(1)} fusion(f32[8,3,512,128,3]{3,2,4,1,0:T(8,128)} %get-tuple-element.470, f32[8,3,3,128]{3,2,1,0:T(4,128)S(1)} %max.10, pred[128,512]{0,1:T(8,128)(4,1)S(1)} %broadcast_compare_fusion.4), kind=kLoop, calls=%fused_computation.6.clone.1 | loop fusion | flops 23583744 | bytes 19013632 | tf_op jit(solution)/shard_map/while/body/reduce_sum | solution.py:65
  187.2 13.6 %multiply_add_fusion.8 = f32[8,3,3,128,64]{3,4,2,1,0:T(8,128)} fusion(f32[8,3,3,128,64]{3,4,2,1,0:T(8,128)} %get-tuple-element.504, bf16[8,512,3,64,1]{1,3,4,2,0:T(8,128)(2,1)} %bitcast.305, f32[8,3,512,128,3]{3,2,4,1,0:T(8,128)} %get-tuple-element.470, f32[8,3,3,128]{3,2,1,0:T(4,128)S(1)} %max.10, pred[128,512]{0,1:T(8,128)(4,1)S(1)} %broadcast_compare_fusion.4, ...), kind=kOutput, calls=%fused_computation.9.clone.1 | convolution fusion | flops 628752384 | bytes 25305088 | tf_op jit(solution)/shard_map/while/body/skgqn,snkd->skgqd/dot_general | solution.py:67
  208.4 7.2 fusion.78
  221.6 7.2 fusion.77
  228.8 23.7 %all-gather.14.cloned.1.call-done = bf16[1536,576]{0,1:T(8,128)(2,1)} async-done(((bf16[768,576]{0,1:T(8,128)(2,1)}), bf16[1536,576]{0,1:T(8,128)(2,1)}) %all-gather.14.cloned.1.call-update) | async-done | bytes 1769488 | tf_op jit(solution)/shard_map/all_gather | solution.py:186
  252.5 10.2 multiply_convert_fusion
  283.9 49.1 %while.31 = (s32[]{:T(128)}, f32[8,128,3,3,64]{1,4,3,2,0:T(8,128)}, bf16[8,2048,192]{1,2,0:T(8,128)(2,1)}, bf16[8,2048,192]{1,2,0:T(8,128)(2,1)}, s32[]{:T(128)}...) while((s32[]{:T(128)}, f32[8,128,3,3,64]{1,4,3,2,0:T(8,128)}, ...), condition=%wide.region_9.10_spmd.clone, body=%wide.region_8.9_spmd.clone.sunk | while | flops 3069903360 | bytes 225232272 | solution.py:265
  292.4 6.5 copy-done.1
  304.7 12.3 %fusion.160 = bf16[8,3,3,128,512]{3,4,2,1,0:T(8,128)(2,1)} fusion(f32[8,3,512,128,3]{3,2,4,1,0:T(8,128)} %copy-done.1, f32[8,3,3,128]{3,2,1,0:T(4,128)S(1)} %get-tuple-element.569, f32[8,3,3,128]{3,2,1,0:T(4,128)S(1)} %get-tuple-element.566, pred[128,512]{0,1:T(8,128)(4,1)S(1)} %broadcast_compare_fusion.5, ...), kind=kOutput, calls=%fused_computation.22.clone.1 | convolution fusion | flops 632291328 | bytes 31203328 | tf_op jit(solution)/shard_map/while/body/sqkgd,snkd->skgqn/dot_general | solution.py:96
  322.6 7.9 bitcast_multiply_fusion.4
  333.0 12.9 %copy.82 = bf16[8,2048,192]{2,0,1:T(8,128)(2,1)} copy(bf16[8,2048,192]{1,2,0:T(8,128)(2,1)} %get-tuple-element.130) | data formatting | bytes 12582912
  345.9 13.5 %reshape.333 = bf16[2048,1536]{1,0:T(8,128)(2,1)} reshape(bf16[2048,8,192]{2,1,0:T(8,128)(2,1)} %bitcast.309) | data formatting | bytes 12582912
  359.6 12.9 %copy.84 = bf16[8,2048,192]{2,0,1:T(8,128)(2,1)} copy(bf16[8,2048,192]{1,2,0:T(8,128)(2,1)} %get-tuple-element.131) | data formatting | bytes 12582912
  372.5 13.6 %reshape.335 = bf16[2048,1536]{1,0:T(8,128)(2,1)} reshape(bf16[2048,8,192]{2,1,0:T(8,128)(2,1)} %bitcast.310) | data formatting | bytes 12582912
  411.1 257.7 %reduce-scatter.28.cloned.1.call-done = bf16[128,1536]{1,0:T(8,128)(2,1)} async-done(((bf16[2048,1536]{1,0:T(8,128)(2,1)}), bf16[128,1536]{1,0:T(8,128)(2,1)}) %reduce-scatter.28.cloned.1.call-update) | async-done | bytes 393232
  670.8 87.0 %reduce-scatter.30.cloned.1.call-done = bf16[128,1536]{1,0:T(8,128)(2,1)} async-done(((bf16[2048,1536]{1,0:T(8,128)(2,1)}), bf16[128,1536]{1,0:T(8,128)(2,1)}) %reduce-scatter.30.cloned.1.call-update) | async-done | bytes 393232
  765.7 11.3 %reduce-scatter.20.cloned.1.call-done = bf16[288,576]{1,0:T(8,128)(2,1)} async-done(((bf16[576,576]{1,0:T(8,128)(2,1)}), bf16[288,576]{1,0:T(8,128)(2,1)}) %reduce-scatter.20.cloned.1.call-update) | async-done | bytes 331792 | tf_op jit(solution)/shard_map/reduce_scatter | solution.py:334
  776.9 19.8 %reduce-scatter.14.cloned.1.call-done = bf16[288,576]{1,0:T(8,128)(2,1)} async-done(((bf16[576,576]{1,0:T(8,128)(2,1)}), bf16[288,576]{1,0:T(8,128)(2,1)}) %reduce-scatter.14.cloned.1.call-update) | async-done | bytes 331792 | tf_op jit(solution)/shard_map/reduce_scatter | solution.py:325
  796.7 30.9 %reduce-scatter.22.cloned.1.call-done = bf16[288,1536]{1,0:T(8,128)(2,1)} async-done(((bf16[576,1536]{1,0:T(8,128)(2,1)}), bf16[288,1536]{1,0:T(8,128)(2,1)}) %reduce-scatter.22.cloned.1.call-update) | async-done | bytes 884752 | tf_op jit(solution)/shard_map/reduce_scatter | solution.py:340
  827.7 31.2 %reduce-scatter.24.cloned.1.call-done = bf16[288,1536]{1,0:T(8,128)(2,1)} async-done(((bf16[576,1536]{1,0:T(8,128)(2,1)}), bf16[288,1536]{1,0:T(8,128)(2,1)}) %reduce-scatter.24.cloned.1.call-update) | async-done | bytes 884752 | tf_op jit(solution)/shard_map/reduce_scatter | solution.py:343
  858.9 31.0 %reduce-scatter.26.cloned.1.call-done = bf16[768,576]{0,1:T(8,128)(2,1)} async-done(((bf16[1536,576]{0,1:T(8,128)(2,1)}), bf16[768,576]{0,1:T(8,128)(2,1)}) %reduce-scatter.26.cloned.1.call-update) | async-done | bytes 884752 | tf_op jit(solution)/shard_map/reduce_scatter | solution.py:346
  889.8 14.4 %reduce-scatter.18.cloned.1.call-done = bf16[288,192]{1,0:T(8,128)(2,1)} async-done(((bf16[576,192]{1,0:T(8,128)(2,1)}), bf16[288,192]{1,0:T(8,128)(2,1)}) %reduce-scatter.18.cloned.1.call-update) | async-done | bytes 110608 | tf_op jit(solution)/shard_map/reduce_scatter | solution.py:331
  904.2 14.8 %reduce-scatter.16.cloned.1.call-done = bf16[288,192]{1,0:T(8,128)(2,1)} async-done(((bf16[576,192]{1,0:T(8,128)(2,1)}), bf16[288,192]{1,0:T(8,128)(2,1)}) %reduce-scatter.16.cloned.1.call-update) | async-done | bytes 110608 | tf_op jit(solution)/shard_map/reduce_scatter | solution.py:328
  919.1 6.3 fusion.31
  940.8 31.3 %all-reduce.4 = (bf16[288]{0:T(512)(128)(2,1)}, bf16[288]{0:T(512)(128)(2,1)}) all-reduce(bf16[288]{0:T(512)(128)(2,1)S(1)} %dynamic-slice.3, bf16[288]{0:T(512)(128)(2,1)} %dynamic-slice.5), channel_id=1, replica_groups=mesh['fsdp'=2,'ctx'=16] {'ctx'}, use_global_device_ids=true, to_apply=%region_14.15 | all-reduce | flops 576 | bytes 2304 | tf_op jit(solution)/shard_map/psum | solution.py:311
  979.2 53.7 %all-reduce.10.cloned.1.call-done = (bf16[288,576]{1,0:T(8,128)(2,1)}, bf16[288,192]{1,0:T(8,128)(2,1)}, bf16[288,192]{1,0:T(8,128)(2,1)}, bf16[288,576]{1,0:T(8...) async-done(((bf16[288,576]{1,0:T(8,128)(2,1)}, bf16[288,192]{1,0:T(8,128)(2,1)}, bf16[288,192]{1,0:T(8,128)(2,1)}, ...) | async-done | bytes 3538960 | tf_op jit(solution)/shard_map/psum | solution.py:312
  (231 shorter events, 162.0 us)
Async XLA Ops:
  7.2 245.3 %copy-start = (bf16[8,128,576]{1,2,0:T(8,128)(2,1)S(1)}, bf16[8,128,576]{1,2,0:T(8,128)(2,1)}, u32[]{:S(2)}) copy-start(bf16[8,128,576]{1,2,0:T(8,128)(2,1)} %param.25) | copy-start | bytes 3538948
  7.2 88.2 %all-gather.8.cloned.1.call-start = ((), (), s32[]{:S(2)}) async-start(), calls=%async_computation.10 | async-start | bytes 6684672 | tf_op jit(solution)/shard_map/all_gather | solution.py:170
  15.4 37.1 %copy-start.41 = (f32[576]{0:T(1024)}, f32[576]{0:T(1024)S(1)}, u32[]{:S(2)}) copy-start(f32[576]{0:T(1024)S(1)} %convert_element_type.206) | copy-start | bytes 6916
  16.9 8.5 copy-start.39
  16.9 35.6 %copy-start.45 = (f32[8,128]{1,0:T(8,128)}, f32[8,128]{1,0:T(8,128)S(1)}, u32[]{:S(2)}) copy-start(f32[8,128]{1,0:T(8,128)S(1)} %get-tuple-element.330) | copy-start | bytes 12292
  22.6 8.5 copy-start.9
  25.4 136.6 %all-gather.6.cloned.1.call-start = ((), (), s32[]{:S(2)}) async-start(), calls=%async_computation.9 | async-start | bytes 6684672 | tf_op jit(solution)/shard_map/all_gather | solution.py:169
  31.1 23.7 %copy-start.34 = (f32[128,32]{0,1:T(8,128)}, f32[128,32]{0,1:T(8,128)S(1)}, u32[]{:S(2)}) copy-start(f32[128,32]{0,1:T(8,128)S(1)} %get-tuple-element.333) | copy-start | bytes 49156
  32.6 175.8 %all-gather.12.cloned.1.call-start = ((), (), s32[]{:S(2)}) async-start(), calls=%async_computation.12 | async-start | bytes 2654208 | tf_op jit(solution)/shard_map/all_gather | solution.py:185
  33.3 188.2 %all-gather.10.cloned.1.call-start = ((), (), s32[]{:S(2)}) async-start(), calls=%async_computation.11 | async-start | bytes 2654208 | tf_op jit(solution)/shard_map/all_gather | solution.py:184
  33.9 218.5 %all-gather.14.cloned.1.call-start = ((), (), s32[]{:S(2)}) async-start(), calls=%async_computation.13 | async-start | bytes 2654208 | tf_op jit(solution)/shard_map/all_gather | solution.py:186
  34.5 634.3 %reduce-scatter.28.cloned.1.call-start = ((), (), s32[]{:S(2)}) async-start(), calls=%async_computation.21 | async-start | bytes 6684672
  42.0 12.8 %copy-start.15 = (bf16[576,576]{1,0:T(8,128)(2,1)}, bf16[576,576]{1,0:T(8,128)(2,1)S(1)}, u32[]{:S(2)}) copy-start(bf16[576,576]{1,0:T(8,128)(2,1)S(1)} %all_gather.38) | copy-start | bytes 1990660
  252.5 10.2 copy-start.49
  292.4 6.5 copy-start.1
  304.7 12.3 %copy-start.4 = (f32[8,128,3,3,64]{1,4,3,2,0:T(8,128)S(1)}, f32[8,128,3,3,64]{1,4,3,2,0:T(8,128)}, u32[]{:S(2)}) copy-start(f32[8,128,3,3,64]{1,4,3,2,0:T(8,128)} %get-tuple-element.544) | copy-start | bytes 7077892 | tf_op jit(solution)/shard_map/while
  322.6 7.9 copy-start.5
  322.6 7.9 copy-start.7
  359.5 398.3 %reduce-scatter.30.cloned.1.call-start = ((), (), s32[]{:S(2)}) async-start(), calls=%async_computation.22 | async-start | bytes 6684672
  386.1 390.8 %reduce-scatter.20.cloned.1.call-start = ((), (), s32[]{:S(2)}) async-start(), calls=%async_computation.17 | async-start | bytes 1105920 | tf_op jit(solution)/shard_map/reduce_scatter | solution.py:334
  390.4 406.3 %reduce-scatter.14.cloned.1.call-start = ((), (), s32[]{:S(2)}) async-start(), calls=%async_computation.14 | async-start | bytes 1105920 | tf_op jit(solution)/shard_map/reduce_scatter | solution.py:325
  395.6 432.1 %reduce-scatter.22.cloned.1.call-start = ((), (), s32[]{:S(2)}) async-start(), calls=%async_computation.18 | async-start | bytes 2654208 | tf_op jit(solution)/shard_map/reduce_scatter | solution.py:340
  400.8 458.1 %reduce-scatter.24.cloned.1.call-start = ((), (), s32[]{:S(2)}) async-start(), calls=%async_computation.19 | async-start | bytes 2654208 | tf_op jit(solution)/shard_map/reduce_scatter | solution.py:343
  405.9 483.9 %reduce-scatter.26.cloned.1.call-start = ((), (), s32[]{:S(2)}) async-start(), calls=%async_computation.20 | async-start | bytes 2654208 | tf_op jit(solution)/shard_map/reduce_scatter | solution.py:346
  411.1 493.1 %reduce-scatter.18.cloned.1.call-start = ((), (), s32[]{:S(2)}) async-start(), calls=%async_computation.16 | async-start | bytes 442368 | tf_op jit(solution)/shard_map/reduce_scatter | solution.py:331
  670.8 91.8 %copy-start.37 = (f32[128,32]{0,1:T(8,128)S(1)}, f32[128,32]{0,1:T(8,128)}, u32[]{:S(2)}) copy-start(f32[128,32]{0,1:T(8,128)} %get-tuple-element.331) | copy-start | bytes 49156
  762.4 156.7 %reduce-scatter.16.cloned.1.call-start = ((), (), s32[]{:S(2)}) async-start(), calls=%async_computation.15 | async-start | bytes 442368 | tf_op jit(solution)/shard_map/reduce_scatter | solution.py:328
  765.1 267.9 %all-reduce.10.cloned.1.call-start = ((), (), s32[]{:S(2)}) async-start(), calls=%async_computation.23 | async-start | bytes 7372800 | tf_op jit(solution)/shard_map/psum | solution.py:312
  919.1 6.3 copy-start.16
  919.1 6.3 copy-start.27
  931.5 43.1 %copy-start.23 = (bf16[72,8,8,128]{3,2,1,0:T(8,128)(2,1)S(1)}, bf16[72,8,8,128]{3,2,1,0:T(8,128)(2,1)}, u32[]{:S(2)}) copy-start(bf16[72,8,8,128]{3,2,1,0:T(8,128)(2,1)} %fusion.31) | copy-start | bytes 3538948
  1033.0 7.2 copy-start.32
  (35 other events, 89.1 us)
Sparse Core Ops, SparseCore 0:
  25.5 69.8 all-gather.7
  98.1 63.8 all-gather.5
  163.5 27.1 all-gather.11
  192.1 29.4 all-gather.9
  223.0 29.4 all-gather.13
  359.6 309.1 reduce-scatter.27
  673.3 84.4 reduce-scatter.29
  760.1 16.8 reduce-scatter.19
  779.8 16.8 reduce-scatter.13
  799.4 28.2 reduce-scatter.21
  830.6 28.2 reduce-scatter.23
  861.6 28.2 reduce-scatter.25
  892.1 12.0 reduce-scatter.17
  907.0 12.0 reduce-scatter.15
  924.3 108.6 all-reduce.9
where the time goes:
time: 1060 us; the launch traced here: 1050 us
  waiting for transfers between devices  688 us (65%)
  matrix products  132 us (12%)
  local copies, waits for them, and re-layouts  104 us (10%)
  blocking collectives  66.8 us (6%)
  other arithmetic  42.6 us (4%)
  between operations  16 us (2%)
    unnamed x17, waiting for transfers between devices  347 us
    unnamed x108, local copies, waits for them, and re-layouts  72.1 us
    all_gather x1, waiting for transfers between devices, local(): lax.all_gather(key_rot, 'ctx', axis=1, tiled=True)  66.6 us
    psum x1, waiting for transfers between devices, local(): lax.psum(local_grads[1].astype(jnp.bfloat16), 'ctx').astype(jnp.float32)  53.7 us
    all_gather x1, waiting for transfers between devices, local(): lax.all_gather(value_loc, 'ctx', axis=1, tiled=True)  37.9 us
    psum x1, blocking collectives, local(): lax.psum(local_grads[0].astype(jnp.bfloat16), 'ctx').astype(jnp.float32)  31.3 us
    reduce_scatter x1, waiting for transfers between devices, local(): lax.psum_scatter(summed_grads[7].astype(jnp.bfloat16), 'fsdp', scatter_di...  31.2 us
    reduce_scatter x1, waiting for transfers between devices, local(): lax.psum_scatter(summed_grads[8].astype(jnp.bfloat16), 'fsdp', scatter_di...  31 us
  transfers between devices with their start and end apart: 15, of which 14 were waited for; matrix products, arithmetic and copies ran while one was open for 14% of the time, Pallas kernels for 0%

commit v1 on v0

v1 whole, which is shorter than its diff:
```python
import jax, functools
import jax.numpy as jnp
from jax import lax
from jax.experimental import pallas as pl
from jax.experimental.pallas import tpu as pltpu
F32=jnp.float32; BF=jnp.bfloat16
NT=(((1,),(1,)),((),()))
NN=(((1,),(0,)),((),()))
def mm(a,b,dims=NN):
    return lax.dot_general(a,b,dims,preferred_element_type=F32)

def heads_of(ref, kv, group):
    return jnp.concatenate([ref[(kv*group+h)*64:(kv*group+h+1)*64,:] for h in range(group)],axis=1)

def fwd_kernel(bias_ref, q_ref, kv_ref, o_ref, lse_ref, k_scr, m_scr, acc_scr, *, kvs, group, slots, rows):
    i=pl.program_id(0)
    kw=kvs*64
    @pl.when(i==0)
    def _():
        for s in range(slots):
            for h in range(kvs):
                k_scr[h,s]=kv_ref[s,h*64:(h+1)*64,:].T
    qs=[heads_of(q_ref,h,group) for h in range(kvs)]
    width=group*128
    m_scr[...]=jnp.full(m_scr.shape,-1e30,F32)
    acc_scr[...]=jnp.zeros(acc_scr.shape,F32)
    ones=jnp.ones((8,slots*128),BF)
    def chunk(c, masked):
        off=pl.multiple_of(c*128,128)
        for h in range(kvs):
            k=jnp.concatenate([k_scr[h,s,pl.ds(off,128),:] for s in range(slots)],axis=0)
            v=jnp.concatenate([kv_ref[s,kw+h*64:kw+(h+1)*64,pl.ds(off,128)] for s in range(slots)],axis=1)
            v=jnp.concatenate([v,ones],axis=0)
            st=mm(k,qs[h])
            if masked:
                b=bias_ref[...].reshape(slots*128,128)
                st=st+jnp.concatenate([b]*group,axis=1)
            m_old=m_scr[h:h+1,:]
            m_new=jnp.maximum(m_old,jnp.max(st,axis=0,keepdims=True))
            p=jnp.exp2(st-m_new).astype(BF)
            acc_scr[h]=acc_scr[h]*jnp.exp2(m_old-m_new)+mm(v,p)
            m_scr[h:h+1,:]=m_new
    def body(c,_):
        chunk(c,False); return 0
    lax.fori_loop(0,i,body,0)
    chunk(i,True)
    for h in range(kvs):
        acc=acc_scr[h]
        tot=acc[64:65,:]
        o=acc[:64,:]*(1.0/tot)
        lse=m_scr[h:h+1,:]+jnp.log2(tot)
        for g in range(group):
            r=h*group+g
            o_ref[r*64:(r+1)*64,:]=o[:,g*128:(g+1)*128]
            lse_ref[r:r+1,:]=lse[:,g*128:(g+1)*128]

def attn_fwd(bias, qT, kvT, kvs=3, group=3):
    slots,_,rows=kvT.shape
    n=rows//128
    heads=kvs*group
    return pl.pallas_call(
        functools.partial(fwd_kernel,kvs=kvs,group=group,slots=slots,rows=rows),
        grid=(n,),
        in_specs=[pl.BlockSpec((slots,128,128),lambda i:(0,0,0)),
                  pl.BlockSpec((heads*64,128),lambda i:(0,i)),
                  pl.BlockSpec((slots,2*kvs*64,rows),lambda i:(0,0,0))],
        out_specs=[pl.BlockSpec((heads*64,128),lambda i:(0,i)),
                   pl.BlockSpec((16,128),lambda i:(0,i))],
        out_shape=[jax.ShapeDtypeStruct((heads*64,rows),F32),jax.ShapeDtypeStruct((16,rows),F32)],
        scratch_shapes=[pltpu.VMEM((kvs,slots,rows,64),BF),pltpu.VMEM((8,group*128),F32),
                        pltpu.VMEM((kvs,72,group*128),F32)],
        compiler_params=pltpu.CompilerParams(vmem_limit_bytes=56*2**20),
        cost_estimate=pl.CostEstimate(flops=int(6e9),bytes_accessed=int(8e6),transcendentals=int(1e7)),
    )(bias,qT,kvT)

def bwd_kernel(bias_ref, q_ref, kv_ref, do_ref, lse_ref, rd_ref, dq_ref, dkv_ref, kv_scr, acc_scr, *, kvs, group, slots, rows, n):
    i=pl.program_id(0)
    kw=kvs*64
    @pl.when(i==0)
    def _():
        for s in range(slots):
            for h in range(2*kvs):
                kv_scr[h,s]=kv_ref[s,h*64:(h+1)*64,:].T
        acc_scr[...]=jnp.zeros(acc_scr.shape,F32)
    dq_ref[...]=jnp.zeros(dq_ref.shape,F32)
    qs=[heads_of(q_ref,h,group) for h in range(kvs)]
    dos=[heads_of(do_ref,h,group) for h in range(kvs)]
    lses=[jnp.concatenate([lse_ref[h*group+g:h*group+g+1,:] for g in range(group)],axis=1) for h in range(kvs)]
    rds=[jnp.concatenate([rd_ref[h*group+g:h*group+g+1,:] for g in range(group)],axis=1) for h in range(kvs)]
    def chunk(c, masked):
        off=pl.multiple_of(c*128,128)
        for h in range(kvs):
            k=jnp.concatenate([kv_scr[h,s,pl.ds(off,128),:] for s in range(slots)],axis=0)
            v=jnp.concatenate([kv_scr[kvs+h,s,pl.ds(off,128),:] for s in range(slots)],axis=0)
            kT=jnp.concatenate([kv_ref[s,h*64:(h+1)*64,pl.ds(off,128)] for s in range(slots)],axis=1)
            st=mm(k,qs[h])
            if masked:
                b=bias_ref[...].reshape(slots*128,128)
                st=st+jnp.concatenate([b]*group,axis=1)
            p=jnp.exp2(st-lses[h])
            dp=mm(v,dos[h])
            ds=(p*(dp-rds[h])).astype(BF)
            dk=mm(qs[h],ds,NT)
            dv=mm(dos[h],p.astype(BF),NT)
            dq=mm(kT,ds)
            for s in range(slots):
                acc_scr[s,h*64:(h+1)*64,pl.ds(off,128)]+=dk[:,s*128:(s+1)*128]
                acc_scr[s,kw+h*64:kw+(h+1)*64,pl.ds(off,128)]+=dv[:,s*128:(s+1)*128]
            for g in range(group):
                r=h*group+g
                dq_ref[r*64:(r+1)*64,:]+=dq[:,g*128:(g+1)*128]
    def body(c,_):
        chunk(c,False); return 0
    lax.fori_loop(0,i,body,0)
    chunk(i,True)
    @pl.when(i==n-1)
    def _():
        dkv_ref[...]=acc_scr[...]

def attn_bwd(bias, qT, kvT, doT, lse, rd, kvs=3, group=3):
    slots,_,rows=kvT.shape
    n=rows//128
    heads=kvs*group
    return pl.pallas_call(
        functools.partial(bwd_kernel,kvs=kvs,group=group,slots=slots,rows=rows,n=n),
        grid=(n,),
        in_specs=[pl.BlockSpec((slots,128,128),lambda i:(0,0,0)),
                  pl.BlockSpec((heads*64,128),lambda i:(0,i)),
                  pl.BlockSpec((slots,2*kvs*64,rows),lambda i:(0,0,0)),
                  pl.BlockSpec((heads*64,128),lambda i:(0,i)),
                  pl.BlockSpec((16,128),lambda i:(0,i)),
                  pl.BlockSpec((16,128),lambda i:(0,i))],
        out_specs=[pl.BlockSpec((heads*64,128),lambda i:(0,i)),
                   pl.BlockSpec((slots,2*kvs*64,rows),lambda i:(0,0,0))],
        out_shape=[jax.ShapeDtypeStruct((heads*64,rows),F32),jax.ShapeDtypeStruct((slots,2*kvs*64,rows),F32)],
        scratch_shapes=[pltpu.VMEM((2*kvs,slots,rows,64),BF),pltpu.VMEM((slots,2*kvs*64,rows),F32)],
        compiler_params=pltpu.CompilerParams(vmem_limit_bytes=56*2**20),
        cost_estimate=pl.CostEstimate(flops=int(15e9),bytes_accessed=int(16e6),transcendentals=int(1e7)),
    )(bias,qT,kvT,doT,lse,rd)


from jax.sharding import PartitionSpec as P

HEADS = 9
KV_HEADS = 3
HEAD_DIM = 64
EPSILON = 1e-05
THETA = 100000.0
NEGATIVE = -1e30
LOG2E = 1.4426950408889634
LN2 = 0.6931471805599453


def swap(x, axis, bit):
    n = lax.axis_size(axis)
    return lax.ppermute(x, axis, [(i, i ^ (1 << bit)) for i in range(n)])


def bit_of(axis, bit):
    return (lax.axis_index(axis) >> bit) & 1


def in_order(flag, mine, other, axis):
    return jnp.where(
        flag == 0,
        jnp.concatenate([mine, other], axis=axis),
        jnp.concatenate([other, mine], axis=axis),
    )


def gather_rows(shard, split):
    if lax.axis_size("fsdp") != 2:
        return lax.all_gather(shard, "fsdp", axis=0, tiled=True)
    core = bit_of("ctx", 0)
    half = shard.shape[split] // 2
    mine = lax.dynamic_slice_in_dim(shard, core * half, half, split)
    got = swap(mine, "fsdp", 0)
    other = in_order(core, got, swap(got, "ctx", 0), split)
    return in_order(bit_of("fsdp", 0), shard, other, 0)


def half_sum(x, axis, bit, dim):
    me = bit_of(axis, bit)
    half = x.shape[dim] // 2
    keep = lax.dynamic_slice_in_dim(x, me * half, half, dim)
    send = lax.dynamic_slice_in_dim(x, (1 - me) * half, half, dim)
    got = swap(send, axis, bit)
    return (keep.astype(F32) + got.astype(F32)).astype(BF)


def half_join(x, axis, bit, dim):
    return in_order(bit_of(axis, bit), x, swap(x, axis, bit), dim)


def reduce_rows(x):
    x = x.astype(BF)
    count = lax.axis_size("ctx")
    if lax.axis_size("fsdp") != 2 or count != 16:
        mine = lax.psum_scatter(x, "fsdp", scatter_dimension=0, tiled=True)
        return lax.psum(mine, "ctx").astype(F32)
    wide = x.shape[1] % 512 == 0
    if wide:
        stages = [("ctx", 0, 1), ("fsdp", 0, 0), ("ctx", 1, 1), ("ctx", 2, 0), ("ctx", 3, 0)]
    else:
        rows = x.shape[0]
        x = x.reshape(2, rows // 2, x.shape[1])
        stages = [("ctx", 0, 1), ("fsdp", 0, 0), ("ctx", 1, 1), ("ctx", 2, 1), ("ctx", 3, 1)]
    for axis, bit, dim in stages:
        x = half_sum(x, axis, bit, dim)
    for axis, bit, dim in reversed(stages):
        if axis == "ctx":
            x = half_join(x, axis, bit, dim)
    if not wide:
        x = x.reshape(rows // 2, x.shape[2])
    return x.astype(F32)


def rms_scale(values):
    return lax.rsqrt(jnp.mean(values * values, axis=-1, keepdims=True) + EPSILON)


def rotate_t(values, cosine, sine):
    halves = values.shape[1] // 2
    a, b = values[:, :halves], values[:, halves:]
    return jnp.concatenate([a * cosine - b * sine, b * cosine + a * sine], axis=1)


def norm_backward(grad_hidden, normed, scale_rows, gain_rows):
    grad_gain = jnp.sum(grad_hidden * normed, axis=0)
    grad_normed = grad_hidden * gain_rows
    inner_mean = jnp.mean(grad_normed * normed, axis=-1, keepdims=True)
    return grad_gain, scale_rows * (grad_normed - normed * inner_mean)


def local(tokens, gain_attn, w_query, w_key, w_value, w_out, gain_ffn, w_gate, w_up, w_down, cotangent):
    seqs, length, width = tokens.shape
    count = lax.axis_size("ctx")
    team = count // seqs
    sub = length // team
    rows = count * sub
    kv_width = KV_HEADS * HEAD_DIM
    index = lax.axis_index("ctx")
    place = index % team

    def spread(x):
        x = x.reshape(count, sub, width)
        return lax.all_to_all(x, "ctx", 0, 0, tiled=True).reshape(rows, width)

    def home(x):
        x = lax.all_to_all(x.reshape(count, sub, width), "ctx", 0, 0, tiled=True)
        return x.reshape(seqs, length, width)

    source_low = spread(tokens)
    gains = jnp.zeros((8, w_gate.shape[1]), BF)
    own = gain_attn.shape[0]
    gains = gains.at[0, :own].set(gain_attn).at[1, :own].set(gain_ffn)
    first = jnp.concatenate([w_query, w_key, w_value, w_out], axis=1)
    first = jnp.concatenate([first, gains], axis=0)
    first = gather_rows(first, 1).reshape(-1, own + 8, first.shape[1])
    gain_first = first[:, own, :own].reshape(width).astype(F32)
    gain_second = first[:, own + 1, :own].reshape(width).astype(F32)
    first = first[:, :own].reshape(width, first.shape[2])
    gate_w, up_w, down_w = gather_rows(w_gate, 1), gather_rows(w_up, 1), gather_rows(w_down, 0)
    cot_rows = spread(cotangent)
    qkv_cols = width + 2 * kv_width
    qkv_w, out_w = first[:, :qkv_cols], first[:, qkv_cols:]

    row = jnp.arange(rows, dtype=jnp.int32)
    position = (row // sub) * length + place * sub + row % sub
    frequency = THETA ** (-jnp.arange(HEAD_DIM // 2, dtype=F32) * 2.0 / HEAD_DIM)
    angles = frequency[:, None] * position.astype(F32)[None, :]
    cosine, sine = jnp.cos(angles), jnp.sin(angles)

    source = source_low.astype(F32)
    scale_one = rms_scale(source)
    normed_one = source * scale_one
    hidden_one = (normed_one * gain_first).astype(BF)
    qkv = lax.dot_general(qkv_w, hidden_one, (((0,), (1,)), ((), ())), preferred_element_type=F32)
    query = rotate_t(qkv[:width].reshape(HEADS, HEAD_DIM, rows), cosine, sine)
    query = (query * (HEAD_DIM**-0.5 * LOG2E)).astype(BF).reshape(width, rows)
    key = rotate_t(qkv[width : width + kv_width].reshape(KV_HEADS, HEAD_DIM, rows), cosine, sine)
    kv_own = jnp.concatenate([key.reshape(kv_width, rows), qkv[width + kv_width :]], axis=0).astype(BF)
    groups = [[t * team + p for p in range(team)] for t in range(seqs)]
    if team == 2:
        kv_all = jnp.stack([kv_own, swap(kv_own, "ctx", 0)])
        slots = jnp.stack([place, 1 - place])
    else:
        kv_all = lax.all_gather(kv_own, "ctx", axis=0, axis_index_groups=groups)
        slots = jnp.arange(team)
    head_row = jnp.arange(128, dtype=jnp.int32)
    base = (head_row // sub) * length + head_row % sub
    key_pos = base[None, :] + slots[:, None] * sub
    query_pos = base + place * sub
    bias = jnp.where(key_pos[:, :, None] <= query_pos[None, None, :], 0.0, NEGATIVE).astype(F32)

    attended, log_total = attn_fwd(bias, query, kv_all)
    mixed = attended.astype(BF)
    residual = source + lax.dot_general(mixed, out_w, (((0,), (0,)), ((), ())), preferred_element_type=F32)
    scale_two = rms_scale(residual)
    normed_two = residual * scale_two
    hidden_two = (normed_two * gain_second).astype(BF)
    gate_lin = mm(hidden_two, gate_w)
    up_lin = mm(hidden_two, up_w)
    sigmoid_gate = jax.nn.sigmoid(gate_lin)
    silu_gate = gate_lin * sigmoid_gate
    activated = (silu_gate * up_lin).astype(BF)
    mixed_out = home((residual + mm(activated, down_w)).astype(BF))

    grad_act = mm(cot_rows, down_w, NT)
    grad_down = mm(activated.T, cot_rows)
    d_gate = (grad_act * up_lin * sigmoid_gate * (1.0 + gate_lin * (1.0 - sigmoid_gate))).astype(BF)
    d_up = (grad_act * silu_gate).astype(BF)
    grad_gate = mm(hidden_two.T, d_gate)
    grad_up = mm(hidden_two.T, d_up)
    d_hidden_two = mm(d_gate, gate_w, NT) + mm(d_up, up_w, NT)
    grad_gain_ffn, d_norm = norm_backward(d_hidden_two, normed_two, scale_two, gain_second)
    d_residual = cot_rows.astype(F32) + d_norm
    d_res_low = d_residual.astype(BF)
    grad_out = mm(mixed, d_res_low)
    d_attended = lax.dot_general(out_w, d_res_low, NT, preferred_element_type=F32).astype(BF)
    row_dot = jnp.sum((d_attended.astype(F32) * attended).reshape(HEADS, HEAD_DIM, rows), axis=1)
    row_dot = jnp.pad(row_dot, ((0, 16 - HEADS), (0, 0)))
    own_down, own_gate, own_up = reduce_rows(grad_down), reduce_rows(grad_gate), reduce_rows(grad_up)

    d_query, d_kv = attn_bwd(bias, query, kv_all, d_attended, log_total, row_dot)
    d_query = d_query * (HEAD_DIM**-0.5)
    if team == 2:
        d_kv = d_kv[0] + swap(d_kv[1].astype(BF), "ctx", 0).astype(F32)
    else:
        d_kv = lax.psum_scatter(
            d_kv.astype(BF), "ctx", scatter_dimension=0, axis_index_groups=groups
        ).astype(F32)
    d_key = d_kv[:kv_width] * LN2
    d_query = rotate_t(d_query.reshape(HEADS, HEAD_DIM, rows), cosine, -sine).reshape(width, rows)
    d_key = rotate_t(d_key.reshape(KV_HEADS, HEAD_DIM, rows), cosine, -sine).reshape(kv_width, rows)
    d_qkv = jnp.concatenate([d_query, d_key, d_kv[kv_width:]], axis=0).astype(BF)
    grad_qkv = lax.dot_general(hidden_one, d_qkv, (((0,), (1,)), ((), ())), preferred_element_type=F32)
    d_hidden_one = lax.dot_general(d_qkv, qkv_w, (((0,), (1,)), ((), ())), preferred_element_type=F32)
    grad_gain_attn, d_norm = norm_backward(d_hidden_one, normed_one, scale_one, gain_first)
    grad_tokens = home((d_residual + d_norm).astype(BF))
    own_first = reduce_rows(jnp.concatenate([grad_qkv, grad_out], axis=1))
    gain_grads = jnp.stack([grad_gain_attn, grad_gain_ffn], axis=1).astype(BF)
    gain_grads = lax.psum(gain_grads, ("fsdp", "ctx"))
    gain_grads = lax.dynamic_slice_in_dim(gain_grads, lax.axis_index("fsdp") * own, own, 0).astype(F32)
    return (
        mixed_out,
        grad_tokens,
        gain_grads[:, 0],
        own_first[:, :width],
        own_first[:, width : width + kv_width],
        own_first[:, width + kv_width : qkv_cols],
        own_first[:, qkv_cols:],
        gain_grads[:, 1],
        own_gate,
        own_up,
        own_down,
    )


def solution(mesh):
    rows, flat, seq = P("fsdp", None), P("fsdp"), P("fsdp", "ctx", None)
    return jax.shard_map(
        local,
        mesh=mesh,
        in_specs=(seq, flat, rows, rows, rows, rows, flat, rows, rows, rows, seq),
        out_specs=(seq, seq, flat, rows, rows, rows, rows, flat, rows, rows, rows),
        check_vma=False,
    )
```

time: 1060 us -> 474 us (0.45)
  waiting for transfers between devices: 688 us -> 105 us
  Pallas kernels: 0 us -> 83.2 us
  matrix products: 132 us -> 54.2 us
  starting transfers between devices: 0.78 us -> 76.7 us
  local copies, waits for them, and re-layouts: 104 us -> 54.2 us
  blocking collectives: 66.8 us -> 39.8 us
  between operations: 16 us -> 1.87 us
  other arithmetic: 42.6 us -> 53.5 us
    unnamed x17 -> x0, waiting for transfers between devices: 347 us -> none
    reduce_scatter x7 -> x0, waiting for transfers between devices: 153 us -> none  [the longest x1 31.2 us: local(): lax.psum_scatter(summed_grads[7].astype(jnp.bfloat16), 'fsdp', scatter_di...]
    all_gather x5 -> x0, waiting for transfers between devices: 134 us -> none  [the longest x1 66.6 us: local(): lax.all_gather(key_rot, 'ctx', axis=1, tiled=True)]
    ppermute x0 -> x46, waiting for transfers between devices: none -> 92.1 us  [swap(): return lax.ppermute(x, axis, [(i, i ^ 1 << bit) for i in range(n)])]
    pallas_call x0 -> x2, Pallas kernels: none -> 83.2 us  [the longest x1 45.2 us: attn_bwd(): pl.pallas_call(functools.partial(bwd_kernel, kvs=kvs, group=group, slots=...]
    dot_general x28 -> x15, matrix products: 132 us -> 54.2 us  [the longest x10 40.7 us: mm(): return lax.dot_general(a, b, dims, preferred_element_type=F32)]
    psum x1 -> x0, waiting for transfers between devices: 53.7 us -> none  [local(): lax.psum(local_grads[1].astype(jnp.bfloat16), 'ctx').astype(jnp.float32)]
    unnamed x108 -> x89, local copies, waits for them, and re-layouts: 72.1 us -> 19.4 us
  transfers between devices with their start and end apart: 15 -> 50, of which waited for: 14 -> 19; matrix products, arithmetic and copies ran while one was open for 14% -> 22% of each run, Pallas kernels for 0% -> 10%
where the time goes in v1:
time: 474 us; the launch traced here: 468 us
  waiting for transfers between devices  105 us (22%)
  Pallas kernels  83.2 us (18%)
  starting transfers between devices  76.7 us (16%)
  local copies, waits for them, and re-layouts  54.2 us (11%)
  matrix products  54.2 us (11%)
  other arithmetic  53.5 us (11%)
  blocking collectives  39.8 us (8%)
    ppermute x46, waiting for transfers between devices, swap(): return lax.ppermute(x, axis, [(i, i ^ 1 << bit) for i in range(n)])  92.1 us
    pallas_call x1, Pallas kernels, attn_bwd(): pl.pallas_call(functools.partial(bwd_kernel, kvs=kvs, group=group, slots=...  45.2 us
    ppermute x46, starting transfers between devices, swap(): return lax.ppermute(x, axis, [(i, i ^ 1 << bit) for i in range(n)])  43.5 us
    dot_general x10, matrix products, mm(): return lax.dot_general(a, b, dims, preferred_element_type=F32)  40.7 us
    psum x1, blocking collectives, local(): gain_grads = lax.psum(gain_grads, ('fsdp', 'ctx'))  39.8 us
    pallas_call x1, Pallas kernels, attn_fwd(): pl.pallas_call(functools.partial(fwd_kernel, kvs=kvs, group=group, slots=...  38.1 us
    all_to_all x2, starting transfers between devices, home(): x = lax.all_to_all(x.reshape(count, sub, width), 'ctx', 0, 0, tiled=True)  20.1 us
    unnamed x89, local copies, waits for them, and re-layouts  19.4 us
  transfers between devices with their start and end apart: 50, of which 19 were waited for; matrix products, arithmetic and copies ran while one was open for 22% of the time, Pallas kernels for 10%

profile of v1, /device:TPU:1, one launch (start us, length us, event | category | flops | bytes accessed | tf_op | source)
XLA Modules:
  0.0 468.3 jit_solution(9498488602526796849)
XLA Ops:
  7.6 6.8 %all-to-all-start = ((bf16[16,64,576]{2,1,0:T(8,128)(2,1)}), bf16[16,64,576]{2,1,0:T(8,128)(2,1)S(1)}, u32[]{:S(2)}, u32[]{:S(2)}) async-start(bf16[16,64,576]{2,1,0:T(8,128)(2,1)} %bitcast), calls=%async_computation | async-start | bytes 2621440 | tf_op jit(solution)/shard_map/all_to_all | solution.py:247
  22.8 14.9 %collective-permute-done.7 = bf16[384,576]{0,1:T(8,128)(2,1)} collective-permute-done((bf16[384,576]{0,1:T(8,128)(2,1)}, bf16[384,576]{0,1:T(8,128)(2,1)}, u32[]{:S(2)}, u32[]{:S(2)}) %collective-permute-start.7) | collective-permute-done | bytes 442400 | tf_op jit(solution)/shard_map/ppermute | solution.py:156
  39.1 8.1 %collective-permute-done.5 = bf16[288,768]{1,0:T(8,128)(2,1)} collective-permute-done((bf16[288,768]{1,0:T(8,128)(2,1)}, bf16[288,768]{1,0:T(8,128)(2,1)}, u32[]{:S(2)}, u32[]{:S(2)}) %collective-permute-start.5) | collective-permute-done | bytes 442400 | tf_op jit(solution)/shard_map/ppermute | solution.py:156
  51.2 2.7 maximum_select_fusion.7
  59.3 6.3 %all-to-all-start.2 = ((bf16[16,64,576]{2,1,0:T(8,128)(2,1)}), bf16[16,64,576]{2,1,0:T(8,128)(2,1)}, u32[]{:S(2)}, u32[]{:S(2)}) async-start(bf16[16,64,576]{2,1,0:T(8,128)(2,1)} %bitcast.15), calls=%async_computation.2 | async-start | bytes 2621440 | tf_op jit(solution)/shard_map/all_to_all | solution.py:247
  71.9 3.1 fusion.8
  80.8 12.6 %all-to-all-done.2 = bf16[16,64,576]{2,1,0:T(8,128)(2,1)} async-done(((bf16[16,64,576]{2,1,0:T(8,128)(2,1)}), bf16[16,64,576]{2,1,0:T(8,128)(2,1)}, u32[]{:S(2)}, u32[]{:S(2)}) %all-to-all-start.2) | async-done | bytes 1179680 | tf_op jit(solution)/shard_map/all_to_all | solution.py:247
  96.2 7.7 %fusion.24 = f32[1536,1024]{0,1:T(8,128)} fusion(bf16[1024,576]{1,0:T(8,128)(2,1)} %bitcast.16, bf16[768,576]{0,1:T(8,128)(2,1)} %maximum_select_fusion.7, bf16[768,576]{0,1:T(8,128)(2,1)} %param.24, pred[]{:T(512)S(6)} %eq.16), kind=kOutput, calls=%fused_computation.104 | convolution fusion | flops 1819901952 | bytes 9240577 | tf_op jit(solution)/shard_map/dot_general | solution.py:10
  106.3 38.1 %shard_map.194 = (f32[576,1024]{1,0:T(8,128)}, f32[16,1024]{1,0:T(8,128)}) custom-call(f32[2,128,128]{2,1,0:T(8,128)} %compare_select_fusion.bias_ref, bf16[576,1024]{1,0:T(8,128)(2,1)} %bitcast.81, bf16[2,384,1024]{2,1,0:T(8,128)(2,1)} %pad_maximum_fusion.1.kv_ref), custom_call_target="tpu_custom_call" | custom-call | flops 6000000000 | bytes 8000000 | tf_op jit(solution)/shard_map/pallas_call | solution.py:61
  144.4 3.2 multiply_reduce_fusion.5
  150.0 2.7 fusion.27
  152.9 7.5 %fusion.2 = (bf16[1024,1536]{1,0:T(8,128)(2,1)}, bf16[1024,1536]{1,0:T(8,128)(2,1)}, bf16[1024,1536]{1,0:T(8,128)(2,1)S(1)}) fusion(f32[1536,1024]{0,1:T(8,128)S(1)} %bitcast.91, f32[1024,1536]{1,0:T(8,128)S(1)} %fusion.27, bf16[1024,576]{0,1:T(8,128)(2,1)S(1)} %multiply_convert_fusion.1, bf16[288,1536]{1,0:T(8,128)(2,1)S(1)} %copy-done.29, ...), kind=kOutput, calls=%fused_computation.4 | convolution fusion | flops 1843494912 | bytes 24969216 | tf_op jit(solution)/shard_map/dot_general | solution.py:10
  160.5 5.3 %convolution_convert_fusion.1 = bf16[576,1536]{1,0:T(8,128)(2,1)} fusion(bf16[1024,576]{0,1:T(8,128)(2,1)S(1)} %multiply_convert_fusion.1, bf16[1024,1536]{1,0:T(8,128)(2,1)} %get-tuple-element.63), kind=kOutput, calls=%fused_computation.10 | convolution fusion | flops 1812824064 | bytes 6094848 | tf_op jit(solution)/shard_map/dot_general | solution.py:10
  165.7 3.5 fusion.25
  169.2 4.7 %convolution_convert_fusion = bf16[1536,576]{0,1:T(8,128)(2,1)} fusion(bf16[1024,1536]{1,0:T(8,128)(2,1)S(1)} %get-tuple-element.64, bf16[1024,576]{1,0:T(8,128)(2,1)} %bitcast.16), kind=kOutput, calls=%fused_computation.9 | convolution fusion | flops 1812824064 | bytes 6094848 | tf_op jit(solution)/shard_map/dot_general | solution.py:10
  174.0 3.1 add_convert_fusion.1
  177.1 4.5 reshape.768
  191.0 3.1 multiply_reduce_fusion.1
  195.8 4.0 convert_multiply_fusion
  202.4 45.2 %shard_map.195 = (f32[576,1024]{1,0:T(8,128)}, f32[2,384,1024]{2,1,0:T(8,128)}) custom-call(f32[2,128,128]{2,1,0:T(8,128)} %compare_select_fusion.bias_ref, bf16[576,1024]{1,0:T(8,128)(2,1)} %bitcast.82, bf16[2,384,1024]{2,1,0:T(8,128)(2,1)} %pad_maximum_fusion.1.kv_ref, bf16[576,1024]{1,0:T(8,128)(2,1)} %get-tuple-element.86.do_ref, ...), custom_call_target="tpu_custom_call" | custom-call | flops 15000000512 | bytes 16000000 | tf_op jit(solution)/shard_map/pallas_call | solution.py:124
  247.6 3.5 broadcast_multiply_fusion
  255.5 8.1 %all-to-all-start.1 = ((bf16[16,64,576]{2,1,0:T(8,128)(2,1)}), bf16[16,64,576]{2,1,0:T(8,128)(2,1)}, u32[]{:S(2)}, u32[]{:S(2)}) async-start(bf16[16,64,576]{2,1,0:T(8,128)(2,1)} %bitcast.72), calls=%async_computation.1 | async-start | bytes 2621440 | tf_op jit(solution)/shard_map/all_to_all | solution.py:250
  281.3 39.8 %psum.7 = bf16[576,2]{0,1:T(2,128)(2,1)S(1)} all-reduce(bf16[576,2]{0,1:T(2,128)(2,1)S(1)} %pad_maximum_fusion.7), channel_id=1, replica_groups=mesh['fsdp'=2,'ctx'=16] {'fsdp','ctx'}, use_global_device_ids=true, to_apply=%region_7.8 | all-reduce | flops 1152 | bytes 4608 | tf_op jit(solution)/shard_map/psum | solution.py:343
  329.9 4.6 collective-permute-done.38
  336.0 8.0 %collective-permute-done.29 = bf16[288,768]{1,0:T(8,128)(2,1)S(1)} collective-permute-done((bf16[288,768]{1,0:T(8,128)(2,1)S(1)}, bf16[288,768]{1,0:T(8,128)(2,1)S(1)}, u32[]{:S(2)}, u32[]{:S(2)}) %collective-permute-start.29) | collective-permute-done | bytes 442400 | tf_op jit(solution)/shard_map/ppermute | solution.py:156
  345.4 8.1 %collective-permute-done.20 = bf16[288,768]{1,0:T(8,128)(2,1)S(1)} collective-permute-done((bf16[288,768]{1,0:T(8,128)(2,1)S(1)}, bf16[288,768]{1,0:T(8,128)(2,1)S(1)}, u32[]{:S(2)}, u32[]{:S(2)}) %collective-permute-start.20) | collective-permute-done | bytes 442400 | tf_op jit(solution)/shard_map/ppermute | solution.py:156
  373.9 5.3 %collective-permute-done.42 = bf16[1,48,576]{1,2,0:T(8,128)(2,1)S(1)} collective-permute-done((bf16[1,48,576]{1,2,0:T(8,128)(2,1)S(1)}, bf16[1,48,576]{1,2,0:T(8,128)(2,1)S(1)}, u32[]{:S(2)}, u32[]{:S(2)}) %collective-permute-start.42) | collective-permute-done | bytes 55328 | tf_op jit(solution)/shard_map/ppermute | solution.py:156
  390.1 12.0 %all-to-all-start.3 = ((bf16[16,64,576]{2,1,0:T(8,128)(2,1)}), bf16[16,64,576]{2,1,0:T(8,128)(2,1)S(1)}, u32[]{:S(2)}, u32[]{:S(2)}) async-start(bf16[16,64,576]{2,1,0:T(8,128)(2,1)} %bitcast.25), calls=%async_computation.3 | async-start | bytes 2621440 | tf_op jit(solution)/shard_map/all_to_all | solution.py:250
  405.9 30.1 %collective-permute-done.14 = bf16[72,384]{1,0:T(8,128)(2,1)S(1)} collective-permute-done((bf16[72,384]{1,0:T(8,128)(2,1)S(1)}, bf16[72,384]{1,0:T(8,128)(2,1)S(1)}, u32[]{:S(2)}, u32[]{:S(2)}) %collective-permute-start.14) | collective-permute-done | bytes 55328 | tf_op jit(solution)/shard_map/ppermute | solution.py:156
  446.5 3.2 collective-permute-start.27
  455.2 2.6 fusion.14
  460.4 2.6 fusion.13
  (304 shorter events, 151.6 us)
Async XLA Ops:
  4.0 47.2 %collective-permute-start = (bf16[296,768]{1,0:T(8,128)(2,1)S(1)}, bf16[296,768]{1,0:T(8,128)(2,1)S(1)}, u32[]{:S(2)}, u32[]{:S(2)}) collective-permute-start(bf16[296,768]{1,0:T(8,128)(2,1)S(1)} %fusion.23), channel_id=1, source_target_pairs={{0,16},{16,0},{1,17},{17,1},{2,18},{18,2},{3,19},{19,3},{4,20},{20... | collective-permute-start | bytes 1363976 | tf_op jit(solution)/shard_map/ppermute | solution.py:156
  7.6 51.8 %all-to-all-start = ((bf16[16,64,576]{2,1,0:T(8,128)(2,1)}), bf16[16,64,576]{2,1,0:T(8,128)(2,1)S(1)}, u32[]{:S(2)}, u32[]{:S(2)}) async-start(bf16[16,64,576]{2,1,0:T(8,128)(2,1)} %bitcast), calls=%async_computation | async-start | bytes 2621440 | tf_op jit(solution)/shard_map/all_to_all | solution.py:247
  16.1 23.0 %collective-permute-start.3 = (bf16[288,768]{1,0:T(8,128)(2,1)}, bf16[288,768]{1,0:T(8,128)(2,1)}, u32[]{:S(2)}, u32[]{:S(2)}) collective-permute-start(bf16[288,768]{1,0:T(8,128)(2,1)} %constant_dynamic-slice_fusion.23), channel_id=1, source_target_pairs={{0,16},{16,0},{1,17},{17,1},{2,18},{18,2},{3,19},{19,3},{4,20},{20... | collective-permute-start | bytes 1327112 | tf_op jit(solution)/shard_map/ppermute | solution.py:156
  18.2 19.5 %collective-permute-start.7 = (bf16[384,576]{0,1:T(8,128)(2,1)}, bf16[384,576]{0,1:T(8,128)(2,1)}, u32[]{:S(2)}, u32[]{:S(2)}) collective-permute-start(bf16[384,576]{0,1:T(8,128)(2,1)} %constant_dynamic-slice_fusion.21), channel_id=1, source_target_pairs={{0,16},{16,0},{1,17},{17,1},{2,18},{18,2},{3,19},{19,3},{4,20},{20... | collective-permute-start | bytes 1327112 | tf_op jit(solution)/shard_map/ppermute | solution.py:156
  21.2 25.9 %collective-permute-start.5 = (bf16[288,768]{1,0:T(8,128)(2,1)}, bf16[288,768]{1,0:T(8,128)(2,1)}, u32[]{:S(2)}, u32[]{:S(2)}) collective-permute-start(bf16[288,768]{1,0:T(8,128)(2,1)} %constant_dynamic-slice_fusion.22), channel_id=1, source_target_pairs={{0,16},{16,0},{1,17},{17,1},{2,18},{18,2},{3,19},{19,3},{4,20},{20... | collective-permute-start | bytes 1327112 | tf_op jit(solution)/shard_map/ppermute | solution.py:156
  37.7 13.5 %collective-permute-start.8 = (bf16[384,576]{0,1:T(8,128)(2,1)}, bf16[384,576]{0,1:T(8,128)(2,1)}, u32[]{:S(2)}, u32[]{:S(2)}) collective-permute-start(bf16[384,576]{0,1:T(8,128)(2,1)} %collective-permute-done.7), channel_id=1, source_target_pairs={{0,1},{1,0},{2,3},{3,2},{4,5},{5,4},{6,7},{7,6},{8,9},{9,8},{10,11... | collective-permute-start | bytes 1327112 | tf_op jit(solution)/shard_map/ppermute | solution.py:156
  39.1 14.8 %collective-permute-start.4 = (bf16[288,768]{1,0:T(8,128)(2,1)}, bf16[288,768]{1,0:T(8,128)(2,1)}, u32[]{:S(2)}, u32[]{:S(2)}) collective-permute-start(bf16[288,768]{1,0:T(8,128)(2,1)} %collective-permute-done.3), channel_id=1, source_target_pairs={{0,1},{1,0},{2,3},{3,2},{4,5},{5,4},{6,7},{7,6},{8,9},{9,8},{10,11... | collective-permute-start | bytes 1327112 | tf_op jit(solution)/shard_map/ppermute | solution.py:156
  59.3 34.1 %all-to-all-start.2 = ((bf16[16,64,576]{2,1,0:T(8,128)(2,1)}), bf16[16,64,576]{2,1,0:T(8,128)(2,1)}, u32[]{:S(2)}, u32[]{:S(2)}) async-start(bf16[16,64,576]{2,1,0:T(8,128)(2,1)} %bitcast.15), calls=%async_computation.2 | async-start | bytes 2621440 | tf_op jit(solution)/shard_map/all_to_all | solution.py:247
  78.0 25.8 %collective-permute-start.2 = (bf16[384,1024]{1,0:T(8,128)(2,1)}, bf16[384,1024]{1,0:T(8,128)(2,1)}, u32[]{:S(2)}, u32[]{:S(2)}) collective-permute-start(bf16[384,1024]{1,0:T(8,128)(2,1)} %pad_maximum_fusion.5), channel_id=1, source_target_pairs={{0,1},{1,0},{2,3},{3,2},{4,5},{5,4},{6,7},{7,6},{8,9},{9,8},{10,11... | collective-permute-start | bytes 2359304 | tf_op jit(solution)/shard_map/ppermute | solution.py:156
  184.8 137.0 %collective-permute-start.37 = (bf16[2,384,576]{1,2,0:T(8,128)(2,1)}, bf16[2,384,576]{1,2,0:T(8,128)(2,1)}, u32[]{:S(2)}, u32[]{:S(2)}) collective-permute-start(bf16[2,384,576]{1,2,0:T(8,128)(2,1)} %copy.39), channel_id=1, source_target_pairs={{0,1},{1,0},{2,3},{3,2},{4,5},{5,4},{6,7},{7,6},{8,9},{9,8},{10,11... | collective-permute-start | bytes 2654216 | tf_op jit(solution)/shard_map/ppermute | solution.py:156
  186.5 139.0 %collective-permute-start.28 = (bf16[576,768]{1,0:T(8,128)(2,1)}, bf16[576,768]{1,0:T(8,128)(2,1)}, u32[]{:S(2)}, u32[]{:S(2)}) collective-permute-start(bf16[576,768]{1,0:T(8,128)(2,1)} %constant_dynamic-slice_fusion.10), channel_id=1, source_target_pairs={{0,1},{1,0},{2,3},{3,2},{4,5},{5,4},{6,7},{7,6},{8,9},{9,8},{10,11... | collective-permute-start | bytes 2654216 | tf_op jit(solution)/shard_map/ppermute | solution.py:156
  190.0 137.2 %collective-permute-start.19 = (bf16[576,768]{1,0:T(8,128)(2,1)}, bf16[576,768]{1,0:T(8,128)(2,1)}, u32[]{:S(2)}, u32[]{:S(2)}) collective-permute-start(bf16[576,768]{1,0:T(8,128)(2,1)} %constant_dynamic-slice_fusion.15), channel_id=1, source_target_pairs={{0,1},{1,0},{2,3},{3,2},{4,5},{5,4},{6,7},{7,6},{8,9},{9,8},{10,11... | collective-permute-start | bytes 2654216 | tf_op jit(solution)/shard_map/ppermute | solution.py:156
  253.6 14.9 %collective-permute-start.9 = (bf16[384,1024]{1,0:T(8,128)(2,1)}, bf16[384,1024]{1,0:T(8,128)(2,1)}, u32[]{:S(2)}, u32[]{:S(2)}) collective-permute-start(bf16[384,1024]{1,0:T(8,128)(2,1)} %fusion.16), channel_id=1, source_target_pairs={{0,1},{1,0},{2,3},{3,2},{4,5},{5,4},{6,7},{7,6},{8,9},{9,8},{10,11... | collective-permute-start | bytes 2359304 | tf_op jit(solution)/shard_map/ppermute | solution.py:156
  255.5 134.5 %all-to-all-start.1 = ((bf16[16,64,576]{2,1,0:T(8,128)(2,1)}), bf16[16,64,576]{2,1,0:T(8,128)(2,1)}, u32[]{:S(2)}, u32[]{:S(2)}) async-start(bf16[16,64,576]{2,1,0:T(8,128)(2,1)} %bitcast.72), calls=%async_computation.1 | async-start | bytes 2621440 | tf_op jit(solution)/shard_map/all_to_all | solution.py:250
  277.1 87.8 %collective-permute-start.10 = (bf16[576,768]{1,0:T(8,128)(2,1)}, bf16[576,768]{1,0:T(8,128)(2,1)}, u32[]{:S(2)}, u32[]{:S(2)}) collective-permute-start(bf16[576,768]{1,0:T(8,128)(2,1)} %fusion.10), channel_id=1, source_target_pairs={{0,1},{1,0},{2,3},{3,2},{4,5},{5,4},{6,7},{7,6},{8,9},{9,8},{10,11... | collective-permute-start | bytes 2654216 | tf_op jit(solution)/shard_map/ppermute | solution.py:156
  323.3 11.2 %collective-permute-start.38 = (bf16[1,384,576]{1,2,0:T(8,128)(2,1)S(1)}, bf16[1,384,576]{1,2,0:T(8,128)(2,1)S(1)}, u32[]{:S(2)}, u32[]{:S(2)}) collective-permute-start(bf16[1,384,576]{1,2,0:T(8,128)(2,1)S(1)} %constant_dynamic-slice_fusion.3), channel_id=1, source_target_pairs={{0,16},{16,0},{1,17},{17,1},{2,18},{18,2},{3,19},{19,3},{4,20},{20... | collective-permute-start | bytes 1327112 | tf_op jit(solution)/shard_map/ppermute | solution.py:156
  326.9 17.1 %collective-permute-start.29 = (bf16[288,768]{1,0:T(8,128)(2,1)S(1)}, bf16[288,768]{1,0:T(8,128)(2,1)S(1)}, u32[]{:S(2)}, u32[]{:S(2)}) collective-permute-start(bf16[288,768]{1,0:T(8,128)(2,1)S(1)} %constant_dynamic-slice_fusion.9), channel_id=1, source_target_pairs={{0,16},{16,0},{1,17},{17,1},{2,18},{18,2},{3,19},{19,3},{4,20},{20... | collective-permute-start | bytes 1327112 | tf_op jit(solution)/shard_map/ppermute | solution.py:156
  328.6 24.8 %collective-permute-start.20 = (bf16[288,768]{1,0:T(8,128)(2,1)S(1)}, bf16[288,768]{1,0:T(8,128)(2,1)S(1)}, u32[]{:S(2)}, u32[]{:S(2)}) collective-permute-start(bf16[288,768]{1,0:T(8,128)(2,1)S(1)} %constant_dynamic-slice_fusion.14), channel_id=1, source_target_pairs={{0,16},{16,0},{1,17},{17,1},{2,18},{18,2},{3,19},{19,3},{4,20},{20... | collective-permute-start | bytes 1327112 | tf_op jit(solution)/shard_map/ppermute | solution.py:156
  334.8 20.1 %collective-permute-start.39 = (bf16[1,192,576]{1,2,0:T(8,128)(2,1)S(1)}, bf16[1,192,576]{1,2,0:T(8,128)(2,1)S(1)}, u32[]{:S(2)}, u32[]{:S(2)}) collective-permute-start(bf16[1,192,576]{1,2,0:T(8,128)(2,1)S(1)} %constant_dynamic-slice_fusion.2), channel_id=1, source_target_pairs={{0,2},{1,3},{2,0},{3,1},{4,6},{5,7},{6,4},{7,5},{8,10},{9,11},{10,... | collective-permute-start | bytes 663560 | tf_op jit(solution)/shard_map/ppermute | solution.py:156
  344.1 11.1 %collective-permute-start.30 = (bf16[288,384]{1,0:T(8,128)(2,1)S(1)}, bf16[288,384]{1,0:T(8,128)(2,1)S(1)}, u32[]{:S(2)}, u32[]{:S(2)}) collective-permute-start(bf16[288,384]{1,0:T(8,128)(2,1)S(1)} %constant_dynamic-slice_fusion.8), channel_id=1, source_target_pairs={{0,2},{1,3},{2,0},{3,1},{4,6},{5,7},{6,4},{7,5},{8,10},{9,11},{10,... | collective-permute-start | bytes 663560 | tf_op jit(solution)/shard_map/ppermute | solution.py:156
  366.9 15.7 %collective-permute-start.11 = (bf16[288,768]{1,0:T(8,128)(2,1)S(1)}, bf16[288,768]{1,0:T(8,128)(2,1)S(1)}, u32[]{:S(2)}, u32[]{:S(2)}) collective-permute-start(bf16[288,768]{1,0:T(8,128)(2,1)S(1)} %constant_dynamic-slice_fusion.19), channel_id=1, source_target_pairs={{0,16},{16,0},{1,17},{17,1},{2,18},{18,2},{3,19},{19,3},{4,20},{20... | collective-permute-start | bytes 1327112 | tf_op jit(solution)/shard_map/ppermute | solution.py:156
  382.4 22.2 %collective-permute-start.25 = (bf16[144,384]{1,0:T(8,128)(2,1)S(1)}, bf16[144,384]{1,0:T(8,128)(2,1)S(1)}, u32[]{:S(2)}, u32[]{:S(2)}) collective-permute-start(bf16[144,384]{1,0:T(8,128)(2,1)S(1)} %maximum_select_fusion.31), channel_id=1, source_target_pairs={{0,4},{1,5},{2,6},{3,7},{4,0},{5,1},{6,2},{7,3},{8,12},{9,13},{10,... | collective-permute-start | bytes 331784 | tf_op jit(solution)/shard_map/ppermute | solution.py:156
  386.7 49.3 %collective-permute-start.44 = (bf16[1,192,576]{1,2,0:T(8,128)(2,1)S(1)}, bf16[1,192,576]{1,2,0:T(8,128)(2,1)S(1)}, u32[]{:S(2)}, u32[]{:S(2)}) collective-permute-start(bf16[1,192,576]{1,2,0:T(8,128)(2,1)S(1)} %maximum_select_fusion.24), channel_id=1, source_target_pairs={{0,2},{1,3},{2,0},{3,1},{4,6},{5,7},{6,4},{7,5},{8,10},{9,11},{10,... | collective-permute-start | bytes 663560 | tf_op jit(solution)/shard_map/ppermute | solution.py:156
  387.6 52.8 %collective-permute-start.35 = (bf16[288,384]{1,0:T(8,128)(2,1)S(1)}, bf16[288,384]{1,0:T(8,128)(2,1)S(1)}, u32[]{:S(2)}, u32[]{:S(2)}) collective-permute-start(bf16[288,384]{1,0:T(8,128)(2,1)S(1)} %maximum_select_fusion.27), channel_id=1, source_target_pairs={{0,2},{1,3},{2,0},{3,1},{4,6},{5,7},{6,4},{7,5},{8,10},{9,11},{10,... | collective-permute-start | bytes 663560 | tf_op jit(solution)/shard_map/ppermute | solution.py:156
  388.9 13.1 %collective-permute-start.13 = (bf16[144,384]{1,0:T(8,128)(2,1)S(1)}, bf16[144,384]{1,0:T(8,128)(2,1)S(1)}, u32[]{:S(2)}, u32[]{:S(2)}) collective-permute-start(bf16[144,384]{1,0:T(8,128)(2,1)S(1)} %constant_dynamic-slice_fusion.17), channel_id=1, source_target_pairs={{0,4},{1,5},{2,6},{3,7},{4,0},{5,1},{6,2},{7,3},{8,12},{9,13},{10,... | collective-permute-start | bytes 331784 | tf_op jit(solution)/shard_map/ppermute | solution.py:156
  390.1 72.9 %all-to-all-start.3 = ((bf16[16,64,576]{2,1,0:T(8,128)(2,1)}), bf16[16,64,576]{2,1,0:T(8,128)(2,1)S(1)}, u32[]{:S(2)}, u32[]{:S(2)}) async-start(bf16[16,64,576]{2,1,0:T(8,128)(2,1)} %bitcast.25), calls=%async_computation.3 | async-start | bytes 2621440 | tf_op jit(solution)/shard_map/all_to_all | solution.py:250
  402.1 33.8 %collective-permute-start.14 = (bf16[72,384]{1,0:T(8,128)(2,1)S(1)}, bf16[72,384]{1,0:T(8,128)(2,1)S(1)}, u32[]{:S(2)}, u32[]{:S(2)}) collective-permute-start(bf16[72,384]{1,0:T(8,128)(2,1)S(1)} %constant_dynamic-slice_fusion.16), channel_id=1, source_target_pairs={{0,8},{1,9},{2,10},{3,11},{4,12},{5,13},{6,14},{7,15},{8,0},{9,1},... | collective-permute-start | bytes 165896 | tf_op jit(solution)/shard_map/ppermute | solution.py:156
  404.6 41.7 %collective-permute-start.26 = (bf16[288,384]{1,0:T(8,128)(2,1)S(1)}, bf16[288,384]{1,0:T(8,128)(2,1)S(1)}, u32[]{:S(2)}, u32[]{:S(2)}) collective-permute-start(bf16[288,384]{1,0:T(8,128)(2,1)S(1)} %maximum_select_fusion.26), channel_id=1, source_target_pairs={{0,2},{1,3},{2,0},{3,1},{4,6},{5,7},{6,4},{7,5},{8,10},{9,11},{10,... | collective-permute-start | bytes 663560 | tf_op jit(solution)/shard_map/ppermute | solution.py:156
  437.2 20.7 %collective-permute-start.45 = (bf16[1,384,576]{1,2,0:T(8,128)(2,1)}, bf16[1,384,576]{1,2,0:T(8,128)(2,1)}, u32[]{:S(2)}, u32[]{:S(2)}) collective-permute-start(bf16[1,384,576]{1,2,0:T(8,128)(2,1)} %maximum_select_fusion.16), channel_id=1, source_target_pairs={{0,1},{1,0},{2,3},{3,2},{4,5},{5,4},{6,7},{7,6},{8,9},{9,8},{10,11... | collective-permute-start | bytes 1327112 | tf_op jit(solution)/shard_map/ppermute | solution.py:156
  440.6 14.6 %collective-permute-start.36 = (bf16[288,768]{1,0:T(8,128)(2,1)S(1)}, bf16[288,768]{1,0:T(8,128)(2,1)}, u32[]{:S(2)}, u32[]{:S(2)}) collective-permute-start(bf16[288,768]{1,0:T(8,128)(2,1)S(1)} %maximum_select_fusion.14), channel_id=1, source_target_pairs={{0,1},{1,0},{2,3},{3,2},{4,5},{5,4},{6,7},{7,6},{8,9},{9,8},{10,11... | collective-permute-start | bytes 1327112 | tf_op jit(solution)/shard_map/ppermute | solution.py:156
  446.5 13.9 %collective-permute-start.27 = (bf16[288,768]{1,0:T(8,128)(2,1)S(1)}, bf16[288,768]{1,0:T(8,128)(2,1)}, u32[]{:S(2)}, u32[]{:S(2)}) collective-permute-start(bf16[288,768]{1,0:T(8,128)(2,1)S(1)} %maximum_select_fusion.13), channel_id=1, source_target_pairs={{0,1},{1,0},{2,3},{3,2},{4,5},{5,4},{6,7},{7,6},{8,9},{9,8},{10,11... | collective-permute-start | bytes 1327112 | tf_op jit(solution)/shard_map/ppermute | solution.py:156
  453.4 11.0 %collective-permute-start.18 = (bf16[288,768]{1,0:T(8,128)(2,1)S(1)}, bf16[288,768]{1,0:T(8,128)(2,1)}, u32[]{:S(2)}, u32[]{:S(2)}) collective-permute-start(bf16[288,768]{1,0:T(8,128)(2,1)S(1)} %maximum_select_fusion.12), channel_id=1, source_target_pairs={{0,1},{1,0},{2,3},{3,2},{4,5},{5,4},{6,7},{7,6},{8,9},{9,8},{10,11... | collective-permute-start | bytes 1327112 | tf_op jit(solution)/shard_map/ppermute | solution.py:156
  (61 other events, 482.2 us)

commit v2 on v1

v2 whole, which is shorter than its diff:
```python
import functools

import jax
import jax.numpy as jnp
from jax import lax
from jax.experimental import pallas as pl
from jax.experimental.pallas import tpu as pltpu
from jax.sharding import PartitionSpec as P

HEADS = 9
KV_HEADS = 3
HEAD_DIM = 64
EPSILON = 1e-05
THETA = 100000.0
NEGATIVE = -1e30
LOG2E = 1.4426950408889634
LN2 = 0.6931471805599453
F32=jnp.float32; BF=jnp.bfloat16
NT=(((1,),(1,)),((),()))
NN=(((1,),(0,)),((),()))
def mm(a,b,dims=NN):
    return lax.dot_general(a,b,dims,preferred_element_type=F32)

def heads_of(ref, kv, group):
    return jnp.concatenate([ref[(kv*group+h)*64:(kv*group+h+1)*64,:] for h in range(group)],axis=1)

def fwd_kernel(bias_ref, q_ref, kv_ref, o_ref, lse_ref, k_scr, m_scr, acc_scr, *, kvs, group, slots, rows, qb):
    i=pl.program_id(0)
    kw=kvs*64
    @pl.when(i==0)
    def _():
        for s in range(slots):
            for h in range(kvs):
                k_scr[h,s]=kv_ref[s,h*64:(h+1)*64,:].T
    qs=[heads_of(q_ref,h,group) for h in range(kvs)]
    width=group*qb
    m_scr[...]=jnp.full(m_scr.shape,-1e30,F32)
    acc_scr[...]=jnp.zeros(acc_scr.shape,F32)
    ones=jnp.ones((8,slots*qb),BF)
    def chunk(c, masked):
        off=pl.multiple_of(c*qb,qb)
        for h in range(kvs):
            k=jnp.concatenate([k_scr[h,s,pl.ds(off,qb),:] for s in range(slots)],axis=0)
            v=jnp.concatenate([kv_ref[s,kw+h*64:kw+(h+1)*64,pl.ds(off,qb)] for s in range(slots)],axis=1)
            v=jnp.concatenate([v,ones],axis=0)
            st=mm(k,qs[h])
            if masked:
                b=bias_ref[...].reshape(slots*qb,qb)
                st=st+jnp.concatenate([b]*group,axis=1)
            m_old=m_scr[h:h+1,:]
            m_new=jnp.maximum(m_old,jnp.max(st,axis=0,keepdims=True))
            p=jnp.exp2(st-m_new).astype(BF)
            acc_scr[h]=acc_scr[h]*jnp.exp2(m_old-m_new)+mm(v,p)
            m_scr[h:h+1,:]=m_new
    def body(c,_):
        chunk(c,False); return 0
    lax.fori_loop(0,i,body,0)
    chunk(i,True)
    for h in range(kvs):
        acc=acc_scr[h]
        tot=acc[64:65,:]
        o=acc[:64,:]*(1.0/tot)
        lse=m_scr[h:h+1,:]+jnp.log2(tot)
        for g in range(group):
            r=h*group+g
            o_ref[r*64:(r+1)*64,:]=o[:,g*qb:(g+1)*qb]
            lse_ref[r:r+1,:]=lse[:,g*qb:(g+1)*qb]

def attn_fwd(bias, qT, kvT, kvs=3, group=3, qb=256):
    slots,_,rows=kvT.shape
    n=rows//qb
    heads=kvs*group
    return pl.pallas_call(
        functools.partial(fwd_kernel,kvs=kvs,group=group,slots=slots,rows=rows,qb=qb),
        grid=(n,),
        in_specs=[pl.BlockSpec((slots,qb,qb),lambda i:(0,0,0)),
                  pl.BlockSpec((heads*64,qb),lambda i:(0,i)),
                  pl.BlockSpec((slots,2*kvs*64,rows),lambda i:(0,0,0))],
        out_specs=[pl.BlockSpec((heads*64,qb),lambda i:(0,i)),
                   pl.BlockSpec((16,qb),lambda i:(0,i))],
        out_shape=[jax.ShapeDtypeStruct((heads*64,rows),F32),jax.ShapeDtypeStruct((16,rows),F32)],
        scratch_shapes=[pltpu.VMEM((kvs,slots,rows,64),BF),pltpu.VMEM((8,group*qb),F32),
                        pltpu.VMEM((kvs,72,group*qb),F32)],
        compiler_params=pltpu.CompilerParams(vmem_limit_bytes=56*2**20),
        cost_estimate=pl.CostEstimate(flops=int(25e9),bytes_accessed=int(8e6),transcendentals=int(1e7)),
    )(bias,qT,kvT)

def bwd_kernel(*refs, kvs, group, slots, qb, lo, first, last):
    bias_ref, q_ref, kv_ref, do_ref, lse_ref, rd_ref = refs[:6]
    refs = refs[6:]
    if not first:
        before_ref, refs = refs[0], refs[1:]
    if last:
        dq_ref, dkv_ref, low_ref, kv_scr = refs
    else:
        dq_ref, dkv_ref, kv_scr = refs
    step = pl.program_id(0)
    kw = kvs * 64

    @pl.when(step == 0)
    def _():
        for s in range(slots):
            for h in range(2 * kvs):
                kv_scr[h, s] = kv_ref[s, h * 64 : (h + 1) * 64, :].T
        dkv_ref[...] = jnp.zeros(dkv_ref.shape, F32) if first else before_ref[...]

    dq_ref[...] = jnp.zeros(dq_ref.shape, F32)
    qs = [heads_of(q_ref, h, group) for h in range(kvs)]
    dos = [heads_of(do_ref, h, group) for h in range(kvs)]

    def along(ref, h):
        return jnp.concatenate([ref[h * group + g : h * group + g + 1, :] for g in range(group)], axis=1)

    lses = [along(lse_ref, h) for h in range(kvs)]
    rds = [along(rd_ref, h) for h in range(kvs)]

    def chunk(c, masked):
        off = pl.multiple_of(c * qb, qb)
        for h in range(kvs):
            k = jnp.concatenate([kv_scr[h, s, pl.ds(off, qb), :] for s in range(slots)], axis=0)
            v = jnp.concatenate([kv_scr[kvs + h, s, pl.ds(off, qb), :] for s in range(slots)], axis=0)
            k_t = jnp.concatenate([kv_ref[s, h * 64 : (h + 1) * 64, pl.ds(off, qb)] for s in range(slots)], axis=1)
            st = mm(k, qs[h])
            if masked:
                st = st + jnp.concatenate([bias_ref[...].reshape(slots * qb, qb)] * group, axis=1)
            p = jnp.exp2(st - lses[h])
            dp = mm(v, dos[h])
            ds = (p * (dp - rds[h])).astype(BF)
            dk = mm(qs[h], ds, NT)
            dv = mm(dos[h], p.astype(BF), NT)
            dq = mm(k_t, ds)
            for s in range(slots):
                dkv_ref[s, h * 64 : (h + 1) * 64, pl.ds(off, qb)] += dk[:, s * qb : (s + 1) * qb]
                dkv_ref[s, kw + h * 64 : kw + (h + 1) * 64, pl.ds(off, qb)] += dv[:, s * qb : (s + 1) * qb]
            for g in range(group):
                r = h * group + g
                dq_ref[r * 64 : (r + 1) * 64, :] += dq[:, g * qb : (g + 1) * qb]

    def body(c, carry):
        chunk(c, False)
        return carry

    lax.fori_loop(0, step + lo, body, 0)
    chunk(step + lo, True)
    if last:

        @pl.when(step == pl.num_programs(0) - 1)
        def _():
            low_ref[...] = dkv_ref[...].astype(BF)


def attn_bwd(bias, q_t, kv_t, do_t, lse, rd, lo, hi, before=None, last=False, kvs=3, group=3, qb=256):
    slots, _, rows = kv_t.shape
    width = kvs * group * 64
    whole = pl.BlockSpec((slots, 2 * kvs * 64, rows), lambda i: (0, 0, 0))
    tall = pl.BlockSpec((width, qb), lambda i: (0, i + lo))
    stat = pl.BlockSpec((16, qb), lambda i: (0, i + lo))
    out_specs = [pl.BlockSpec((width, qb), lambda i: (0, i)), whole]
    out_shape = [
        jax.ShapeDtypeStruct((width, (hi - lo) * qb), F32),
        jax.ShapeDtypeStruct((slots, 2 * kvs * 64, rows), F32),
    ]
    if last:
        out_specs.append(whole)
        out_shape.append(jax.ShapeDtypeStruct((slots, 2 * kvs * 64, rows), BF))
    args = (bias, q_t, kv_t, do_t, lse, rd) + (() if before is None else (before,))
    units = sum(range(lo + 1, hi + 1))
    return pl.pallas_call(
        functools.partial(
            bwd_kernel, kvs=kvs, group=group, slots=slots, qb=qb, lo=lo, first=before is None, last=last
        ),
        grid=(hi - lo,),
        in_specs=[pl.BlockSpec((slots, qb, qb), lambda i: (0, 0, 0)), tall, whole, tall, stat, stat]
        + ([] if before is None else [whole]),
        out_specs=out_specs,
        out_shape=out_shape,
        scratch_shapes=[pltpu.VMEM((2 * kvs, slots, rows, 64), BF)],
        compiler_params=pltpu.CompilerParams(vmem_limit_bytes=60 * 2**20),
        cost_estimate=pl.CostEstimate(flops=int(4e9) * units, bytes_accessed=int(16e6), transcendentals=0),
    )(*args)


TN = (((0,), (0,)), ((), ()))
TT = (((0,), (1,)), ((), ()))
BLOCK = 256
PIECES = 8
LIMIT = 60 * 2**20


def rotated(values, cosine, sine):
    a, b = values[:32], values[32:]
    return jnp.concatenate([a * cosine - b * sine, b * cosine + a * sine], axis=0)


def flat_rows(ref):
    count, sub, width = ref.shape
    return ref[...].reshape(count * sub, width)


def rms(values):
    return lax.rsqrt(jnp.mean(values * values, axis=-1, keepdims=True) + EPSILON)


def qkv_kernel(x_ref, w_ref, gain_ref, cos_ref, sin_ref, q_ref, kv_ref, wt_scr):
    @pl.when(pl.program_id(0) == 0)
    def _():
        wt_scr[...] = w_ref[:, : wt_scr.shape[0]].T

    source = flat_rows(x_ref).astype(F32)
    hidden = (source * rms(source) * gain_ref[0:1, :]).astype(BF)
    out = mm(wt_scr[...], hidden, NT)
    cosine, sine = cos_ref[...], sin_ref[...]
    for h in range(HEADS):
        part = rotated(out[h * 64 : (h + 1) * 64], cosine, sine)
        q_ref[h * 64 : (h + 1) * 64, :] = (part * (HEAD_DIM**-0.5 * LOG2E)).astype(BF)
    top = HEADS * 64
    for h in range(KV_HEADS):
        part = rotated(out[top + h * 64 : top + (h + 1) * 64], cosine, sine)
        kv_ref[h * 64 : (h + 1) * 64, :] = part.astype(BF)
    kv_ref[KV_HEADS * 64 :, :] = out[top + KV_HEADS * 64 :].astype(BF)


def project_qkv(x, first, gains, cosine, sine):
    count, sub, width = x.shape
    rows = count * sub
    per = BLOCK // sub
    kv2 = 2 * KV_HEADS * HEAD_DIM
    return pl.pallas_call(
        qkv_kernel,
        grid=(rows // BLOCK,),
        in_specs=[
            pl.BlockSpec((per, sub, width), lambda i: (i, 0, 0)),
            pl.BlockSpec(first.shape, lambda i: (0, 0)),
            pl.BlockSpec(gains.shape, lambda i: (0, 0)),
            pl.BlockSpec((32, BLOCK), lambda i: (0, i)),
            pl.BlockSpec((32, BLOCK), lambda i: (0, i)),
        ],
        out_specs=[pl.BlockSpec((width, BLOCK), lambda i: (0, i)), pl.BlockSpec((kv2, BLOCK), lambda i: (0, i))],
        out_shape=[jax.ShapeDtypeStruct((width, rows), BF), jax.ShapeDtypeStruct((kv2, rows), BF)],
        scratch_shapes=[pltpu.VMEM((width + kv2, width), BF)],
        compiler_params=pltpu.CompilerParams(vmem_limit_bytes=LIMIT),
        cost_estimate=pl.CostEstimate(flops=int(6e9), bytes_accessed=int(5e6), transcendentals=0),
    )(x, first, gains, cosine, sine)


def ffn_kernel(
    place_ref, o_ref, x_ref, cot_ref, first_ref, gate_ref, up_ref, down_ref, gain_ref,
    mixed_ref, dres_ref, datt_ref, rd_ref, keep_gu, send_gu, keep_do, send_do, gg_ref,
    acc_gu, acc_down, acc_out, out_scr,
):
    step = pl.program_id(0)
    width = x_ref.shape[2]

    @pl.when(step == 0)
    def _():
        acc_gu[...] = jnp.zeros(acc_gu.shape, F32)
        acc_down[...] = jnp.zeros(acc_down.shape, F32)
        acc_out[...] = jnp.zeros(acc_out.shape, F32)
        gg_ref[...] = jnp.zeros(gg_ref.shape, F32)

    cols = first_ref.shape[1]
    out_w = first_ref[:, cols - width :]
    attended = o_ref[...]
    mixed = attended.astype(BF)
    residual = flat_rows(x_ref).astype(F32) + mm(mixed, out_w, TN)
    scale = rms(residual)
    normed = residual * scale
    gain = gain_ref[1:2, :]
    hidden = (normed * gain).astype(BF)
    gate = mm(hidden, gate_ref[...])
    up = mm(hidden, up_ref[...])
    sig = 0.5 * jnp.tanh(0.5 * gate) + 0.5
    silu = gate * sig
    activated = (silu * up).astype(BF)
    mixed_out = (residual + mm(activated, down_ref[...])).astype(BF)
    mixed_ref[...] = mixed_out.reshape(mixed_ref.shape)
    cot = flat_rows(cot_ref)
    d_act = mm(cot, down_ref[...], NT)
    acc_down[...] += mm(activated, cot, TN)
    d_gate = (d_act * up * sig * (1.0 + gate * (1.0 - sig))).astype(BF)
    d_up = (d_act * silu).astype(BF)
    acc_gu[0] += mm(hidden, d_gate, TN)
    acc_gu[1] += mm(hidden, d_up, TN)
    d_hidden = mm(d_gate, gate_ref[...], NT) + mm(d_up, up_ref[...], NT)
    dn = d_hidden * normed
    gg_ref[...] += jnp.sum(dn.reshape(-1, 8, width), axis=0)
    inner = jnp.mean(dn * gain, axis=-1, keepdims=True)
    d_res = cot.astype(F32) + scale * (d_hidden * gain - normed * inner)
    dres_ref[...] = d_res
    d_low = d_res.astype(BF)
    acc_out[: acc_out.shape[0] - 16] += mm(mixed, d_low)
    d_att = mm(out_w, d_low, NT).astype(BF)
    datt_ref[...] = d_att
    prod = d_att.astype(F32) * attended
    for h in range(HEADS):
        rd_ref[h : h + 1, :] = jnp.sum(prod[h * 64 : (h + 1) * 64], axis=0, keepdims=True)
    rd_ref[HEADS:, :] = jnp.zeros((16 - HEADS, rd_ref.shape[1]), F32)

    @pl.when(step == pl.num_programs(0) - 1)
    def _():
        core = place_ref[0]
        half = width // 2
        ff = acc_gu.shape[2]
        for y in range(2):
            for p in range(PIECES):
                rs = slice(y * half + (p // 4) * (half // 2), y * half + (p // 4 + 1) * (half // 2))
                cs = slice((p % 4) * (ff // 4), (p % 4 + 1) * (ff // 4))
                keep_gu[y, p] = acc_gu[core, rs, cs].astype(BF)
                send_gu[y, p] = acc_gu[1 - core, rs, cs].astype(BF)
        down_rows, out_rows = ff // 32, width // 32
        for m in range(32):
            out_scr[m] = acc_out[m * out_rows : m * out_rows + 24, :].astype(F32)
        for y in range(2):
            for p in range(PIECES):
                for ref, c in ((keep_do, core), (send_do, 1 - core)):
                    start = pl.multiple_of(y * (ff // 2) + (PIECES * c + p) * down_rows, 16)
                    ref[y, p, :down_rows] = acc_down[pl.ds(start, down_rows), :].astype(BF)
                    ref[y, p, down_rows:] = out_scr[y * 16 + PIECES * c + p].astype(BF)


def feed_forward(place, attended, x, cot, first, gate_w, up_w, down_w, gains):
    count, sub, width = x.shape
    rows, ff = count * sub, gate_w.shape[1]
    per = BLOCK // sub
    gu = (2, PIECES, width // 4, ff // 4)
    do = (2, PIECES, ff // 32 + 24, width)

    def whole(shape):
        return pl.BlockSpec(shape, lambda i: (0,) * len(shape))

    seq = pl.BlockSpec((per, sub, width), lambda i: (i, 0, 0))
    tall = pl.BlockSpec((width, BLOCK), lambda i: (0, i))
    return pl.pallas_call(
        ffn_kernel,
        grid=(rows // BLOCK,),
        in_specs=[
            pl.BlockSpec(memory_space=pltpu.SMEM), tall, seq, seq,
            whole(first.shape), whole(gate_w.shape), whole(up_w.shape), whole(down_w.shape), whole(gains.shape),
        ],
        out_specs=[
            seq, pl.BlockSpec((BLOCK, width), lambda i: (i, 0)), tall, pl.BlockSpec((16, BLOCK), lambda i: (0, i)),
            whole(gu), whole(gu), whole(do), whole(do), whole((8, width)),
        ],
        out_shape=[
            jax.ShapeDtypeStruct(x.shape, BF),
            jax.ShapeDtypeStruct((rows, width), F32),
            jax.ShapeDtypeStruct((width, rows), BF),
            jax.ShapeDtypeStruct((16, rows), F32),
            jax.ShapeDtypeStruct(gu, BF), jax.ShapeDtypeStruct(gu, BF),
            jax.ShapeDtypeStruct(do, BF), jax.ShapeDtypeStruct(do, BF),
            jax.ShapeDtypeStruct((8, width), F32),
        ],
        scratch_shapes=[
            pltpu.VMEM((2, width, ff), F32), pltpu.VMEM((ff, width), F32), pltpu.VMEM((width + 16, width), F32),
            pltpu.VMEM((32, 24, width), F32),
        ],
        compiler_params=pltpu.CompilerParams(vmem_limit_bytes=LIMIT),
        cost_estimate=pl.CostEstimate(flops=int(32e9), bytes_accessed=int(20e6), transcendentals=0),
    )(place, attended, x, cot, first, gate_w, up_w, down_w, gains)


def back_kernel(*refs, spans):
    place_ref, refs = refs[0], refs[1:]
    dq_refs, refs = refs[: len(spans)], refs[len(spans) :]
    own_ref, got_ref, x_ref, dres_ref, first_ref, gain_ref, cos_ref, sin_ref, gg_ref, dx_ref = refs[:10]
    keep_ref, send_ref, acc, dt_scr, ga_scr, w_scr = refs[10:]
    step = pl.program_id(0)
    width = x_ref.shape[2]
    kv = KV_HEADS * 64
    total = width + 2 * kv

    @pl.when(step == 0)
    def _():
        acc[...] = jnp.zeros(acc.shape, F32)
        ga_scr[...] = jnp.zeros(ga_scr.shape, F32)
        w_scr[...] = first_ref[:, :total].T

    cosine, sine = cos_ref[...], -sin_ref[...]
    for (lo, hi), dq_ref in zip(spans, dq_refs):

        @pl.when((step >= lo) & (step < hi))
        def _():
            for h in range(HEADS):
                part = dq_ref[h * 64 : (h + 1) * 64, :] * (HEAD_DIM**-0.5)
                dt_scr[h * 64 : (h + 1) * 64, :] = rotated(part, cosine, sine).astype(BF)

    d_kv = own_ref[0] + got_ref[...].astype(F32)
    for h in range(KV_HEADS):
        part = d_kv[h * 64 : (h + 1) * 64] * LN2
        dt_scr[width + h * 64 : width + (h + 1) * 64, :] = rotated(part, cosine, sine).astype(BF)
    dt_scr[width + kv :, :] = d_kv[kv:].astype(BF)
    d_t = dt_scr[...]
    source = flat_rows(x_ref).astype(F32)
    scale = rms(source)
    normed = source * scale
    gain = gain_ref[0:1, :]
    hidden = (normed * gain).astype(BF)
    acc[:total] += mm(d_t, hidden)
    d_hidden = mm(d_t, w_scr[...], TN)
    dn = d_hidden * normed
    ga_scr[...] += jnp.sum(dn.reshape(-1, 8, width), axis=0)
    inner = jnp.mean(dn * gain, axis=-1, keepdims=True)
    grad = dres_ref[...] + scale * (d_hidden * gain - normed * inner)
    dx_ref[...] = grad.astype(BF).reshape(dx_ref.shape)

    @pl.when(step == pl.num_programs(0) - 1)
    def _():
        core = place_ref[0]
        acc[total : total + 1, :] = jnp.sum(ga_scr[...], axis=0, keepdims=True)
        acc[total + 1 : total + 2, :] = jnp.sum(gg_ref[...], axis=0, keepdims=True)
        half, deep = width // 2, width // 4
        for ct in range(4):
            for ref, c in ((keep_ref, core), (send_ref, 1 - core)):
                start = pl.multiple_of(c * 512 + ct * 128, 128)
                block = acc[pl.ds(start, 128), :].T.astype(BF)
                for y in range(2):
                    for rh in range(2):
                        low = y * half + rh * deep
                        ref[y, rh * 4 + ct] = block[low : low + deep]


def back_qkv(place, spans, d_query, d_kv, got, x, d_res, first, gains, cosine, sine, gg):
    count, sub, width = x.shape
    rows = count * sub
    per = BLOCK // sub
    kv2 = 2 * KV_HEADS * HEAD_DIM
    piece = (2, PIECES, width // 4, 128)

    def whole(shape):
        return pl.BlockSpec(shape, lambda i: (0,) * len(shape))

    seq = pl.BlockSpec((per, sub, width), lambda i: (i, 0, 0))
    return pl.pallas_call(
        functools.partial(back_kernel, spans=spans),
        grid=(rows // BLOCK,),
        in_specs=[
            pl.BlockSpec(memory_space=pltpu.SMEM),
            *(
                pl.BlockSpec((width, BLOCK), lambda i, lo=lo, hi=hi: (0, jnp.clip(i - lo, 0, hi - lo - 1)))
                for lo, hi in spans
            ),
            pl.BlockSpec((1, kv2, BLOCK), lambda i: (0, 0, i)),
            pl.BlockSpec((kv2, BLOCK), lambda i: (0, i)),
            seq, pl.BlockSpec((BLOCK, width), lambda i: (i, 0)),
            whole(first.shape), whole(gains.shape),
            pl.BlockSpec((32, BLOCK), lambda i: (0, i)), pl.BlockSpec((32, BLOCK), lambda i: (0, i)),
            whole(gg.shape),
        ],
        out_specs=[seq, whole(piece), whole(piece)],
        out_shape=[jax.ShapeDtypeStruct(x.shape, BF), jax.ShapeDtypeStruct(piece, BF), jax.ShapeDtypeStruct(piece, BF)],
        scratch_shapes=[
            pltpu.VMEM((1024, width), F32), pltpu.VMEM((width + kv2, BLOCK), BF), pltpu.VMEM((8, width), F32),
            pltpu.VMEM((width + kv2, width), BF),
        ],
        compiler_params=pltpu.CompilerParams(vmem_limit_bytes=LIMIT),
        cost_estimate=pl.CostEstimate(flops=int(10e9), bytes_accessed=int(10e6), transcendentals=0),
    )(place, *d_query, d_kv, got, x, d_res, first, gains, cosine, sine, gg)


def swap(x, axis, bit):
    n = lax.axis_size(axis)
    return lax.ppermute(x, axis, [(i, i ^ (1 << bit)) for i in range(n)])


def bit_of(axis, bit):
    return (lax.axis_index(axis) >> bit) & 1


def pin(*arrays):
    return lax.optimization_barrier(arrays)


def pick(x, at):
    return lax.dynamic_index_in_dim(x, at, 0, keepdims=False)


def in_order(flag, mine, other, axis):
    return jnp.where(
        flag == 0,
        jnp.concatenate([mine, other], axis=axis),
        jnp.concatenate([other, mine], axis=axis),
    )


def plus(a, b):
    return (a.astype(F32) + b.astype(F32)).astype(BF)


def two_level():
    return lax.axis_size("fsdp") == 2 and lax.axis_size("ctx") == 16


def z_groups():
    return [[4 * z + r for z in range(4)] for r in range(4)]


def z_sum(x):
    x = lax.all_to_all(x, "ctx", 0, 0, tiled=True, axis_index_groups=z_groups())
    return jnp.sum(x.astype(F32), axis=0).astype(BF)


def z_join(piece):
    whole = jnp.broadcast_to(piece[None], (4,) + piece.shape)
    return lax.all_to_all(whole, "ctx", 0, 0, tiled=True, axis_index_groups=z_groups())


def join(x, bit):
    return swap(x, "ctx", bit)


def natural_gu(pieces):
    _, a, b = pieces.shape
    return pieces.reshape(2, 4, a, b).transpose(0, 2, 1, 3).reshape(2 * a, 4 * b).astype(F32)


def other_sum(x):
    x = lax.psum_scatter(x.astype(BF), "fsdp", scatter_dimension=0, tiled=True)
    return lax.psum(x, "ctx").astype(F32)


def local(tokens, gain_attn, w_query, w_key, w_value, w_out, gain_ffn, w_gate, w_up, w_down, cotangent):
    seqs, length, width = tokens.shape
    count = lax.axis_size("ctx")
    team = count // seqs
    sub = length // team
    rows = count * sub
    ff = w_gate.shape[1]
    kv_width = KV_HEADS * HEAD_DIM
    qkv_cols = width + 2 * kv_width
    place = lax.axis_index("ctx") % team
    own = gain_attn.shape[0]
    fast = two_level()

    def move(x):
        return lax.all_to_all(x.reshape(count, sub, width), "ctx", 0, 0, tiled=True)

    x = move(tokens)
    gain_rows = jnp.zeros((8, ff), BF).at[0, :own].set(gain_attn).at[1, :own].set(gain_ffn)
    first = jnp.concatenate([jnp.concatenate([w_query, w_key, w_value, w_out], axis=1), gain_rows], axis=0)
    if fast:
        core, rank = bit_of("ctx", 0), bit_of("fsdp", 0)

        def halved(shard, axis):
            half = shard.shape[axis] // 2
            return lax.dynamic_slice_in_dim(shard, core * half, half, axis)

        def other_shard(got, axis):
            return in_order(core, got, swap(got, "ctx", 0), axis)

        got = swap(halved(first, 1), "fsdp", 0)
        other = other_shard(got, 1)
        gains = in_order(rank, first[own : own + 2, :own], other[own : own + 2, :own], 1).astype(F32)
        first = in_order(rank, first[:own], other[:own], 0)
        gate_half, up_half, down_half, got = pin(halved(w_gate, 1), halved(w_up, 1), halved(w_down, 0), got)
        gate_w = in_order(rank, w_gate, other_shard(swap(gate_half, "fsdp", 0), 1), 0)
        up_w = in_order(rank, w_up, other_shard(swap(up_half, "fsdp", 0), 1), 0)
        down_w = in_order(rank, w_down, other_shard(swap(down_half, "fsdp", 0), 0), 0)
    else:
        first = lax.all_gather(first, "fsdp", axis=0)
        gains = first[:, own : own + 2, :own].transpose(1, 0, 2).reshape(2, width).astype(F32)
        first = first[:, :own].reshape(width, first.shape[2])
        gate_w, up_w, down_w = (lax.all_gather(w, "fsdp", axis=0, tiled=True) for w in (w_gate, w_up, w_down))
    gains = jnp.pad(gains, ((0, 6), (0, 0)))

    row = jnp.arange(rows, dtype=jnp.int32)
    position = (row // sub) * length + place * sub + row % sub
    frequency = THETA ** (-jnp.arange(HEAD_DIM // 2, dtype=F32) * 2.0 / HEAD_DIM)
    angles = frequency[:, None] * position.astype(F32)[None, :]
    cosine, sine = jnp.cos(angles), jnp.sin(angles)
    groups = [[t * team + p for p in range(team)] for t in range(seqs)]
    slots = jnp.stack([place, 1 - place]) if team == 2 else jnp.arange(team)
    block_row = jnp.arange(BLOCK, dtype=jnp.int32)
    base = (block_row // sub) * length + block_row % sub
    key_pos = base[None, :] + slots[:, None] * sub
    query_pos = base + place * sub
    bias = jnp.where(key_pos[:, :, None] <= query_pos[None, None, :], 0.0, NEGATIVE).astype(F32)
    flags = jnp.stack([core, rank]) if fast else jnp.zeros((2,), jnp.int32)

    x, cot_send = pin(x, cotangent)
    cot = move(cot_send)
    query, kv_own = project_qkv(x, first, gains, cosine, sine)
    if team == 2:
        kv_all = jnp.stack([kv_own, swap(kv_own, "ctx", 0)])
    else:
        kv_all = lax.all_gather(kv_own, "ctx", axis=0, axis_index_groups=groups)
    attended, log_total = attn_fwd(bias, query, kv_all)
    attended, cot = pin(attended, cot)
    mixed, d_res, d_att, row_dot, keep_gu, send_gu, keep_do, send_do, gain_sum = feed_forward(
        flags, attended, x, cot, first, gate_w, up_w, down_w, gains
    )
    mixed_out = move(mixed)

    n = rows // BLOCK
    spans = ((0, n // 2), (n - 1, n), (n // 2, n - 1))
    part = functools.partial(attn_bwd, bias, query, kv_all, d_att, log_total, row_dot)
    if fast:
        got_gu, got_do = swap(send_gu, "ctx", 0), swap(send_do, "ctx", 0)
        dq_a, before = part(*spans[0])
        got_gu, got_do, before = pin(got_gu, got_do, before)
        x_bit = bit_of("ctx", 1)
        gu, do = plus(keep_gu, got_gu), plus(keep_do, got_do)
        gu = gu.reshape((2, 2, 4) + gu.shape[2:]).swapaxes(0, 1)
        keep_gu, send_gu = pick(gu, x_bit), pick(gu, 1 - x_bit)
        keep_do, send_do = pick(do, rank), pick(do, 1 - rank)
        send_gu, send_do, before = pin(send_gu, send_do, before)
        got_gu, got_do = swap(send_gu, "ctx", 1), swap(send_do, "fsdp", 0)
        dq_b, before = part(*spans[1], before=before)
        got_gu, got_do, mixed_out, before = pin(got_gu, got_do, mixed_out, before)
        gu, do = plus(keep_gu, got_gu), plus(keep_do, got_do)
        do = do.reshape((2, 4) + do.shape[1:])
        keep_gu, send_gu = pick(gu, rank), pick(gu, 1 - rank)
        keep_do, send_do = pick(do, x_bit), pick(do, 1 - x_bit)
        send_gu, send_do, before = pin(send_gu, send_do, before)
        got_gu, got_do = swap(send_gu, "fsdp", 0), swap(send_do, "ctx", 1)
        dq_c, d_kv, d_kv_low = part(*spans[2], before=before, last=True)
        got_gu, got_do, d_kv_low, dq_c = pin(got_gu, got_do, d_kv_low, dq_c)
        gu, do = plus(keep_gu, got_gu), plus(keep_do, got_do)
    else:
        dq_a, before = part(*spans[0])
        dq_b, before = part(*spans[1], before=before)
        dq_c, d_kv, d_kv_low = part(*spans[2], before=before, last=True)
    if team == 2:
        own_kv, got_kv = d_kv[:1], swap(d_kv_low[1], "ctx", 0)
    else:
        own_kv = lax.psum_scatter(d_kv_low, "ctx", scatter_dimension=0, axis_index_groups=groups)
        own_kv, got_kv = own_kv.astype(F32)[None], jnp.zeros((2 * kv_width, rows), BF)
    d_x, keep_t, send_t = back_qkv(
        flags, spans, (dq_a, dq_b, dq_c), own_kv, got_kv, x, d_res, first, gains, cosine, sine, gain_sum
    )
    grad_tokens = move(d_x)
    if fast:
        gu, do = z_sum(gu), z_sum(do)
        t = plus(keep_t, swap(send_t, "ctx", 0))
        t = plus(pick(t, rank), swap(pick(t, 1 - rank), "fsdp", 0))
        t = t.reshape((2, 4) + t.shape[1:])
        t = plus(pick(t, x_bit), swap(pick(t, 1 - x_bit), "ctx", 1))
        t = z_sum(t)

        def widen(piece):
            four = z_join(piece)
            eight = in_order(x_bit, four, join(four, 1), 0)
            return eight, join(eight, 0)

        gu, gu_other = widen(gu)
        do, do_other = widen(do)
        t, t_other = widen(t)
        own_gate = natural_gu(jnp.where(core == 0, gu, gu_other))
        own_up = natural_gu(jnp.where(core == 0, gu_other, gu))
        do = in_order(core, do, do_other, 0)
        deep = ff // 32
        own_down = do[:, :deep].reshape(ff // 2, width).astype(F32)
        own_out = do[:, deep : deep + width // 32].reshape(width // 2, width).astype(F32)
        t0, t1 = jnp.where(core == 0, t, t_other), jnp.where(core == 0, t_other, t)
        own_t = jnp.concatenate([natural_gu(t0), natural_gu(t1)], axis=1)
    else:
        pair = jnp.stack([keep_gu, send_gu])
        gate, up = (jnp.concatenate([natural_gu(pair[c, y]) for y in range(2)], axis=0) for c in range(2))
        do = jnp.stack([keep_do, send_do], axis=1).reshape((32,) + keep_do.shape[2:])
        deep = ff // 32
        own_gate, own_up = other_sum(gate), other_sum(up)
        own_down = other_sum(do[:, :deep].reshape(ff, width))
        own_out = other_sum(do[:, deep : deep + width // 32].reshape(width, width))
        pair = jnp.stack([keep_t, send_t])
        t = [jnp.concatenate([natural_gu(pair[c, y]) for c in range(2)], axis=1) for y in range(2)]
        own_t = other_sum(jnp.concatenate(t, axis=0))
    return (
        mixed_out.reshape(tokens.shape),
        grad_tokens.reshape(tokens.shape),
        own_t[:, qkv_cols],
        own_t[:, :width],
        own_t[:, width : width + kv_width],
        own_t[:, width + kv_width : qkv_cols],
        own_out,
        own_t[:, qkv_cols + 1],
        own_gate,
        own_up,
        own_down,
    )


def solution(mesh):
    rows, flat, seq = P("fsdp", None), P("fsdp"), P("fsdp", "ctx", None)
    return jax.shard_map(
        local,
        mesh=mesh,
        in_specs=(seq, flat, rows, rows, rows, rows, flat, rows, rows, rows, seq),
        out_specs=(seq, seq, flat, rows, rows, rows, rows, flat, rows, rows, rows),
        check_vma=False,
    )
```

time: 474 us -> 375 us (0.79)
  the two profiles are of different devices: /device:TPU:1 before, /device:TPU:15 now
where the time goes in v2:
time: 375 us; the launch traced here: 367 us
  Pallas kernels  130 us (35%)
  waiting for transfers between devices  81.3 us (22%)
  starting transfers between devices  78.5 us (21%)
  local copies, waits for them, and re-layouts  38.6 us (10%)
  other arithmetic  37.3 us (10%)
    ppermute x25, waiting for transfers between devices, swap(): return lax.ppermute(x, axis, [(i, i ^ 1 << bit) for i in range(n)])  55.2 us
    pallas_call x3, Pallas kernels, attn_bwd(): pl.pallas_call(functools.partial(bwd_kernel, kvs=kvs, group=group, slots=...  46.6 us
    pallas_call x1, Pallas kernels, feed_forward(): pl.pallas_call(ffn_kernel, grid=(rows // BLOCK,), in_specs=[pl.BlockSpec(...  41.1 us
    pallas_call x1, Pallas kernels, attn_fwd(): pl.pallas_call(functools.partial(fwd_kernel, kvs=kvs, group=group, slots=...  26 us
    all_to_all x4, starting transfers between devices, move(): return lax.all_to_all(x.reshape(count, sub, width), 'ctx', 0, 0, tiled=True)  25 us
    ppermute x25, starting transfers between devices, swap(): return lax.ppermute(x, axis, [(i, i ^ 1 << bit) for i in range(n)])  23.6 us
    select_n x13, other arithmetic, in_order(): jnp.where(flag == 0, jnp.concatenate([mine, other], axis=axis), jnp.conca...  16.2 us
    unnamed x35, local copies, waits for them, and re-layouts  15.7 us
  transfers between devices with their start and end apart: 35, of which 12 were waited for; matrix products, arithmetic and copies ran while one was open for 17% of the time, Pallas kernels for 24%

profile of v2, /device:TPU:15, one launch (start us, length us, event | category | flops | bytes accessed | tf_op | source)
XLA Modules:
  0.0 367.5 jit_solution(16239073668304919156)
XLA Ops:
  5.7 7.0 %all-to-all-start = ((bf16[16,64,576]{2,1,0:T(8,128)(2,1)}), bf16[16,64,576]{2,1,0:T(8,128)(2,1)}, u32[]{:S(2)}, u32[]{:S(2)}) async-start(bf16[16,64,576]{2,1,0:T(8,128)(2,1)} %bitcast.4), calls=%async_computation | async-start | bytes 2621440 | tf_op jit(solution)/shard_map/all_to_all | solution.py:535
  23.3 7.6 %collective-permute-done.7 = bf16[384,576]{1,0:T(8,128)(2,1)S(1)} collective-permute-done((bf16[384,576]{1,0:T(8,128)(2,1)S(1)}, bf16[384,576]{1,0:T(8,128)(2,1)S(1)}, u32[]{:S(2)}, u32[]{:S(2)}) %collective-permute-start.7) | collective-permute-done | bytes 442400 | tf_op jit(solution)/shard_map/ppermute | solution.py:462
  32.8 7.5 %collective-permute-done.3 = bf16[288,768]{1,0:T(8,128)(2,1)S(1)} collective-permute-done((bf16[288,768]{1,0:T(8,128)(2,1)}, bf16[288,768]{1,0:T(8,128)(2,1)S(1)}, u32[]{:S(2)}, u32[]{:S(2)}) %collective-permute-start.3) | collective-permute-done | bytes 442400 | tf_op jit(solution)/shard_map/ppermute | solution.py:462
  42.2 7.5 %collective-permute-done.5 = bf16[288,768]{1,0:T(8,128)(2,1)S(1)} collective-permute-done((bf16[288,768]{1,0:T(8,128)(2,1)}, bf16[288,768]{1,0:T(8,128)(2,1)S(1)}, u32[]{:S(2)}, u32[]{:S(2)}) %collective-permute-start.5) | collective-permute-done | bytes 442400 | tf_op jit(solution)/shard_map/ppermute | solution.py:462
  58.0 5.9 %shard_map.194 = (bf16[576,1024]{1,0:T(8,128)(2,1)}, bf16[384,1024]{1,0:T(8,128)(2,1)}) custom-call(bf16[16,64,576]{2,1,0:T(8,128)(2,1)} %all-to-all-done.x_ref.refs_6_, bf16[576,1536]{1,0:T(8,128)(2,1)} %maximum_select_fusion.1.w_ref.first_ref.refs_8_, f32[8,576]{1,0:T(8,128)} %pad_convert_fusion.gain_ref.refs_9_, ...), custom_call_target="tpu_custom_call" | custom-call | flops 6000000000 | bytes 5000000 | tf_op jit(solution)/shard_map/pallas_call | solution.py:228
  69.3 2.4 copy.39
  71.8 6.8 %all-to-all-start.1 = ((bf16[16,64,576]{2,1,0:T(8,128)(2,1)}), bf16[16,64,576]{2,1,0:T(8,128)(2,1)S(1)}, u32[]{:S(2)}, u32[]{:S(2)}) async-start(bf16[16,64,576]{2,1,0:T(8,128)(2,1)} %bitcast.7), calls=%async_computation.1 | async-start | bytes 2621440 | tf_op jit(solution)/shard_map/all_to_all | solution.py:535
  78.5 2.4 pad_maximum_fusion.kv_ref.refs_2_
  81.0 26.0 %shard_map.195 = (f32[576,1024]{1,0:T(8,128)}, f32[16,1024]{1,0:T(8,128)}) custom-call(f32[2,256,256]{2,1,0:T(8,128)} %compare_select_fusion.bias_ref.refs_0_, bf16[576,1024]{1,0:T(8,128)(2,1)} %get-tuple-element.83.q_ref.refs_1_, bf16[2,384,1024]{2,1,0:T(8,128)(2,1)} %pad_maximum_fusion.kv_ref.refs_2_), custom_call_target="tpu_custom_call" | custom-call | flops 24999999488 | bytes 8000000 | tf_op jit(solution)/shard_map/pallas_call | solution.py:73
  110.0 41.1 %shard_map.196 = (bf16[16,64,576]{2,1,0:T(8,128)(2,1)}, f32[1024,576]{1,0:T(8,128)}, bf16[576,1024]{1,0:T(8,128)(2,1)}, f32[16,1024]{1,0:T(8,128)}, bf16[2,8,144...) custom-call(s32[2]{0:T(128)} %pad_add_fusion.place_ref.refs_0_, ...), custom_call_target="tpu_custom_call" | custom-call | flops 32000000000 | bytes 20000000 | tf_op jit(solution)/shard_map/pallas_call | solution.py:333
  151.7 5.2 %all-to-all-start.2 = ((bf16[16,64,576]{2,1,0:T(8,128)(2,1)}), bf16[16,64,576]{2,1,0:T(8,128)(2,1)}, u32[]{:S(2)}, u32[]{:S(2)}) async-start(bf16[16,64,576]{2,1,0:T(8,128)(2,1)} %get-tuple-element.105), calls=%async_computation.2 | async-start | bytes 2621440 | tf_op jit(solution)/shard_map/all_to_all | solution.py:535
  156.9 14.0 %shard_map.197 = (f32[576,512]{1,0:T(8,128)}, f32[2,384,1024]{2,1,0:T(8,128)}) custom-call(f32[2,256,256]{2,1,0:T(8,128)} %compare_select_fusion.bias_ref.refs_0_, bf16[576,1024]{1,0:T(8,128)(2,1)} %get-tuple-element.83.q_ref.refs_1_, bf16[2,384,1024]{2,1,0:T(8,128)(2,1)} %pad_maximum_fusion.kv_ref.refs_2_, bf16[576,1024]{1,0:T(8,128)(2,1)} %get-tuple-element.95.refs_3_, ...), custom_call_target="tpu_custom_call" | custom-call | flops 12000000000 | bytes 16000000 | tf_op jit(solution)/shard_map/pallas_call | solution.py:168
  179.7 17.6 %shard_map.198 = (f32[576,256]{1,0:T(8,128)}, f32[2,384,1024]{2,1,0:T(8,128)}) custom-call(f32[2,256,256]{2,1,0:T(8,128)} %compare_select_fusion.bias_ref.refs_0_, bf16[576,1024]{1,0:T(8,128)(2,1)} %get-tuple-element.83.q_ref.refs_1_, bf16[2,384,1024]{2,1,0:T(8,128)(2,1)} %pad_maximum_fusion.kv_ref.refs_2_, bf16[576,1024]{1,0:T(8,128)(2,1)} %get-tuple-element.95.refs_3_, ...), custom_call_target="tpu_custom_call" | custom-call | flops 16000000000 | bytes 16000000 | tf_op jit(solution)/shard_map/pallas_call | solution.py:168
  197.4 3.8 %collective-permute-done.11 = bf16[2,4,144,384]{3,2,1,0:T(8,128)(2,1)} collective-permute-done((bf16[2,4,144,384]{3,2,1,0:T(8,128)(2,1)}, bf16[2,4,144,384]{3,2,1,0:T(8,128)(2,1)}, u32[]{:S(2)}, u32[]{:S(2)}) %collective-permute-start.11) | collective-permute-done | bytes 884768 | tf_op jit(solution)/shard_map/ppermute | solution.py:462
  206.4 15.0 %shard_map.199 = (f32[576,256]{1,0:T(8,128)}, f32[2,384,1024]{2,1,0:T(8,128)}, bf16[2,384,1024]{2,1,0:T(8,128)(2,1)}) custom-call(f32[2,256,256]{2,1,0:T(8,128)} %compare_select_fusion.bias_ref.refs_0_, bf16[576,1024]{1,0:T(8,128)(2,1)} %get-tuple-element.83.q_ref.refs_1_, bf16[2,384,1024]{2,1,0:T(8,128)(2,1)} %pad_maximum_fusion.kv_ref.refs_2_, ...), custom_call_target="tpu_custom_call" | custom-call | flops 12000000000 | bytes 16000000 | tf_op jit(solution)/shard_map/pallas_call | solution.py:168
  225.3 4.9 %all-to-all-start.6 = ((bf16[4,72,576]{2,1,0:T(8,128)(2,1)}), bf16[4,72,576]{2,1,0:T(8,128)(2,1)S(1)}, u32[]{:S(2)}, u32[]{:S(2)}) async-start(bf16[4,72,576]{2,1,0:T(8,128)(2,1)} %fusion.3), calls=%async_computation.6 | async-start | bytes 737280 | tf_op jit(solution)/shard_map/all_to_all | solution.py:498
  230.2 2.7 slice.74.refs_4_
  233.8 5.5 %all-to-all-done.6 = bf16[4,72,576]{2,1,0:T(8,128)(2,1)S(1)} async-done(((bf16[4,72,576]{2,1,0:T(8,128)(2,1)}), bf16[4,72,576]{2,1,0:T(8,128)(2,1)S(1)}, u32[]{:S(2)}, u32[]{:S(2)}) %all-to-all-start.6) | async-done | bytes 331808 | tf_op jit(solution)/shard_map/all_to_all | solution.py:498
  239.4 5.8 %all-to-all-start.8 = ((bf16[4,144,384]{2,1,0:T(8,128)(2,1)}), bf16[4,144,384]{2,1,0:T(8,128)(2,1)S(1)}, u32[]{:S(2)}, u32[]{:S(2)}) async-start(bf16[4,144,384]{2,1,0:T(8,128)(2,1)} %fusion.2), calls=%async_computation.8 | async-start | bytes 884736 | tf_op jit(solution)/shard_map/all_to_all | solution.py:498
  246.1 10.6 %shard_map.200 = (bf16[16,64,576]{2,1,0:T(8,128)(2,1)}, bf16[2,8,144,128]{3,2,1,0:T(8,128)(2,1)}, bf16[2,8,144,128]{3,2,1,0:T(8,128)(2,1)}) custom-call(s32[2]{0:T(128)} %pad_add_fusion.place_ref.refs_0_, f32[576,512]{1,0:T(8,128)} %get-tuple-element.109.refs_1_, f32[576,256]{1,0:T(8,128)} %get-tuple-element.110.refs_2_, ...), custom_call_target="tpu_custom_call" | custom-call | flops 10000000000 | bytes 10000000 | tf_op jit(solution)/shard_map/pallas_call | solution.py:433
  258.7 4.5 %all-to-all-start.7 = ((bf16[4,72,576]{2,1,0:T(8,128)(2,1)}), bf16[4,72,576]{2,1,0:T(8,128)(2,1)S(1)}, u32[]{:S(2)}, u32[]{:S(2)}) async-start(bf16[4,72,576]{2,1,0:T(8,128)(2,1)} %broadcast_in_dim.17), calls=%async_computation.7 | async-start | bytes 737280 | tf_op jit(solution)/shard_map/all_to_all | solution.py:504
  263.3 8.7 %all-to-all-done.7 = bf16[4,72,576]{2,1,0:T(8,128)(2,1)S(1)} async-done(((bf16[4,72,576]{2,1,0:T(8,128)(2,1)}), bf16[4,72,576]{2,1,0:T(8,128)(2,1)S(1)}, u32[]{:S(2)}, u32[]{:S(2)}) %all-to-all-start.7) | async-done | bytes 331808 | tf_op jit(solution)/shard_map/all_to_all | solution.py:504
  272.8 5.6 %all-to-all-start.9 = ((bf16[4,144,384]{2,1,0:T(8,128)(2,1)}), bf16[4,144,384]{2,1,0:T(8,128)(2,1)S(1)}, u32[]{:S(2)}, u32[]{:S(2)}) async-start(bf16[4,144,384]{2,1,0:T(8,128)(2,1)} %broadcast_in_dim.18), calls=%async_computation.9 | async-start | bytes 884736 | tf_op jit(solution)/shard_map/all_to_all | solution.py:504
  279.8 7.5 %collective-permute-done.21 = bf16[4,72,576]{2,1,0:T(8,128)(2,1)} collective-permute-done((bf16[4,72,576]{2,1,0:T(8,128)(2,1)S(1)}, bf16[4,72,576]{2,1,0:T(8,128)(2,1)}, u32[]{:S(2)}, u32[]{:S(2)}) %collective-permute-start.21) | collective-permute-done | bytes 331808 | tf_op jit(solution)/shard_map/ppermute | solution.py:462
  288.5 2.4 collective-permute-start.22
  292.6 13.2 %collective-permute-done.18 = bf16[4,144,128]{2,1,0:T(8,128)(2,1)S(1)} collective-permute-done((bf16[4,144,128]{2,1,0:T(8,128)(2,1)S(1)}, bf16[4,144,128]{2,1,0:T(8,128)(2,1)S(1)}, u32[]{:S(2)}, u32[]{:S(2)}) %collective-permute-start.18) | collective-permute-done | bytes 147488 | tf_op jit(solution)/shard_map/ppermute | solution.py:462
  306.5 4.5 %all-to-all-start.4 = ((bf16[4,144,128]{2,1,0:T(8,128)(2,1)}), bf16[4,144,128]{2,1,0:T(8,128)(2,1)S(1)}, u32[]{:S(2)}, u32[]{:S(2)}) async-start(bf16[4,144,128]{2,1,0:T(8,128)(2,1)} %fusion.6), calls=%async_computation.4 | async-start | bytes 294912 | tf_op jit(solution)/shard_map/all_to_all | solution.py:498
  313.5 2.4 copy.47
  319.4 4.5 %all-to-all-start.5 = ((bf16[4,144,128]{2,1,0:T(8,128)(2,1)}), bf16[4,144,128]{2,1,0:T(8,128)(2,1)}, u32[]{:S(2)}, u32[]{:S(2)}) async-start(bf16[4,144,128]{2,1,0:T(8,128)(2,1)} %broadcast_in_dim.16), calls=%async_computation.5 | async-start | bytes 294912 | tf_op jit(solution)/shard_map/all_to_all | solution.py:504
  328.9 6.1 %all-to-all-start.3 = ((bf16[16,64,576]{2,1,0:T(8,128)(2,1)}), bf16[16,64,576]{2,1,0:T(8,128)(2,1)S(1)}, u32[]{:S(2)}, u32[]{:S(2)}) async-start(bf16[16,64,576]{2,1,0:T(8,128)(2,1)} %get-tuple-element.124), calls=%async_computation.3 | async-start | bytes 2621440 | tf_op jit(solution)/shard_map/all_to_all | solution.py:535
  338.4 8.0 %collective-permute-done.19 = bf16[4,144,128]{2,1,0:T(8,128)(2,1)S(1)} collective-permute-done((bf16[4,144,128]{2,1,0:T(8,128)(2,1)}, bf16[4,144,128]{2,1,0:T(8,128)(2,1)S(1)}, u32[]{:S(2)}, u32[]{:S(2)}) %collective-permute-start.19) | collective-permute-done | bytes 147488 | tf_op jit(solution)/shard_map/ppermute | solution.py:462
  357.7 7.9 %all-to-all-done.3 = bf16[16,64,576]{2,1,0:T(8,128)(2,1)S(1)} async-done(((bf16[16,64,576]{2,1,0:T(8,128)(2,1)}), bf16[16,64,576]{2,1,0:T(8,128)(2,1)S(1)}, u32[]{:S(2)}, u32[]{:S(2)}) %all-to-all-start.3) | async-done | bytes 1179680 | tf_op jit(solution)/shard_map/all_to_all | solution.py:535
  (156 shorter events, 91.0 us)
Async XLA Ops:
  4.0 14.3 %collective-permute-start = (bf16[296,768]{1,0:T(8,128)(2,1)S(1)}, bf16[296,768]{1,0:T(8,128)(2,1)}, u32[]{:S(2)}, u32[]{:S(2)}) collective-permute-start(bf16[296,768]{1,0:T(8,128)(2,1)S(1)} %fusion.5), channel_id=1, source_target_pairs={{0,16},{16,0},{1,17},{17,1},{2,18},{18,2},{3,19},{19,3},{4,20},{20... | collective-permute-start | bytes 1363976 | tf_op jit(solution)/shard_map/ppermute | solution.py:462
  5.7 52.3 %all-to-all-start = ((bf16[16,64,576]{2,1,0:T(8,128)(2,1)}), bf16[16,64,576]{2,1,0:T(8,128)(2,1)}, u32[]{:S(2)}, u32[]{:S(2)}) async-start(bf16[16,64,576]{2,1,0:T(8,128)(2,1)} %bitcast.4), calls=%async_computation | async-start | bytes 2621440 | tf_op jit(solution)/shard_map/all_to_all | solution.py:535
  18.3 12.6 %collective-permute-start.7 = (bf16[384,576]{1,0:T(8,128)(2,1)S(1)}, bf16[384,576]{1,0:T(8,128)(2,1)S(1)}, u32[]{:S(2)}, u32[]{:S(2)}) collective-permute-start(bf16[384,576]{1,0:T(8,128)(2,1)S(1)} %constant_dynamic-slice_fusion), channel_id=1, source_target_pairs={{0,16},{16,0},{1,17},{17,1},{2,18},{18,2},{3,19},{19,3},{4,20},{20... | collective-permute-start | bytes 1327112 | tf_op jit(solution)/shard_map/ppermute | solution.py:462
  19.6 20.7 %collective-permute-start.3 = (bf16[288,768]{1,0:T(8,128)(2,1)}, bf16[288,768]{1,0:T(8,128)(2,1)S(1)}, u32[]{:S(2)}, u32[]{:S(2)}) collective-permute-start(bf16[288,768]{1,0:T(8,128)(2,1)} %get-tuple-element.89), channel_id=1, source_target_pairs={{0,16},{16,0},{1,17},{17,1},{2,18},{18,2},{3,19},{19,3},{4,20},{20... | collective-permute-start | bytes 1327112 | tf_op jit(solution)/shard_map/ppermute | solution.py:462
  19.8 29.9 %collective-permute-start.5 = (bf16[288,768]{1,0:T(8,128)(2,1)}, bf16[288,768]{1,0:T(8,128)(2,1)S(1)}, u32[]{:S(2)}, u32[]{:S(2)}) collective-permute-start(bf16[288,768]{1,0:T(8,128)(2,1)} %get-tuple-element.90), channel_id=1, source_target_pairs={{0,16},{16,0},{1,17},{17,1},{2,18},{18,2},{3,19},{19,3},{4,20},{20... | collective-permute-start | bytes 1327112 | tf_op jit(solution)/shard_map/ppermute | solution.py:462
  21.0 29.9 %collective-permute-start.1 = (bf16[296,768]{1,0:T(8,128)(2,1)}, bf16[296,768]{1,0:T(8,128)(2,1)S(1)}, u32[]{:S(2)}, u32[]{:S(2)}) collective-permute-start(bf16[296,768]{1,0:T(8,128)(2,1)} %collective-permute-done), channel_id=1, source_target_pairs={{0,1},{1,0},{2,3},{3,2},{4,5},{5,4},{6,7},{7,6},{8,9},{9,8},{10,11... | collective-permute-start | bytes 1363976 | tf_op jit(solution)/shard_map/ppermute | solution.py:462
  30.9 24.1 %collective-permute-start.8 = (bf16[384,576]{1,0:T(8,128)(2,1)S(1)}, bf16[384,576]{1,0:T(8,128)(2,1)S(1)}, u32[]{:S(2)}, u32[]{:S(2)}) collective-permute-start(bf16[384,576]{1,0:T(8,128)(2,1)S(1)} %collective-permute-done.7), channel_id=1, source_target_pairs={{0,1},{1,0},{2,3},{3,2},{4,5},{5,4},{6,7},{7,6},{8,9},{9,8},{10,11... | collective-permute-start | bytes 1327112 | tf_op jit(solution)/shard_map/ppermute | solution.py:462
  40.3 15.1 %collective-permute-start.4 = (bf16[288,768]{1,0:T(8,128)(2,1)S(1)}, bf16[288,768]{1,0:T(8,128)(2,1)S(1)}, u32[]{:S(2)}, u32[]{:S(2)}) collective-permute-start(bf16[288,768]{1,0:T(8,128)(2,1)S(1)} %collective-permute-done.3), channel_id=1, source_target_pairs={{0,1},{1,0},{2,3},{3,2},{4,5},{5,4},{6,7},{7,6},{8,9},{9,8},{10,11... | collective-permute-start | bytes 1327112 | tf_op jit(solution)/shard_map/ppermute | solution.py:462
  49.8 14.2 %collective-permute-start.6 = (bf16[288,768]{1,0:T(8,128)(2,1)S(1)}, bf16[288,768]{1,0:T(8,128)(2,1)}, u32[]{:S(2)}, u32[]{:S(2)}) collective-permute-start(bf16[288,768]{1,0:T(8,128)(2,1)S(1)} %collective-permute-done.5), channel_id=1, source_target_pairs={{0,1},{1,0},{2,3},{3,2},{4,5},{5,4},{6,7},{7,6},{8,9},{9,8},{10,11... | collective-permute-start | bytes 1327112 | tf_op jit(solution)/shard_map/ppermute | solution.py:462
  64.0 14.6 %collective-permute-start.2 = (bf16[384,1024]{1,0:T(8,128)(2,1)}, bf16[384,1024]{1,0:T(8,128)(2,1)}, u32[]{:S(2)}, u32[]{:S(2)}) collective-permute-start(bf16[384,1024]{1,0:T(8,128)(2,1)} %get-tuple-element.84), channel_id=1, source_target_pairs={{0,1},{1,0},{2,3},{3,2},{4,5},{5,4},{6,7},{7,6},{8,9},{9,8},{10,11... | collective-permute-start | bytes 2359304 | tf_op jit(solution)/shard_map/ppermute | solution.py:462
  71.8 37.2 %all-to-all-start.1 = ((bf16[16,64,576]{2,1,0:T(8,128)(2,1)}), bf16[16,64,576]{2,1,0:T(8,128)(2,1)S(1)}, u32[]{:S(2)}, u32[]{:S(2)}) async-start(bf16[16,64,576]{2,1,0:T(8,128)(2,1)} %bitcast.7), calls=%async_computation.1 | async-start | bytes 2621440 | tf_op jit(solution)/shard_map/all_to_all | solution.py:535
  151.1 19.8 %collective-permute-start.9 = (bf16[2,8,144,384]{3,2,1,0:T(8,128)(2,1)}, bf16[2,8,144,384]{3,2,1,0:T(8,128)(2,1)S(1)}, u32[]{:S(2)}, u32[]{:S(2)}) collective-permute-start(bf16[2,8,144,384]{3,2,1,0:T(8,128)(2,1)} %get-tuple-element.93), channel_id=1, source_target_pairs={{0,1},{1,0},{2,3},{3,2},{4,5},{5,4},{6,7},{7,6},{8,9},{9,8},{10,11... | collective-permute-start | bytes 5308424 | tf_op jit(solution)/shard_map/ppermute | solution.py:462
  151.4 19.5 %collective-permute-start.10 = (bf16[2,8,72,576]{3,2,1,0:T(8,128)(2,1)}, bf16[2,8,72,576]{3,2,1,0:T(8,128)(2,1)S(1)}, u32[]{:S(2)}, u32[]{:S(2)}) collective-permute-start(bf16[2,8,72,576]{3,2,1,0:T(8,128)(2,1)} %get-tuple-element.94), channel_id=1, source_target_pairs={{0,1},{1,0},{2,3},{3,2},{4,5},{5,4},{6,7},{7,6},{8,9},{9,8},{10,11... | collective-permute-start | bytes 3981320 | tf_op jit(solution)/shard_map/ppermute | solution.py:462
  151.7 45.7 %all-to-all-start.2 = ((bf16[16,64,576]{2,1,0:T(8,128)(2,1)}), bf16[16,64,576]{2,1,0:T(8,128)(2,1)}, u32[]{:S(2)}, u32[]{:S(2)}) async-start(bf16[16,64,576]{2,1,0:T(8,128)(2,1)} %get-tuple-element.105), calls=%async_computation.2 | async-start | bytes 2621440 | tf_op jit(solution)/shard_map/all_to_all | solution.py:535
  178.2 22.9 %collective-permute-start.11 = (bf16[2,4,144,384]{3,2,1,0:T(8,128)(2,1)}, bf16[2,4,144,384]{3,2,1,0:T(8,128)(2,1)}, u32[]{:S(2)}, u32[]{:S(2)}) collective-permute-start(bf16[2,4,144,384]{3,2,1,0:T(8,128)(2,1)} %dynamic-slice_bitcast_fusion), channel_id=1, source_target_pairs={{0,2},{1,3},{2,0},{3,1},{4,6},{5,7},{6,4},{7,5},{8,10},{9,11},{10,... | collective-permute-start | bytes 2654216 | tf_op jit(solution)/shard_map/ppermute | solution.py:462
  178.5 18.9 %collective-permute-start.12 = (bf16[8,72,576]{2,1,0:T(8,128)(2,1)}, bf16[8,72,576]{2,1,0:T(8,128)(2,1)}, u32[]{:S(2)}, u32[]{:S(2)}) collective-permute-start(bf16[8,72,576]{2,1,0:T(8,128)(2,1)} %dynamic-slice_bitcast_fusion.1), channel_id=1, source_target_pairs={{0,16},{16,0},{1,17},{17,1},{2,18},{18,2},{3,19},{19,3},{4,20},{20... | collective-permute-start | bytes 1990664 | tf_op jit(solution)/shard_map/ppermute | solution.py:462
  204.8 16.6 %collective-permute-start.13 = (bf16[4,144,384]{2,1,0:T(8,128)(2,1)S(1)}, bf16[4,144,384]{2,1,0:T(8,128)(2,1)S(1)}, u32[]{:S(2)}, u32[]{:S(2)}) collective-permute-start(bf16[4,144,384]{2,1,0:T(8,128)(2,1)S(1)} %dynamic-slice_bitcast_fusion.2), channel_id=1, source_target_pairs={{0,16},{16,0},{1,17},{17,1},{2,18},{18,2},{3,19},{19,3},{4,20},{20... | collective-permute-start | bytes 1327112 | tf_op jit(solution)/shard_map/ppermute | solution.py:462
  206.1 15.3 %collective-permute-start.14 = (bf16[4,72,576]{2,1,0:T(8,128)(2,1)S(1)}, bf16[4,72,576]{2,1,0:T(8,128)(2,1)S(1)}, u32[]{:S(2)}, u32[]{:S(2)}) collective-permute-start(bf16[4,72,576]{2,1,0:T(8,128)(2,1)S(1)} %dynamic-slice_bitcast_fusion.3), channel_id=1, source_target_pairs={{0,2},{1,3},{2,0},{3,1},{4,6},{5,7},{6,4},{7,5},{8,10},{9,11},{10,... | collective-permute-start | bytes 995336 | tf_op jit(solution)/shard_map/ppermute | solution.py:462
  222.7 22.5 %collective-permute-start.15 = (bf16[384,1024]{1,0:T(8,128)(2,1)S(1)}, bf16[384,1024]{1,0:T(8,128)(2,1)S(1)}, u32[]{:S(2)}, u32[]{:S(2)}) collective-permute-start(bf16[384,1024]{1,0:T(8,128)(2,1)S(1)} %slice_bitcast_fusion), channel_id=1, source_target_pairs={{0,1},{1,0},{2,3},{3,2},{4,5},{5,4},{6,7},{7,6},{8,9},{9,8},{10,11... | collective-permute-start | bytes 2359304 | tf_op jit(solution)/shard_map/ppermute | solution.py:462
  225.3 14.0 %all-to-all-start.6 = ((bf16[4,72,576]{2,1,0:T(8,128)(2,1)}), bf16[4,72,576]{2,1,0:T(8,128)(2,1)S(1)}, u32[]{:S(2)}, u32[]{:S(2)}) async-start(bf16[4,72,576]{2,1,0:T(8,128)(2,1)} %fusion.3), calls=%async_computation.6 | async-start | bytes 737280 | tf_op jit(solution)/shard_map/all_to_all | solution.py:498
  239.4 18.5 %all-to-all-start.8 = ((bf16[4,144,384]{2,1,0:T(8,128)(2,1)}), bf16[4,144,384]{2,1,0:T(8,128)(2,1)S(1)}, u32[]{:S(2)}, u32[]{:S(2)}) async-start(bf16[4,144,384]{2,1,0:T(8,128)(2,1)} %fusion.2), calls=%async_computation.8 | async-start | bytes 884736 | tf_op jit(solution)/shard_map/all_to_all | solution.py:498
  256.7 22.6 %collective-permute-start.16 = (bf16[2,8,144,128]{3,2,1,0:T(8,128)(2,1)}, bf16[2,8,144,128]{3,2,1,0:T(8,128)(2,1)S(1)}, u32[]{:S(2)}, u32[]{:S(2)}) collective-permute-start(bf16[2,8,144,128]{3,2,1,0:T(8,128)(2,1)} %get-tuple-element.126), channel_id=1, source_target_pairs={{0,1},{1,0},{2,3},{3,2},{4,5},{5,4},{6,7},{7,6},{8,9},{9,8},{10,11... | collective-permute-start | bytes 1769480 | tf_op jit(solution)/shard_map/ppermute | solution.py:462
  258.7 13.3 %all-to-all-start.7 = ((bf16[4,72,576]{2,1,0:T(8,128)(2,1)}), bf16[4,72,576]{2,1,0:T(8,128)(2,1)S(1)}, u32[]{:S(2)}, u32[]{:S(2)}) async-start(bf16[4,72,576]{2,1,0:T(8,128)(2,1)} %broadcast_in_dim.17), calls=%async_computation.7 | async-start | bytes 737280 | tf_op jit(solution)/shard_map/all_to_all | solution.py:504
  272.8 18.1 %all-to-all-start.9 = ((bf16[4,144,384]{2,1,0:T(8,128)(2,1)}), bf16[4,144,384]{2,1,0:T(8,128)(2,1)S(1)}, u32[]{:S(2)}, u32[]{:S(2)}) async-start(bf16[4,144,384]{2,1,0:T(8,128)(2,1)} %broadcast_in_dim.18), calls=%async_computation.9 | async-start | bytes 884736 | tf_op jit(solution)/shard_map/all_to_all | solution.py:504
  279.5 12.3 %collective-permute-start.17 = (bf16[8,144,128]{2,1,0:T(8,128)(2,1)S(1)}, bf16[8,144,128]{2,1,0:T(8,128)(2,1)S(1)}, u32[]{:S(2)}, u32[]{:S(2)}) collective-permute-start(bf16[8,144,128]{2,1,0:T(8,128)(2,1)S(1)} %dynamic-slice_bitcast_fusion.4), channel_id=1, source_target_pairs={{0,16},{16,0},{1,17},{17,1},{2,18},{18,2},{3,19},{19,3},{4,20},{20... | collective-permute-start | bytes 884744 | tf_op jit(solution)/shard_map/ppermute | solution.py:462
  288.5 27.4 %collective-permute-start.22 = (bf16[8,72,576]{2,1,0:T(8,128)(2,1)S(1)}, bf16[8,72,576]{2,1,0:T(8,128)(2,1)}, u32[]{:S(2)}, u32[]{:S(2)}) collective-permute-start(bf16[8,72,576]{2,1,0:T(8,128)(2,1)S(1)} %maximum_select_fusion.10), channel_id=1, source_target_pairs={{0,1},{1,0},{2,3},{3,2},{4,5},{5,4},{6,7},{7,6},{8,9},{9,8},{10,11... | collective-permute-start | bytes 1990664 | tf_op jit(solution)/shard_map/ppermute | solution.py:462
  290.9 20.1 %collective-permute-start.23 = (bf16[4,144,384]{2,1,0:T(8,128)(2,1)S(1)}, bf16[4,144,384]{2,1,0:T(8,128)(2,1)S(1)}, u32[]{:S(2)}, u32[]{:S(2)}) collective-permute-start(bf16[4,144,384]{2,1,0:T(8,128)(2,1)S(1)} %all-to-all-done.9), channel_id=1, source_target_pairs={{0,2},{1,3},{2,0},{3,1},{4,6},{5,7},{6,4},{7,5},{8,10},{9,11},{10,... | collective-permute-start | bytes 1327112 | tf_op jit(solution)/shard_map/ppermute | solution.py:462
  291.9 13.9 %collective-permute-start.18 = (bf16[4,144,128]{2,1,0:T(8,128)(2,1)S(1)}, bf16[4,144,128]{2,1,0:T(8,128)(2,1)S(1)}, u32[]{:S(2)}, u32[]{:S(2)}) collective-permute-start(bf16[4,144,128]{2,1,0:T(8,128)(2,1)S(1)} %dynamic-slice_bitcast_fusion.5), channel_id=1, source_target_pairs={{0,2},{1,3},{2,0},{3,1},{4,6},{5,7},{6,4},{7,5},{8,10},{9,11},{10,... | collective-permute-start | bytes 442376 | tf_op jit(solution)/shard_map/ppermute | solution.py:462
  306.5 12.2 %all-to-all-start.4 = ((bf16[4,144,128]{2,1,0:T(8,128)(2,1)}), bf16[4,144,128]{2,1,0:T(8,128)(2,1)S(1)}, u32[]{:S(2)}, u32[]{:S(2)}) async-start(bf16[4,144,128]{2,1,0:T(8,128)(2,1)} %fusion.6), calls=%async_computation.4 | async-start | bytes 294912 | tf_op jit(solution)/shard_map/all_to_all | solution.py:498
  312.1 36.3 %collective-permute-start.24 = (bf16[8,144,384]{2,1,0:T(8,128)(2,1)}, bf16[8,144,384]{2,1,0:T(8,128)(2,1)}, u32[]{:S(2)}, u32[]{:S(2)}) collective-permute-start(bf16[8,144,384]{2,1,0:T(8,128)(2,1)} %maximum_select_fusion.9), channel_id=1, source_target_pairs={{0,1},{1,0},{2,3},{3,2},{4,5},{5,4},{6,7},{7,6},{8,9},{9,8},{10,11... | collective-permute-start | bytes 2654216 | tf_op jit(solution)/shard_map/ppermute | solution.py:462
  328.9 36.6 %all-to-all-start.3 = ((bf16[16,64,576]{2,1,0:T(8,128)(2,1)}), bf16[16,64,576]{2,1,0:T(8,128)(2,1)S(1)}, u32[]{:S(2)}, u32[]{:S(2)}) async-start(bf16[16,64,576]{2,1,0:T(8,128)(2,1)} %get-tuple-element.124), calls=%async_computation.3 | async-start | bytes 2621440 | tf_op jit(solution)/shard_map/all_to_all | solution.py:535
  335.0 11.4 %collective-permute-start.19 = (bf16[4,144,128]{2,1,0:T(8,128)(2,1)}, bf16[4,144,128]{2,1,0:T(8,128)(2,1)S(1)}, u32[]{:S(2)}, u32[]{:S(2)}) collective-permute-start(bf16[4,144,128]{2,1,0:T(8,128)(2,1)} %all-to-all-done.5), channel_id=1, source_target_pairs={{0,2},{1,3},{2,0},{3,1},{4,6},{5,7},{6,4},{7,5},{8,10},{9,11},{10,... | collective-permute-start | bytes 442376 | tf_op jit(solution)/shard_map/ppermute | solution.py:462
  (16 other events, 84.0 us)

commit v3 on v2

--- a/solution.py
+++ b/solution.py
@@ -24,14 +24,15 @@
 def heads_of(ref, kv, group):
     return jnp.concatenate([ref[(kv*group+h)*64:(kv*group+h+1)*64,:] for h in range(group)],axis=1)
 
-def fwd_kernel(bias_ref, q_ref, kv_ref, o_ref, lse_ref, k_scr, m_scr, acc_scr, *, kvs, group, slots, rows, qb):
+def fwd_kernel(bias_ref, q_ref, *refs, kvs, group, slots, rows, qb):
+    kv_ref, (o_ref, lse_ref, k_scr, m_scr, acc_scr)=refs[:slots], refs[slots:]
     i=pl.program_id(0)
     kw=kvs*64
     @pl.when(i==0)
     def _():
         for s in range(slots):
             for h in range(kvs):
-                k_scr[h,s]=kv_ref[s,h*64:(h+1)*64,:].T
+                k_scr[h,s]=kv_ref[s][h*64:(h+1)*64,:].T
     qs=[heads_of(q_ref,h,group) for h in range(kvs)]
     width=group*qb
     m_scr[...]=jnp.full(m_scr.shape,-1e30,F32)
@@ -41,7 +42,7 @@
         off=pl.multiple_of(c*qb,qb)
         for h in range(kvs):
             k=jnp.concatenate([k_scr[h,s,pl.ds(off,qb),:] for s in range(slots)],axis=0)
-            v=jnp.concatenate([kv_ref[s,kw+h*64:kw+(h+1)*64,pl.ds(off,qb)] for s in range(slots)],axis=1)
+            v=jnp.concatenate([kv_ref[s][kw+h*64:kw+(h+1)*64,pl.ds(off,qb)] for s in range(slots)],axis=1)
             v=jnp.concatenate([v,ones],axis=0)
             st=mm(k,qs[h])
             if masked:
@@ -67,7 +68,7 @@
             lse_ref[r:r+1,:]=lse[:,g*qb:(g+1)*qb]
 
 def attn_fwd(bias, qT, kvT, kvs=3, group=3, qb=256):
-    slots,_,rows=kvT.shape
+    slots,rows=len(kvT),kvT[0].shape[1]
     n=rows//qb
     heads=kvs*group
     return pl.pallas_call(
@@ -75,7 +76,7 @@
         grid=(n,),
         in_specs=[pl.BlockSpec((slots,qb,qb),lambda i:(0,0,0)),
                   pl.BlockSpec((heads*64,qb),lambda i:(0,i)),
-                  pl.BlockSpec((slots,2*kvs*64,rows),lambda i:(0,0,0))],
+                  *[pl.BlockSpec((2*kvs*64,rows),lambda i:(0,0))]*slots],
         out_specs=[pl.BlockSpec((heads*64,qb),lambda i:(0,i)),
                    pl.BlockSpec((16,qb),lambda i:(0,i))],
         out_shape=[jax.ShapeDtypeStruct((heads*64,rows),F32),jax.ShapeDtypeStruct((16,rows),F32)],
@@ -83,11 +84,11 @@
                         pltpu.VMEM((kvs,72,group*qb),F32)],
         compiler_params=pltpu.CompilerParams(vmem_limit_bytes=56*2**20),
         cost_estimate=pl.CostEstimate(flops=int(25e9),bytes_accessed=int(8e6),transcendentals=int(1e7)),
-    )(bias,qT,kvT)
+    )(bias,qT,*kvT)
 
 def bwd_kernel(*refs, kvs, group, slots, qb, lo, first, last):
-    bias_ref, q_ref, kv_ref, do_ref, lse_ref, rd_ref = refs[:6]
-    refs = refs[6:]
+    bias_ref, q_ref, do_ref, lse_ref, rd_ref = refs[:5]
+    kv_ref, refs = refs[5 : 5 + slots], refs[5 + slots :]
     if not first:
         before_ref, refs = refs[0], refs[1:]
     if last:
@@ -101,7 +102,7 @@
     def _():
         for s in range(slots):
             for h in range(2 * kvs):
-                kv_scr[h, s] = kv_ref[s, h * 64 : (h + 1) * 64, :].T
+                kv_scr[h, s] = kv_ref[s][h * 64 : (h + 1) * 64, :].T
         dkv_ref[...] = jnp.zeros(dkv_ref.shape, F32) if first else before_ref[...]
 
     dq_ref[...] = jnp.zeros(dq_ref.shape, F32)
@@ -119,7 +120,7 @@
         for h in range(kvs):
             k = jnp.concatenate([kv_scr[h, s, pl.ds(off, qb), :] for s in range(slots)], axis=0)
             v = jnp.concatenate([kv_scr[kvs + h, s, pl.ds(off, qb), :] for s in range(slots)], axis=0)
-            k_t = jnp.concatenate([kv_ref[s, h * 64 : (h + 1) * 64, pl.ds(off, qb)] for s in range(slots)], axis=1)
+            k_t = jnp.concatenate([kv_ref[s][h * 64 : (h + 1) * 64, pl.ds(off, qb)] for s in range(slots)], axis=1)
             st = mm(k, qs[h])
             if masked:
                 st = st + jnp.concatenate([bias_ref[...].reshape(slots * qb, qb)] * group, axis=1)
@@ -150,7 +151,7 @@
 
 
 def attn_bwd(bias, q_t, kv_t, do_t, lse, rd, lo, hi, before=None, last=False, kvs=3, group=3, qb=256):
-    slots, _, rows = kv_t.shape
+    slots, rows = len(kv_t), kv_t[0].shape[1]
     width = kvs * group * 64
     whole = pl.BlockSpec((slots, 2 * kvs * 64, rows), lambda i: (0, 0, 0))
     tall = pl.BlockSpec((width, qb), lambda i: (0, i + lo))
@@ -163,14 +164,15 @@
     if last:
         out_specs.append(whole)
         out_shape.append(jax.ShapeDtypeStruct((slots, 2 * kvs * 64, rows), BF))
-    args = (bias, q_t, kv_t, do_t, lse, rd) + (() if before is None else (before,))
+    args = (bias, q_t, do_t, lse, rd, *kv_t) + (() if before is None else (before,))
     units = sum(range(lo + 1, hi + 1))
     return pl.pallas_call(
         functools.partial(
             bwd_kernel, kvs=kvs, group=group, slots=slots, qb=qb, lo=lo, first=before is None, last=last
         ),
         grid=(hi - lo,),
-        in_specs=[pl.BlockSpec((slots, qb, qb), lambda i: (0, 0, 0)), tall, whole, tall, stat, stat]
+        in_specs=[pl.BlockSpec((slots, qb, qb), lambda i: (0, 0, 0)), tall, tall, stat, stat]
+        + [pl.BlockSpec((2 * kvs * 64, rows), lambda i: (0, 0))] * slots
         + ([] if before is None else [whole]),
         out_specs=out_specs,
         out_shape=out_shape,
@@ -246,7 +248,7 @@
 def ffn_kernel(
     place_ref, o_ref, x_ref, cot_ref, first_ref, gate_ref, up_ref, down_ref, gain_ref,
     mixed_ref, dres_ref, datt_ref, rd_ref, keep_gu, send_gu, keep_do, send_do, gg_ref,
-    acc_gu, acc_down, acc_out, out_scr,
+    acc_gu, acc_down, acc_out,
 ):
     step = pl.program_id(0)
     width = x_ref.shape[2]
@@ -288,7 +290,7 @@
     d_res = cot.astype(F32) + scale * (d_hidden * gain - normed * inner)
     dres_ref[...] = d_res
     d_low = d_res.astype(BF)
-    acc_out[: acc_out.shape[0] - 16] += mm(mixed, d_low)
+    acc_out[...] += mm(mixed, d_low)
     d_att = mm(out_w, d_low, NT).astype(BF)
     datt_ref[...] = d_att
     prod = d_att.astype(F32) * attended
@@ -307,15 +309,14 @@
                 cs = slice((p % 4) * (ff // 4), (p % 4 + 1) * (ff // 4))
                 keep_gu[y, p] = acc_gu[core, rs, cs].astype(BF)
                 send_gu[y, p] = acc_gu[1 - core, rs, cs].astype(BF)
-        down_rows, out_rows = ff // 32, width // 32
-        for m in range(32):
-            out_scr[m] = acc_out[m * out_rows : m * out_rows + 24, :].astype(F32)
+        down_rows, out_rows = ff // 32, width // 24
         for y in range(2):
             for p in range(PIECES):
                 for ref, c in ((keep_do, core), (send_do, 1 - core)):
                     start = pl.multiple_of(y * (ff // 2) + (PIECES * c + p) * down_rows, 16)
                     ref[y, p, :down_rows] = acc_down[pl.ds(start, down_rows), :].astype(BF)
-                    ref[y, p, down_rows:] = out_scr[y * 16 + PIECES * c + p].astype(BF)
+                    start = y * half + jnp.minimum(PIECES * c + p, half // out_rows - 1) * out_rows
+                    ref[y, p, down_rows:] = acc_out[pl.ds(pl.multiple_of(start, 8), out_rows), :].astype(BF)
 
 
 def feed_forward(place, attended, x, cot, first, gate_w, up_w, down_w, gains):
@@ -323,7 +324,7 @@
     rows, ff = count * sub, gate_w.shape[1]
     per = BLOCK // sub
     gu = (2, PIECES, width // 4, ff // 4)
-    do = (2, PIECES, ff // 32 + 24, width)
+    do = (2, PIECES, ff // 32 + width // 24, width)
 
     def whole(shape):
         return pl.BlockSpec(shape, lambda i: (0,) * len(shape))
@@ -351,8 +352,7 @@
             jax.ShapeDtypeStruct((8, width), F32),
         ],
         scratch_shapes=[
-            pltpu.VMEM((2, width, ff), F32), pltpu.VMEM((ff, width), F32), pltpu.VMEM((width + 16, width), F32),
-            pltpu.VMEM((32, 24, width), F32),
+            pltpu.VMEM((2, width, ff), F32), pltpu.VMEM((ff, width), F32), pltpu.VMEM((width, width), F32),
         ],
         compiler_params=pltpu.CompilerParams(vmem_limit_bytes=LIMIT),
         cost_estimate=pl.CostEstimate(flops=int(32e9), bytes_accessed=int(20e6), transcendentals=0),
@@ -457,6 +457,78 @@
     )(place, *d_query, d_kv, got, x, d_res, first, gains, cosine, sine, gg)
 
 
+def final_kernel(
+    at_ref, gu4, gu_x, gu_c, do4, do_x, do_c, gate_ref, up_ref, down_ref, out_ref
+):
+    core, xb, z = at_ref[0], at_ref[1], at_ref[2]
+    deep, wide = gu4.shape[1:]
+    for f in range(2):
+        for e in range(2):
+            for d in range(4):
+                gu = (gu4[d] if e == 0 else gu_x[d]) if f == 0 else gu_c[e * 4 + d]
+                do = (do4[d] if e == 0 else do_x[d]) if f == 0 else do_c[e * 4 + d]
+                rs = pl.ds(pl.multiple_of((xb ^ e) * deep, 16), deep)
+                cs = pl.ds(pl.multiple_of((z ^ d) * wide, 128), wide)
+                for c, ref in ((0, gate_ref), (1, up_ref)):
+
+                    @pl.when((core ^ f) == c)
+                    def _():
+                        ref[rs, cs] = gu.astype(F32)
+
+                m = (core ^ f) * 8 + (xb ^ e) * 4 + (z ^ d)
+                rows = down_ref.shape[0] // 16
+                down_ref[pl.ds(pl.multiple_of(m * rows, 8), rows), :] = do[:rows].astype(F32)
+                few = do.shape[0] - rows
+
+                @pl.when(m < out_ref.shape[0] // few)
+                def _():
+                    out_ref[pl.ds(pl.multiple_of(m * few, 8), few), :] = do[rows:].astype(F32)
+
+
+def final_ffn(at, gu4, gu_x, gu_c, do4, do_x, do_c, half, ff, width):
+    f32 = lambda *s: jax.ShapeDtypeStruct(s, F32)
+    return pl.pallas_call(
+        final_kernel,
+        in_specs=[pl.BlockSpec(memory_space=pltpu.SMEM)] + [pl.BlockSpec(memory_space=pltpu.VMEM)] * 6,
+        out_specs=[pl.BlockSpec(memory_space=pltpu.VMEM)] * 4,
+        out_shape=[f32(half, ff), f32(half, ff), f32(ff // 2, width), f32(half, width)],
+        compiler_params=pltpu.CompilerParams(vmem_limit_bytes=LIMIT),
+        cost_estimate=pl.CostEstimate(flops=int(5e9), bytes_accessed=int(10e6), transcendentals=0),
+    )(at, gu4, gu_x, gu_c, do4, do_x, do_c)
+
+
+def final_t_kernel(at_ref, t4, t_x, t_c, q_ref, k_ref, v_ref, g_ref, whole):
+    core, xb, z = at_ref[0], at_ref[1], at_ref[2]
+    deep, wide = t4.shape[1:]
+    for f in range(2):
+        for e in range(2):
+            for d in range(4):
+                t = (t4[d] if e == 0 else t_x[d]) if f == 0 else t_c[e * 4 + d]
+                rs = pl.ds(pl.multiple_of((xb ^ e) * deep, 16), deep)
+                cs = pl.ds(pl.multiple_of((core ^ f) * 512 + (z ^ d) * wide, 128), wide)
+                whole[rs, cs] = t.astype(F32)
+    a = q_ref.shape[1]
+    b = a + k_ref.shape[1]
+    c = b + v_ref.shape[1]
+    q_ref[...] = whole[:, :a]
+    k_ref[...] = whole[:, a:b]
+    v_ref[...] = whole[:, b:c]
+    g_ref[...] = whole[:, c:].T[:8]
+
+
+def final_t(at, t4, t_x, t_c, half, width, kv_width):
+    f32 = lambda *s: jax.ShapeDtypeStruct(s, F32)
+    return pl.pallas_call(
+        final_t_kernel,
+        in_specs=[pl.BlockSpec(memory_space=pltpu.SMEM)] + [pl.BlockSpec(memory_space=pltpu.VMEM)] * 3,
+        out_specs=[pl.BlockSpec(memory_space=pltpu.VMEM)] * 4,
+        out_shape=[f32(half, width), f32(half, kv_width), f32(half, kv_width), f32(8, half)],
+        scratch_shapes=[pltpu.VMEM((half, 1024), F32)],
+        compiler_params=pltpu.CompilerParams(vmem_limit_bytes=LIMIT),
+        cost_estimate=pl.CostEstimate(flops=int(1e9), bytes_accessed=int(2e6), transcendentals=0),
+    )(at, t4, t_x, t_c)
+
+
 def swap(x, axis, bit):
     n = lax.axis_size(axis)
     return lax.ppermute(x, axis, [(i, i ^ (1 << bit)) for i in range(n)])
@@ -490,22 +562,20 @@
     return lax.axis_size("fsdp") == 2 and lax.axis_size("ctx") == 16
 
 
-def z_groups():
-    return [[4 * z + r for z in range(4)] for r in range(4)]
+def z_swap(x, by):
+    return lax.ppermute(x, "ctx", [(i, i ^ (4 * by)) for i in range(16)])
 
 
 def z_sum(x):
-    x = lax.all_to_all(x, "ctx", 0, 0, tiled=True, axis_index_groups=z_groups())
-    return jnp.sum(x.astype(F32), axis=0).astype(BF)
+    z = lax.axis_index("ctx") >> 2
+    total = pick(x, z).astype(F32)
+    for by in range(1, 4):
+        total = total + z_swap(pick(x, z ^ by), by).astype(F32)
+    return total.astype(BF)
 
 
 def z_join(piece):
-    whole = jnp.broadcast_to(piece[None], (4,) + piece.shape)
-    return lax.all_to_all(whole, "ctx", 0, 0, tiled=True, axis_index_groups=z_groups())
-
-
-def join(x, bit):
-    return swap(x, "ctx", bit)
+    return jnp.stack([piece] + [z_swap(piece, by) for by in range(1, 4)])
 
 
 def natural_gu(pieces):
@@ -552,9 +622,7 @@
         gains = in_order(rank, first[own : own + 2, :own], other[own : own + 2, :own], 1).astype(F32)
         first = in_order(rank, first[:own], other[:own], 0)
         gate_half, up_half, down_half, got = pin(halved(w_gate, 1), halved(w_up, 1), halved(w_down, 0), got)
-        gate_w = in_order(rank, w_gate, other_shard(swap(gate_half, "fsdp", 0), 1), 0)
-        up_w = in_order(rank, w_up, other_shard(swap(up_half, "fsdp", 0), 1), 0)
-        down_w = in_order(rank, w_down, other_shard(swap(down_half, "fsdp", 0), 0), 0)
+        gate_got, up_got, down_got = (swap(h, "fsdp", 0) for h in (gate_half, up_half, down_half))
     else:
         first = lax.all_gather(first, "fsdp", axis=0)
         gains = first[:, own : own + 2, :own].transpose(1, 0, 2).reshape(2, width).astype(F32)
@@ -579,10 +647,16 @@
     x, cot_send = pin(x, cotangent)
     cot = move(cot_send)
     query, kv_own = project_qkv(x, first, gains, cosine, sine)
+    if fast:
+        kv_own, gate_got, up_got, down_got = pin(kv_own, gate_got, up_got, down_got)
+        gate_w = in_order(rank, w_gate, other_shard(gate_got, 1), 0)
+        up_w = in_order(rank, w_up, other_shard(up_got, 1), 0)
+        down_w = in_order(rank, w_down, other_shard(down_got, 0), 0)
     if team == 2:
-        kv_all = jnp.stack([kv_own, swap(kv_own, "ctx", 0)])
+        kv_all = (kv_own, swap(kv_own, "ctx", 0))
     else:
         kv_all = lax.all_gather(kv_own, "ctx", axis=0, axis_index_groups=groups)
+        kv_all = tuple(kv_all[s] for s in range(team))
     attended, log_total = attn_fwd(bias, query, kv_all)
     attended, cot = pin(attended, cot)
     mixed, d_res, d_att, row_dot, keep_gu, send_gu, keep_do, send_do, gain_sum = feed_forward(
@@ -591,20 +665,19 @@
     mixed_out = move(mixed)
 
     n = rows // BLOCK
-    spans = ((0, n // 2), (n - 1, n), (n // 2, n - 1))
+    spans = ((0, n - 1), (n - 1, n))
     part = functools.partial(attn_bwd, bias, query, kv_all, d_att, log_total, row_dot)
     if fast:
+        x_bit = bit_of("ctx", 1)
         got_gu, got_do = swap(send_gu, "ctx", 0), swap(send_do, "ctx", 0)
-        dq_a, before = part(*spans[0])
-        got_gu, got_do, before = pin(got_gu, got_do, before)
-        x_bit = bit_of("ctx", 1)
         gu, do = plus(keep_gu, got_gu), plus(keep_do, got_do)
         gu = gu.reshape((2, 2, 4) + gu.shape[2:]).swapaxes(0, 1)
         keep_gu, send_gu = pick(gu, x_bit), pick(gu, 1 - x_bit)
         keep_do, send_do = pick(do, rank), pick(do, 1 - rank)
-        send_gu, send_do, before = pin(send_gu, send_do, before)
+        send_gu, send_do, row_dot = pin(send_gu, send_do, row_dot)
+        part = functools.partial(attn_bwd, bias, query, kv_all, d_att, log_total, row_dot)
         got_gu, got_do = swap(send_gu, "ctx", 1), swap(send_do, "fsdp", 0)
-        dq_b, before = part(*spans[1], before=before)
+        dq_a, before = part(*spans[0])
         got_gu, got_do, mixed_out, before = pin(got_gu, got_do, mixed_out, before)
         gu, do = plus(keep_gu, got_gu), plus(keep_do, got_do)
         do = do.reshape((2, 4) + do.shape[1:])
@@ -612,20 +685,19 @@
         keep_do, send_do = pick(do, x_bit), pick(do, 1 - x_bit)
         send_gu, send_do, before = pin(send_gu, send_do, before)
         got_gu, got_do = swap(send_gu, "fsdp", 0), swap(send_do, "ctx", 1)
-        dq_c, d_kv, d_kv_low = part(*spans[2], before=before, last=True)
-        got_gu, got_do, d_kv_low, dq_c = pin(got_gu, got_do, d_kv_low, dq_c)
+        dq_b, d_kv, d_kv_low = part(*spans[1], before=before, last=True)
+        got_gu, got_do, d_kv_low, dq_b = pin(got_gu, got_do, d_kv_low, dq_b)
         gu, do = plus(keep_gu, got_gu), plus(keep_do, got_do)
     else:
         dq_a, before = part(*spans[0])
-        dq_b, before = part(*spans[1], before=before)
-        dq_c, d_kv, d_kv_low = part(*spans[2], before=before, last=True)
+        dq_b, d_kv, d_kv_low = part(*spans[1], before=before, last=True)
     if team == 2:
         own_kv, got_kv = d_kv[:1], swap(d_kv_low[1], "ctx", 0)
     else:
         own_kv = lax.psum_scatter(d_kv_low, "ctx", scatter_dimension=0, axis_index_groups=groups)
         own_kv, got_kv = own_kv.astype(F32)[None], jnp.zeros((2 * kv_width, rows), BF)
     d_x, keep_t, send_t = back_qkv(
-        flags, spans, (dq_a, dq_b, dq_c), own_kv, got_kv, x, d_res, first, gains, cosine, sine, gain_sum
+        flags, spans, (dq_a, dq_b), own_kv, got_kv, x, d_res, first, gains, cosine, sine, gain_sum
     )
     grad_tokens = move(d_x)
     if fast:
@@ -638,20 +710,12 @@
 
         def widen(piece):
             four = z_join(piece)
-            eight = in_order(x_bit, four, join(four, 1), 0)
-            return eight, join(eight, 0)
-
-        gu, gu_other = widen(gu)
-        do, do_other = widen(do)
-        t, t_other = widen(t)
-        own_gate = natural_gu(jnp.where(core == 0, gu, gu_other))
-        own_up = natural_gu(jnp.where(core == 0, gu_other, gu))
-        do = in_order(core, do, do_other, 0)
-        deep = ff // 32
-        own_down = do[:, :deep].reshape(ff // 2, width).astype(F32)
-        own_out = do[:, deep : deep + width // 32].reshape(width // 2, width).astype(F32)
-        t0, t1 = jnp.where(core == 0, t, t_other), jnp.where(core == 0, t_other, t)
-        own_t = jnp.concatenate([natural_gu(t0), natural_gu(t1)], axis=1)
+            across = swap(four, "ctx", 1)
+            return four, across, swap(jnp.concatenate([four, across], axis=0), "ctx", 0)
+
+        at = jnp.stack([core, x_bit, lax.axis_index("ctx") >> 2])
+        own_gate, own_up, own_down, own_out = final_ffn(at, *widen(gu), *widen(do), width // 2, ff, width)
+        own_query, own_key, own_value, own_gains = final_t(at, *widen(t), width // 2, width, kv_width)
     else:
         pair = jnp.stack([keep_gu, send_gu])
         gate, up = (jnp.concatenate([natural_gu(pair[c, y]) for y in range(2)], axis=0) for c in range(2))
@@ -659,19 +723,22 @@
         deep = ff // 32
         own_gate, own_up = other_sum(gate), other_sum(up)
         own_down = other_sum(do[:, :deep].reshape(ff, width))
-        own_out = other_sum(do[:, deep : deep + width // 32].reshape(width, width))
+        out = do[:, deep:].reshape((2, -1, width))[:, : width // 2]
+        own_out = other_sum(out.reshape(width, width))
         pair = jnp.stack([keep_t, send_t])
         t = [jnp.concatenate([natural_gu(pair[c, y]) for c in range(2)], axis=1) for y in range(2)]
         own_t = other_sum(jnp.concatenate(t, axis=0))
+        own_query, own_key = own_t[:, :width], own_t[:, width : width + kv_width]
+        own_value, own_gains = own_t[:, width + kv_width : qkv_cols], own_t[:, qkv_cols:].T
     return (
         mixed_out.reshape(tokens.shape),
         grad_tokens.reshape(tokens.shape),
-        own_t[:, qkv_cols],
-        own_t[:, :width],
-        own_t[:, width : width + kv_width],
-        own_t[:, width + kv_width : qkv_cols],
+        own_gains[0],
+        own_query,
+        own_key,
+        own_value,
         own_out,
-        own_t[:, qkv_cols + 1],
+        own_gains[1],
         own_gate,
         own_up,
         own_down,

time: 375 us -> 358 us (0.955)
  the two profiles are of different devices: /device:TPU:15 before, /device:TPU:1 now
where the time goes in v3:
time: 358 us; the launch traced here: 353 us
  Pallas kernels  132 us (37%)
  starting transfers between devices  81.9 us (23%)
  waiting for transfers between devices  79.5 us (22%)
  local copies, waits for them, and re-layouts  30.6 us (9%)
  other arithmetic  27.1 us (8%)
    pallas_call x1, Pallas kernels, feed_forward(): pl.pallas_call(ffn_kernel, grid=(rows // BLOCK,), in_specs=[pl.BlockSpec(...  41.1 us
    pallas_call x2, Pallas kernels, attn_bwd(): pl.pallas_call(functools.partial(bwd_kernel, kvs=kvs, group=group, slots=...  40.9 us
    ppermute x25, waiting for transfers between devices, swap(): return lax.ppermute(x, axis, [(i, i ^ 1 << bit) for i in range(n)])  40.6 us
    ppermute x18, waiting for transfers between devices, z_swap(): return lax.ppermute(x, 'ctx', [(i, i ^ 4 * by) for i in range(16)])  36.5 us
    ppermute x25, starting transfers between devices, swap(): return lax.ppermute(x, axis, [(i, i ^ 1 << bit) for i in range(n)])  32.2 us
    all_to_all x4, starting transfers between devices, move(): return lax.all_to_all(x.reshape(count, sub, width), 'ctx', 0, 0, tiled=True)  26.3 us
    pallas_call x1, Pallas kernels, attn_fwd(): pl.pallas_call(functools.partial(fwd_kernel, kvs=kvs, group=group, slots=...  26 us
    ppermute x18, starting transfers between devices, z_swap(): return lax.ppermute(x, 'ctx', [(i, i ^ 4 * by) for i in range(16)])  23.5 us
  transfers between devices with their start and end apart: 47, of which 12 were waited for; matrix products, arithmetic and copies ran while one was open for 12% of the time, Pallas kernels for 26%

profile of v3, /device:TPU:1, one launch (start us, length us, event | category | flops | bytes accessed | tf_op | source)
XLA Modules:
  0.0 353.1 jit_solution(3286527511310946908)
XLA Ops:
  0.6 2.4 copy.30
  3.1 7.5 %all-to-all-start = ((bf16[16,64,576]{2,1,0:T(8,128)(2,1)}), bf16[16,64,576]{2,1,0:T(8,128)(2,1)}, u32[]{:S(2)}, u32[]{:S(2)}) async-start(bf16[16,64,576]{2,1,0:T(8,128)(2,1)} %bitcast.4), calls=%async_computation | async-start | bytes 2621440 | tf_op jit(solution)/shard_map/all_to_all | solution.py:605
  15.2 9.2 %collective-permute-done = bf16[296,768]{1,0:T(8,128)(2,1)} collective-permute-done((bf16[296,768]{1,0:T(8,128)(2,1)}, bf16[296,768]{1,0:T(8,128)(2,1)}, u32[]{:S(2)}, u32[]{:S(2)}) %collective-permute-start) | collective-permute-done | bytes 454688 | tf_op jit(solution)/shard_map/ppermute | solution.py:534
  38.4 6.0 %shard_map.194 = (bf16[576,1024]{1,0:T(8,128)(2,1)}, bf16[384,1024]{1,0:T(8,128)(2,1)}) custom-call(bf16[16,64,576]{2,1,0:T(8,128)(2,1)} %all-to-all-done.x_ref.refs_5_, bf16[576,1536]{1,0:T(8,128)(2,1)} %maximum_select_fusion.1.w_ref.first_ref.refs_7_, f32[8,576]{1,0:T(8,128)} %pad_convert_fusion.gain_ref.refs_8_, ...), custom_call_target="tpu_custom_call" | custom-call | flops 6000000000 | bytes 5000000 | tf_op jit(solution)/shard_map/pallas_call | solution.py:230
  44.5 7.3 %collective-permute-done.2 = bf16[288,768]{1,0:T(8,128)(2,1)} collective-permute-done((bf16[288,768]{1,0:T(8,128)(2,1)}, bf16[288,768]{1,0:T(8,128)(2,1)}, u32[]{:S(2)}, u32[]{:S(2)}) %collective-permute-start.2) | collective-permute-done | bytes 442400 | tf_op jit(solution)/shard_map/ppermute | solution.py:534
  51.7 9.5 %collective-permute-done.3 = bf16[288,768]{1,0:T(8,128)(2,1)} collective-permute-done((bf16[288,768]{1,0:T(8,128)(2,1)}, bf16[288,768]{1,0:T(8,128)(2,1)}, u32[]{:S(2)}, u32[]{:S(2)}) %collective-permute-start.3) | collective-permute-done | bytes 442400 | tf_op jit(solution)/shard_map/ppermute | solution.py:534
  64.9 6.8 %all-to-all-start.1 = ((bf16[16,64,576]{2,1,0:T(8,128)(2,1)}), bf16[16,64,576]{2,1,0:T(8,128)(2,1)S(1)}, u32[]{:S(2)}, u32[]{:S(2)}) async-start(bf16[16,64,576]{2,1,0:T(8,128)(2,1)} %bitcast.5), calls=%async_computation.1 | async-start | bytes 2621440 | tf_op jit(solution)/shard_map/all_to_all | solution.py:605
  82.7 26.0 %shard_map.195 = (f32[576,1024]{1,0:T(8,128)}, f32[16,1024]{1,0:T(8,128)}) custom-call(f32[2,256,256]{2,1,0:T(8,128)} %compare_select_fusion.bias_ref.refs_0_, bf16[576,1024]{1,0:T(8,128)(2,1)} %get-tuple-element.90.q_ref.refs_1_, bf16[384,1024]{1,0:T(8,128)(2,1)} %get-tuple-element.95.refs_0_.refs_5_, bf16[384,1024]{1,0:T(8,128)(2,1)} %collective-permute-done.5.refs_1_.refs_6_), custom_call_target="tpu_custom_call" | custom-call | flops 24999999488 | bytes 8000000 | tf_op jit(solution)/shard_map/pallas_call | solution.py:74
  109.8 41.1 %shard_map.196 = (bf16[16,64,576]{2,1,0:T(8,128)(2,1)}, f32[1024,576]{1,0:T(8,128)}, bf16[576,1024]{1,0:T(8,128)(2,1)}, f32[16,1024]{1,0:T(8,128)}, bf16[2,8,144...) custom-call(s32[2]{0:T(128)} %pad_add_fusion.place_ref.refs_0_, ...), custom_call_target="tpu_custom_call" | custom-call | flops 32000000000 | bytes 20000000 | tf_op jit(solution)/shard_map/pallas_call | solution.py:334
  152.2 6.4 %all-to-all-start.2 = ((bf16[16,64,576]{2,1,0:T(8,128)(2,1)}), bf16[16,64,576]{2,1,0:T(8,128)(2,1)}, u32[]{:S(2)}, u32[]{:S(2)}) async-start(bf16[16,64,576]{2,1,0:T(8,128)(2,1)} %get-tuple-element.110), calls=%async_computation.2 | async-start | bytes 2621440 | tf_op jit(solution)/shard_map/all_to_all | solution.py:605
  168.6 22.7 %shard_map.197 = (f32[576,768]{1,0:T(8,128)}, f32[2,384,1024]{2,1,0:T(8,128)}) custom-call(f32[2,256,256]{2,1,0:T(8,128)} %compare_select_fusion.bias_ref.refs_0_, bf16[576,1024]{1,0:T(8,128)(2,1)} %get-tuple-element.90.q_ref.refs_1_, bf16[576,1024]{1,0:T(8,128)(2,1)} %get-tuple-element.111.refs_2_, f32[16,1024]{1,0:T(8,128)} %get-tuple-element.112.refs_3_, ...), custom_call_target="tpu_custom_call" | custom-call | flops 24000000000 | bytes 16000000 | tf_op jit(solution)/shard_map/pallas_call | solution.py:169
  191.3 3.8 %collective-permute-done.11 = bf16[2,4,144,384]{3,2,1,0:T(8,128)(2,1)} collective-permute-done((bf16[2,4,144,384]{3,2,1,0:T(8,128)(2,1)}, bf16[2,4,144,384]{3,2,1,0:T(8,128)(2,1)}, u32[]{:S(2)}, u32[]{:S(2)}) %collective-permute-start.11) | collective-permute-done | bytes 884768 | tf_op jit(solution)/shard_map/ppermute | solution.py:534
  201.9 18.2 %shard_map.198 = (f32[576,256]{1,0:T(8,128)}, f32[2,384,1024]{2,1,0:T(8,128)}, bf16[2,384,1024]{2,1,0:T(8,128)(2,1)}) custom-call(f32[2,256,256]{2,1,0:T(8,128)} %compare_select_fusion.bias_ref.refs_0_, bf16[576,1024]{1,0:T(8,128)(2,1)} %get-tuple-element.90.q_ref.refs_1_, bf16[576,1024]{1,0:T(8,128)(2,1)} %get-tuple-element.111.refs_2_, ...), custom_call_target="tpu_custom_call" | custom-call | flops 16000000000 | bytes 16000000 | tf_op jit(solution)/shard_map/pallas_call | solution.py:169
  220.1 2.8 slice.59.refs_3_
  222.9 2.5 copy.36
  232.0 2.8 collective-permute-start.28
  237.2 2.8 collective-permute-done.27
  240.0 3.3 collective-permute-done.28
  244.6 3.6 %collective-permute-start.30 = (bf16[144,384]{1,0:T(8,128)(2,1)S(1)}, bf16[144,384]{1,0:T(8,128)(2,1)S(1)}, u32[]{:S(2)}, u32[]{:S(2)}) collective-permute-start(bf16[144,384]{1,0:T(8,128)(2,1)S(1)} %get-tuple-element.170), channel_id=1, source_target_pairs={{0,4},{1,5},{2,6},{3,7},{4,0},{5,1},{6,2},{7,3},{8,12},{9,13},{10,... | collective-permute-start | bytes 331784 | tf_op jit(solution)/shard_map/ppermute | solution.py:566
  249.0 2.4 collective-permute-done.39
  254.1 10.6 %shard_map.199 = (bf16[16,64,576]{2,1,0:T(8,128)(2,1)}, bf16[2,8,144,128]{3,2,1,0:T(8,128)(2,1)}, bf16[2,8,144,128]{3,2,1,0:T(8,128)(2,1)}) custom-call(s32[2]{0:T(128)} %pad_add_fusion.place_ref.refs_0_, f32[576,768]{1,0:T(8,128)} %get-tuple-element.116.refs_1_, f32[576,256]{1,0:T(8,128)} %get-tuple-element.125.refs_2_, f32[1,384,1024]{2,1,0:T(8,128)} %slice.59.refs_3_, ...), custom_call_target="tpu_custom_call" | custom-call | flops 10000000000 | bytes 10000000 | tf_op jit(solution)/shard_map/pallas_call | solution.py:433
  264.6 7.0 %collective-permute-start.16 = (bf16[2,8,144,128]{3,2,1,0:T(8,128)(2,1)}, bf16[2,8,144,128]{3,2,1,0:T(8,128)(2,1)S(1)}, u32[]{:S(2)}, u32[]{:S(2)}) collective-permute-start(bf16[2,8,144,128]{3,2,1,0:T(8,128)(2,1)} %get-tuple-element.132), channel_id=1, source_target_pairs={{0,1},{1,0},{2,3},{3,2},{4,5},{5,4},{6,7},{7,6},{8,9},{9,8},{10,11... | collective-permute-start | bytes 1769480 | tf_op jit(solution)/shard_map/ppermute | solution.py:534
  274.9 8.0 %collective-permute-done.17 = bf16[8,144,128]{2,1,0:T(8,128)(2,1)S(1)} collective-permute-done((bf16[8,144,128]{2,1,0:T(8,128)(2,1)S(1)}, bf16[8,144,128]{2,1,0:T(8,128)(2,1)S(1)}, u32[]{:S(2)}, u32[]{:S(2)}) %collective-permute-start.17) | collective-permute-done | bytes 294944 | tf_op jit(solution)/shard_map/ppermute | solution.py:534
  284.7 5.6 %all-to-all-start.3 = ((bf16[16,64,576]{2,1,0:T(8,128)(2,1)}), bf16[16,64,576]{2,1,0:T(8,128)(2,1)S(1)}, u32[]{:S(2)}, u32[]{:S(2)}) async-start(bf16[16,64,576]{2,1,0:T(8,128)(2,1)} %get-tuple-element.130), calls=%async_computation.3 | async-start | bytes 2621440 | tf_op jit(solution)/shard_map/all_to_all | solution.py:605
  295.8 17.1 %collective-permute-done.19 = bf16[144,128]{1,0:T(8,128)(2,1)S(1)} collective-permute-done((bf16[144,128]{1,0:T(8,128)(2,1)S(1)}, bf16[144,128]{1,0:T(8,128)(2,1)S(1)}, u32[]{:S(2)}, u32[]{:S(2)}) %collective-permute-start.19) | collective-permute-done | bytes 36896 | tf_op jit(solution)/shard_map/ppermute | solution.py:566
  312.9 11.0 %collective-permute-done.20 = bf16[144,128]{1,0:T(8,128)(2,1)S(1)} collective-permute-done((bf16[144,128]{1,0:T(8,128)(2,1)S(1)}, bf16[144,128]{1,0:T(8,128)(2,1)S(1)}, u32[]{:S(2)}, u32[]{:S(2)}) %collective-permute-start.20) | collective-permute-done | bytes 36896 | tf_op jit(solution)/shard_map/ppermute | solution.py:566
  328.4 2.4 collective-permute-start.34
  332.2 2.7 collective-permute-done.25.t_x
  334.9 3.7 %collective-permute-start.26 = (bf16[8,144,128]{2,1,0:T(8,128)(2,1)S(1)}, bf16[8,144,128]{2,1,0:T(8,128)(2,1)S(1)}, u32[]{:S(2)}, u32[]{:S(2)}) collective-permute-start(bf16[8,144,128]{2,1,0:T(8,128)(2,1)S(1)} %constant_dynamic-update-slice_fusion), channel_id=1, source_target_pairs={{0,1},{1,0},{2,3},{3,2},{4,5},{5,4},{6,7},{7,6},{8,9},{9,8},{10,11... | collective-permute-start | bytes 884744 | tf_op jit(solution)/shard_map/ppermute | solution.py:534
  338.6 5.2 %shard_map.201 = (f32[288,1536]{1,0:T(8,128)}, f32[288,1536]{1,0:T(8,128)}, f32[768,576]{1,0:T(8,128)}, f32[288,576]{1,0:T(8,128)}) custom-call(s32[3]{0:T(128)} %pad_add_fusion.1.at_ref, bf16[4,144,384]{2,1,0:T(8,128)(2,1)} %copy-done.9, bf16[4,144,384]{2,1,0:T(8,128)(2,1)} %copy-done.10, bf16[8,144,384]{2,1,0:T(8,128)(2,1)} %collective-permute-done.34.gu_c, ...), custom_call_target="tpu_custom_call" | custom-call | flops 5000000000 | bytes 10000000 | tf_op jit(solution)/shard_map/pallas_call | solution.py:490
  343.9 2.8 copy.38
  347.3 2.4 shard_map.200
  (198 shorter events, 85.9 us)
Async XLA Ops:
  3.1 35.3 %all-to-all-start = ((bf16[16,64,576]{2,1,0:T(8,128)(2,1)}), bf16[16,64,576]{2,1,0:T(8,128)(2,1)}, u32[]{:S(2)}, u32[]{:S(2)}) async-start(bf16[16,64,576]{2,1,0:T(8,128)(2,1)} %bitcast.4), calls=%async_computation | async-start | bytes 2621440 | tf_op jit(solution)/shard_map/all_to_all | solution.py:605
  12.3 12.2 %collective-permute-start = (bf16[296,768]{1,0:T(8,128)(2,1)}, bf16[296,768]{1,0:T(8,128)(2,1)}, u32[]{:S(2)}, u32[]{:S(2)}) collective-permute-start(bf16[296,768]{1,0:T(8,128)(2,1)} %fusion.5), channel_id=1, source_target_pairs={{0,16},{16,0},{1,17},{17,1},{2,18},{18,2},{3,19},{19,3},{4,20},{20... | collective-permute-start | bytes 1363976 | tf_op jit(solution)/shard_map/ppermute | solution.py:534
  29.3 15.2 %collective-permute-start.4 = (bf16[384,576]{1,0:T(8,128)(2,1)S(1)}, bf16[384,576]{1,0:T(8,128)(2,1)}, u32[]{:S(2)}, u32[]{:S(2)}) collective-permute-start(bf16[384,576]{1,0:T(8,128)(2,1)S(1)} %constant_dynamic-slice_fusion), channel_id=1, source_target_pairs={{0,16},{16,0},{1,17},{17,1},{2,18},{18,2},{3,19},{19,3},{4,20},{20... | collective-permute-start | bytes 1327112 | tf_op jit(solution)/shard_map/ppermute | solution.py:534
  30.5 21.2 %collective-permute-start.2 = (bf16[288,768]{1,0:T(8,128)(2,1)}, bf16[288,768]{1,0:T(8,128)(2,1)}, u32[]{:S(2)}, u32[]{:S(2)}) collective-permute-start(bf16[288,768]{1,0:T(8,128)(2,1)} %get-tuple-element.92), channel_id=1, source_target_pairs={{0,16},{16,0},{1,17},{17,1},{2,18},{18,2},{3,19},{19,3},{4,20},{20... | collective-permute-start | bytes 1327112 | tf_op jit(solution)/shard_map/ppermute | solution.py:534
  30.7 30.5 %collective-permute-start.3 = (bf16[288,768]{1,0:T(8,128)(2,1)}, bf16[288,768]{1,0:T(8,128)(2,1)}, u32[]{:S(2)}, u32[]{:S(2)}) collective-permute-start(bf16[288,768]{1,0:T(8,128)(2,1)} %get-tuple-element.93), channel_id=1, source_target_pairs={{0,16},{16,0},{1,17},{17,1},{2,18},{18,2},{3,19},{19,3},{4,20},{20... | collective-permute-start | bytes 1327112 | tf_op jit(solution)/shard_map/ppermute | solution.py:534
  61.2 10.5 %collective-permute-start.7 = (bf16[288,768]{1,0:T(8,128)(2,1)}, bf16[288,768]{1,0:T(8,128)(2,1)}, u32[]{:S(2)}, u32[]{:S(2)}) collective-permute-start(bf16[288,768]{1,0:T(8,128)(2,1)} %collective-permute-done.3), channel_id=1, source_target_pairs={{0,1},{1,0},{2,3},{3,2},{4,5},{5,4},{6,7},{7,6},{8,9},{9,8},{10,11... | collective-permute-start | bytes 1327112 | tf_op jit(solution)/shard_map/ppermute | solution.py:534
  62.0 11.3 %collective-permute-start.8 = (bf16[384,576]{1,0:T(8,128)(2,1)}, bf16[384,576]{1,0:T(8,128)(2,1)}, u32[]{:S(2)}, u32[]{:S(2)}) collective-permute-start(bf16[384,576]{1,0:T(8,128)(2,1)} %collective-permute-done.4), channel_id=1, source_target_pairs={{0,1},{1,0},{2,3},{3,2},{4,5},{5,4},{6,7},{7,6},{8,9},{9,8},{10,11... | collective-permute-start | bytes 1327112 | tf_op jit(solution)/shard_map/ppermute | solution.py:534
  63.0 14.0 %collective-permute-start.6 = (bf16[288,768]{1,0:T(8,128)(2,1)}, bf16[288,768]{1,0:T(8,128)(2,1)}, u32[]{:S(2)}, u32[]{:S(2)}) collective-permute-start(bf16[288,768]{1,0:T(8,128)(2,1)} %collective-permute-done.2), channel_id=1, source_target_pairs={{0,1},{1,0},{2,3},{3,2},{4,5},{5,4},{6,7},{7,6},{8,9},{9,8},{10,11... | collective-permute-start | bytes 1327112 | tf_op jit(solution)/shard_map/ppermute | solution.py:534
  63.5 19.2 %collective-permute-start.5 = (bf16[384,1024]{1,0:T(8,128)(2,1)}, bf16[384,1024]{1,0:T(8,128)(2,1)}, u32[]{:S(2)}, u32[]{:S(2)}) collective-permute-start(bf16[384,1024]{1,0:T(8,128)(2,1)} %get-tuple-element.95.refs_0_.refs_5_), channel_id=1, source_target_pairs={{0,1},{1,0},{2,3},{3,2},{4,5},{5,4},{6,7},{7,6},{8,9},{9,8},{10,11... | collective-permute-start | bytes 2359304 | tf_op jit(solution)/shard_map/ppermute | solution.py:534
  64.9 43.8 %all-to-all-start.1 = ((bf16[16,64,576]{2,1,0:T(8,128)(2,1)}), bf16[16,64,576]{2,1,0:T(8,128)(2,1)S(1)}, u32[]{:S(2)}, u32[]{:S(2)}) async-start(bf16[16,64,576]{2,1,0:T(8,128)(2,1)} %bitcast.5), calls=%async_computation.1 | async-start | bytes 2621440 | tf_op jit(solution)/shard_map/all_to_all | solution.py:605
  151.1 10.7 %collective-permute-start.9 = (bf16[2,8,144,384]{3,2,1,0:T(8,128)(2,1)}, bf16[2,8,144,384]{3,2,1,0:T(8,128)(2,1)S(1)}, u32[]{:S(2)}, u32[]{:S(2)}) collective-permute-start(bf16[2,8,144,384]{3,2,1,0:T(8,128)(2,1)} %get-tuple-element.104), channel_id=1, source_target_pairs={{0,1},{1,0},{2,3},{3,2},{4,5},{5,4},{6,7},{7,6},{8,9},{9,8},{10,11... | collective-permute-start | bytes 5308424 | tf_op jit(solution)/shard_map/ppermute | solution.py:534
  152.2 39.2 %all-to-all-start.2 = ((bf16[16,64,576]{2,1,0:T(8,128)(2,1)}), bf16[16,64,576]{2,1,0:T(8,128)(2,1)}, u32[]{:S(2)}, u32[]{:S(2)}) async-start(bf16[16,64,576]{2,1,0:T(8,128)(2,1)} %get-tuple-element.110), calls=%async_computation.2 | async-start | bytes 2621440 | tf_op jit(solution)/shard_map/all_to_all | solution.py:605
  166.0 29.2 %collective-permute-start.11 = (bf16[2,4,144,384]{3,2,1,0:T(8,128)(2,1)}, bf16[2,4,144,384]{3,2,1,0:T(8,128)(2,1)}, u32[]{:S(2)}, u32[]{:S(2)}) collective-permute-start(bf16[2,4,144,384]{3,2,1,0:T(8,128)(2,1)} %dynamic-slice_bitcast_fusion), channel_id=1, source_target_pairs={{0,2},{1,3},{2,0},{3,1},{4,6},{5,7},{6,4},{7,5},{8,10},{9,11},{10,... | collective-permute-start | bytes 2654216 | tf_op jit(solution)/shard_map/ppermute | solution.py:534
  167.4 24.0 %collective-permute-start.12 = (bf16[8,72,576]{2,1,0:T(8,128)(2,1)}, bf16[8,72,576]{2,1,0:T(8,128)(2,1)}, u32[]{:S(2)}, u32[]{:S(2)}) collective-permute-start(bf16[8,72,576]{2,1,0:T(8,128)(2,1)} %dynamic-slice_bitcast_fusion.1), channel_id=1, source_target_pairs={{0,16},{16,0},{1,17},{17,1},{2,18},{18,2},{3,19},{19,3},{4,20},{20... | collective-permute-start | bytes 1990664 | tf_op jit(solution)/shard_map/ppermute | solution.py:534
  199.6 25.8 %collective-permute-start.13 = (bf16[4,144,384]{2,1,0:T(8,128)(2,1)S(1)}, bf16[4,144,384]{2,1,0:T(8,128)(2,1)S(1)}, u32[]{:S(2)}, u32[]{:S(2)}) collective-permute-start(bf16[4,144,384]{2,1,0:T(8,128)(2,1)S(1)} %dynamic-slice_bitcast_fusion.2), channel_id=1, source_target_pairs={{0,16},{16,0},{1,17},{17,1},{2,18},{18,2},{3,19},{19,3},{4,20},{20... | collective-permute-start | bytes 1327112 | tf_op jit(solution)/shard_map/ppermute | solution.py:534
  200.9 24.5 %collective-permute-start.14 = (bf16[4,72,576]{2,1,0:T(8,128)(2,1)}, bf16[4,72,576]{2,1,0:T(8,128)(2,1)S(1)}, u32[]{:S(2)}, u32[]{:S(2)}) collective-permute-start(bf16[4,72,576]{2,1,0:T(8,128)(2,1)} %dynamic-slice_bitcast_fusion.3), channel_id=1, source_target_pairs={{0,2},{1,3},{2,0},{3,1},{4,6},{5,7},{6,4},{7,5},{8,10},{9,11},{10,... | collective-permute-start | bytes 995336 | tf_op jit(solution)/shard_map/ppermute | solution.py:534
  229.2 24.0 %collective-permute-start.15 = (bf16[384,1024]{1,0:T(8,128)(2,1)S(1)}, bf16[384,1024]{1,0:T(8,128)(2,1)S(1)}, u32[]{:S(2)}, u32[]{:S(2)}) collective-permute-start(bf16[384,1024]{1,0:T(8,128)(2,1)S(1)} %slice_bitcast_fusion), channel_id=1, source_target_pairs={{0,1},{1,0},{2,3},{3,2},{4,5},{5,4},{6,7},{7,6},{8,9},{9,8},{10,11... | collective-permute-start | bytes 2359304 | tf_op jit(solution)/shard_map/ppermute | solution.py:534
  232.0 11.3 %collective-permute-start.28 = (bf16[144,384]{1,0:T(8,128)(2,1)S(1)}, bf16[144,384]{1,0:T(8,128)(2,1)S(1)}, u32[]{:S(2)}, u32[]{:S(2)}) collective-permute-start(bf16[144,384]{1,0:T(8,128)(2,1)S(1)} %get-tuple-element.175), channel_id=1, source_target_pairs={{0,8},{1,9},{2,10},{3,11},{4,12},{5,13},{6,14},{7,15},{8,0},{9,1},... | collective-permute-start | bytes 331784 | tf_op jit(solution)/shard_map/ppermute | solution.py:566
  235.4 12.8 %collective-permute-start.38 = (bf16[72,576]{1,0:T(8,128)(2,1)S(1)}, bf16[72,576]{1,0:T(8,128)(2,1)S(1)}, u32[]{:S(2)}, u32[]{:S(2)}) collective-permute-start(bf16[72,576]{1,0:T(8,128)(2,1)S(1)} %get-tuple-element.168), channel_id=1, source_target_pairs={{0,4},{1,5},{2,6},{3,7},{4,0},{5,1},{6,2},{7,3},{8,12},{9,13},{10,... | collective-permute-start | bytes 248840 | tf_op jit(solution)/shard_map/ppermute | solution.py:566
  240.0 11.4 %collective-permute-start.39 = (bf16[72,576]{1,0:T(8,128)(2,1)S(1)}, bf16[72,576]{1,0:T(8,128)(2,1)S(1)}, u32[]{:S(2)}, u32[]{:S(2)}) collective-permute-start(bf16[72,576]{1,0:T(8,128)(2,1)S(1)} %get-tuple-element.168), channel_id=1, source_target_pairs={{0,8},{1,9},{2,10},{3,11},{4,12},{5,13},{6,14},{7,15},{8,0},{9,1},... | collective-permute-start | bytes 248840 | tf_op jit(solution)/shard_map/ppermute | solution.py:566
  244.6 27.2 %collective-permute-start.30 = (bf16[144,384]{1,0:T(8,128)(2,1)S(1)}, bf16[144,384]{1,0:T(8,128)(2,1)S(1)}, u32[]{:S(2)}, u32[]{:S(2)}) collective-permute-start(bf16[144,384]{1,0:T(8,128)(2,1)S(1)} %get-tuple-element.170), channel_id=1, source_target_pairs={{0,4},{1,5},{2,6},{3,7},{4,0},{5,1},{6,2},{7,3},{8,12},{9,13},{10,... | collective-permute-start | bytes 331784 | tf_op jit(solution)/shard_map/ppermute | solution.py:566
  248.1 23.6 %collective-permute-start.31 = (bf16[144,384]{1,0:T(8,128)(2,1)S(1)}, bf16[144,384]{1,0:T(8,128)(2,1)S(1)}, u32[]{:S(2)}, u32[]{:S(2)}) collective-permute-start(bf16[144,384]{1,0:T(8,128)(2,1)S(1)} %get-tuple-element.170), channel_id=1, source_target_pairs={{0,8},{1,9},{2,10},{3,11},{4,12},{5,13},{6,14},{7,15},{8,0},{9,1},... | collective-permute-start | bytes 331784 | tf_op jit(solution)/shard_map/ppermute | solution.py:566
  251.4 20.4 %collective-permute-start.32 = (bf16[144,384]{1,0:T(8,128)(2,1)S(1)}, bf16[144,384]{1,0:T(8,128)(2,1)S(1)}, u32[]{:S(2)}, u32[]{:S(2)}) collective-permute-start(bf16[144,384]{1,0:T(8,128)(2,1)S(1)} %get-tuple-element.170), channel_id=1, source_target_pairs={{0,12},{1,13},{2,14},{3,15},{4,8},{5,9},{6,10},{7,11},{8,4},{9,5},... | collective-permute-start | bytes 331784 | tf_op jit(solution)/shard_map/ppermute | solution.py:566
  253.1 41.0 %collective-permute-start.41 = (bf16[4,72,576]{2,1,0:T(8,128)(2,1)S(1)}, bf16[4,72,576]{2,1,0:T(8,128)(2,1)S(1)}, u32[]{:S(2)}, u32[]{:S(2)}) collective-permute-start(bf16[4,72,576]{2,1,0:T(8,128)(2,1)S(1)} %pad_maximum_fusion.1.do4), channel_id=1, source_target_pairs={{0,2},{1,3},{2,0},{3,1},{4,6},{5,7},{6,4},{7,5},{8,10},{9,11},{10,... | collective-permute-start | bytes 995336 | tf_op jit(solution)/shard_map/ppermute | solution.py:534
  272.7 54.8 %collective-permute-start.33 = (bf16[4,144,384]{2,1,0:T(8,128)(2,1)S(1)}, bf16[4,144,384]{2,1,0:T(8,128)(2,1)S(1)}, u32[]{:S(2)}, u32[]{:S(2)}) collective-permute-start(bf16[4,144,384]{2,1,0:T(8,128)(2,1)S(1)} %pad_maximum_fusion.gu4), channel_id=1, source_target_pairs={{0,2},{1,3},{2,0},{3,1},{4,6},{5,7},{6,4},{7,5},{8,10},{9,11},{10,... | collective-permute-start | bytes 1327112 | tf_op jit(solution)/shard_map/ppermute | solution.py:534
  284.7 66.5 %all-to-all-start.3 = ((bf16[16,64,576]{2,1,0:T(8,128)(2,1)}), bf16[16,64,576]{2,1,0:T(8,128)(2,1)S(1)}, u32[]{:S(2)}, u32[]{:S(2)}) async-start(bf16[16,64,576]{2,1,0:T(8,128)(2,1)} %get-tuple-element.130), calls=%async_computation.3 | async-start | bytes 2621440 | tf_op jit(solution)/shard_map/all_to_all | solution.py:605
  290.4 22.5 %collective-permute-start.19 = (bf16[144,128]{1,0:T(8,128)(2,1)S(1)}, bf16[144,128]{1,0:T(8,128)(2,1)S(1)}, u32[]{:S(2)}, u32[]{:S(2)}) collective-permute-start(bf16[144,128]{1,0:T(8,128)(2,1)S(1)} %get-tuple-element.179), channel_id=1, source_target_pairs={{0,4},{1,5},{2,6},{3,7},{4,0},{5,1},{6,2},{7,3},{8,12},{9,13},{10,... | collective-permute-start | bytes 110600 | tf_op jit(solution)/shard_map/ppermute | solution.py:566
  291.9 32.0 %collective-permute-start.20 = (bf16[144,128]{1,0:T(8,128)(2,1)S(1)}, bf16[144,128]{1,0:T(8,128)(2,1)S(1)}, u32[]{:S(2)}, u32[]{:S(2)}) collective-permute-start(bf16[144,128]{1,0:T(8,128)(2,1)S(1)} %get-tuple-element.181), channel_id=1, source_target_pairs={{0,8},{1,9},{2,10},{3,11},{4,12},{5,13},{6,14},{7,15},{8,0},{9,1},... | collective-permute-start | bytes 110600 | tf_op jit(solution)/shard_map/ppermute | solution.py:566
  294.0 29.9 %collective-permute-start.21 = (bf16[144,128]{1,0:T(8,128)(2,1)S(1)}, bf16[144,128]{1,0:T(8,128)(2,1)S(1)}, u32[]{:S(2)}, u32[]{:S(2)}) collective-permute-start(bf16[144,128]{1,0:T(8,128)(2,1)S(1)} %get-tuple-element.180), channel_id=1, source_target_pairs={{0,12},{1,13},{2,14},{3,15},{4,8},{5,9},{6,10},{7,11},{8,4},{9,5},... | collective-permute-start | bytes 110600 | tf_op jit(solution)/shard_map/ppermute | solution.py:566
  294.9 43.7 %collective-permute-start.42 = (bf16[8,72,576]{2,1,0:T(8,128)(2,1)}, bf16[8,72,576]{2,1,0:T(8,128)(2,1)}, u32[]{:S(2)}, u32[]{:S(2)}) collective-permute-start(bf16[8,72,576]{2,1,0:T(8,128)(2,1)} %constant_dynamic-update-slice_fusion.10), channel_id=1, source_target_pairs={{0,1},{1,0},{2,3},{3,2},{4,5},{5,4},{6,7},{7,6},{8,9},{9,8},{10,11... | collective-permute-start | bytes 1990664 | tf_op jit(solution)/shard_map/ppermute | solution.py:534
  328.4 10.2 %collective-permute-start.34 = (bf16[8,144,384]{2,1,0:T(8,128)(2,1)}, bf16[8,144,384]{2,1,0:T(8,128)(2,1)}, u32[]{:S(2)}, u32[]{:S(2)}) collective-permute-start(bf16[8,144,384]{2,1,0:T(8,128)(2,1)} %constant_dynamic-update-slice_fusion.5), channel_id=1, source_target_pairs={{0,1},{1,0},{2,3},{3,2},{4,5},{5,4},{6,7},{7,6},{8,9},{9,8},{10,11... | collective-permute-start | bytes 2654216 | tf_op jit(solution)/shard_map/ppermute | solution.py:534
  334.9 11.7 %collective-permute-start.26 = (bf16[8,144,128]{2,1,0:T(8,128)(2,1)S(1)}, bf16[8,144,128]{2,1,0:T(8,128)(2,1)S(1)}, u32[]{:S(2)}, u32[]{:S(2)}) collective-permute-start(bf16[8,144,128]{2,1,0:T(8,128)(2,1)S(1)} %constant_dynamic-update-slice_fusion), channel_id=1, source_target_pairs={{0,1},{1,0},{2,3},{3,2},{4,5},{5,4},{6,7},{7,6},{8,9},{9,8},{10,11... | collective-permute-start | bytes 884744 | tf_op jit(solution)/shard_map/ppermute | solution.py:534
  (41 other events, 324.5 us)
